TPU v7x, 128 devices: a whole 4x4x4 slice. The times are simulated.
128 devices in a mesh: ctx: 16 (over x_hi, z, core), tp: 8 (over y, x_lo).
Axes of the slice: x: 4 (x_hi: 2, x_lo: 2; x = x_hi * 2 + x_lo), y: 4, z: 4, core: 2. Of those that a mesh axis runs over, the one named last changes fastest.
Arguments:
- tokens: bfloat16 [8192, 2048], P('ctx'), may hold values from -6 to 6
- cotangent: bfloat16 [8192, 2048], P('ctx'), may hold values from -6 to 6
- segment_ids: int32 [8192], replicated, may hold values from 0 to 2, as said below
- first_gain: float32 [2048], replicated, may hold values from 0.25 to 1.75
- first_shift: float32 [2048], replicated, may hold values from -3 to 3
- second_gain: float32 [2048], replicated, may hold values from 0.25 to 1.75
- second_shift: float32 [2048], replicated, may hold values from -3 to 3
- w_qkv: bfloat16 [2048, 3, 2048], P(None, None, 'tp'), may hold values from -0.125 to 0.125
- qkv_bias: float32 [3, 2048], P(None, 'tp'), may hold values from -3 to 3
- w_out: bfloat16 [2048, 2048], P('tp'), may hold values from -2 to 2
- w_gate_up: bfloat16 [2048, 2, 5632], P(None, None, 'tp'), may hold values from -0.125 to 0.125
- w_down: bfloat16 [5632, 2048], P('tp'), may hold values from -0.078125 to 0.078125
Outputs:
- layer_out: bfloat16 [8192, 2048], P('ctx')
- grad_tokens: bfloat16 [8192, 2048], P('ctx')
- grad_first_gain: float32 [2048], replicated
- grad_first_shift: float32 [2048], replicated
- grad_second_gain: float32 [2048], replicated
- grad_second_shift: float32 [2048], replicated
- grad_w_qkv: float32 [2048, 3, 2048], P('ctx', None, 'tp')
- grad_qkv_bias: float32 [3, 2048], P(None, 'tp')
- grad_w_out: float32 [2048, 2048], P('tp', 'ctx')
- grad_w_gate_up: float32 [2048, 2, 5632], P('ctx', None, 'tp')
- grad_w_down: float32 [5632, 2048], P('tp', 'ctx')
Inputs may be any that keep to these rules, and one draw needn't show every extreme that they name: `segment_ids`: ids never fall from one token to the next, every id appears, document 0 ends within the first 512 tokens and document 2 begins within the last 512 tokens.
All inputs are finite; a program needn't handle non-finite values.
Results may differ from a plain program's by a relative error of at most 0.029.
Values may be sent and summed in bfloat16 or wider, within the bound.
No kernel may reach another device: no remote copies, remote signals or barrier semaphores. Data moves between devices by JAX's collectives and lax.ppermute only.
A program may use at most 192 MiB of HBM per device.

v0:
```python
import jax
import jax.numpy as jnp
from jax import lax
from jax.sharding import PartitionSpec as P

HDIM = 64
DOCS = 3


def copy_for_each(shard, axis):
    copies = jnp.broadcast_to(shard, (lax.axis_size(axis), *shard.shape))
    return lax.all_to_all(copies, axis, split_axis=0, concat_axis=0, tiled=True)


def laid_out(parts, dim):
    parts = jnp.moveaxis(parts, 0, dim)
    dims = parts.shape
    return parts.reshape(*dims[:dim], dims[dim] * dims[dim + 1], *dims[dim + 2 :])


def gathered_copies(shard, axis, dim):
    parts = copy_for_each(shard, axis)
    return laid_out(parts, dim)


def sent_together(arrays, axis, dim, along):
    widths = [a.shape[along] for a in arrays]
    both = jnp.concatenate(arrays, axis=along)
    filled = lax.all_gather(both, axis, axis=dim, tiled=True)
    return tuple(jnp.split(filled, [sum(widths[:k]) for k in range(1, len(widths))], axis=along))


def sent_together_2(arrays, axis, dim, along):
    both = jnp.concatenate(arrays, axis=along)
    filled, at, done = (lax.psum_scatter(both, axis, scatter_dimension=dim, tiled=True), 0, [])
    for a in arrays:
        done.append(lax.slice_in_dim(filled, at, at + a.shape[along], axis=along))
        at += a.shape[along]
    return tuple(done)


def of_everyone(shard, axis):
    everything = copy_for_each(shard, axis)
    return jnp.sum(everything.astype(jnp.float32), axis=0)


def split_up(shard, dim, peers):
    before, after = (shard.shape[:dim], shard.shape[dim + 1 :])
    return jnp.moveaxis(shard.reshape(*before, peers, -1, *after), dim, 0)


def sum_packed(arrays, axis, dims):
    peers = lax.axis_size(axis)
    parts = [split_up(a, dim, peers) for a, dim in zip(arrays, dims)]
    lines = jnp.concatenate([b.reshape(peers, -1) for b in parts], axis=1)
    rows = max(16, -(-lines.shape[1] // 1024) * 8)
    lines = jnp.pad(lines, ((0, 0), (0, rows * 128 - lines.shape[1]))).reshape(-1, 128)
    line, at, done = (lax.psum_scatter(lines, axis, tiled=True).reshape(-1), 0, [])
    for b in parts:
        part = b[0]
        done.append(line[at : at + part.size].reshape(part.shape))
        at += part.size
    return tuple(done)


def norm_forward(values, gain, shift):
    center = values - jnp.mean(values, axis=-1, keepdims=True)
    scaling = lax.rsqrt(jnp.mean(center * center, axis=-1, keepdims=True) + 1e-05)
    normal_rows = center * scaling
    return (normal_rows * gain + shift, normal_rows, scaling)


def norm_backward(grad_out, normal_rows, scaling, gain):
    scaled = grad_out * gain
    grad_in = scaling * (
        scaled
        - jnp.mean(scaled, axis=-1, keepdims=True)
        - normal_rows * jnp.mean(scaled * normal_rows, axis=-1, keepdims=True)
    )
    return (grad_in, jnp.sum(grad_out * normal_rows, axis=0), jnp.sum(grad_out, axis=0))


def rotary(values, places, turning):
    frequency = 10000.0 ** (-jnp.arange(8, dtype=jnp.float32) / 8.0)
    angles = places.astype(jnp.float32)[:, None] * frequency[None, :]
    cosine = jnp.cos(angles)[:, None, :]
    sine_part = turning * jnp.sin(angles)[:, None, :]
    front_half = values[..., :8]
    back_half = values[..., 8:16]
    return jnp.concatenate(
        [
            front_half * cosine - back_half * sine_part,
            back_half * cosine + front_half * sine_part,
            values[..., 16:],
        ],
        axis=-1,
    )


def masked_scores(query_heads, key_block, segment_ids, own_segment, own_rows, key_start):
    key_count = key_block.shape[0]
    key_heads = key_block.reshape(key_count, query_heads.shape[1], HDIM)
    scores = jnp.einsum("qhd,khd->hqk", query_heads, key_heads, preferred_element_type=jnp.float32)
    key_segment = lax.dynamic_slice_in_dim(segment_ids, key_start, key_count)
    key_places = key_start + jnp.arange(key_count, dtype=jnp.int32)
    allowed = (own_segment[:, None] == key_segment[None, :]) & (
        own_rows[:, None] >= key_places[None, :]
    )
    return jnp.where(allowed[None], scores, -1e30)


def keep_same(current):
    return current


def tp_share(partial_sum):
    return lax.psum_scatter(
        partial_sum.astype(jnp.bfloat16), "tp", scatter_dimension=0, tiled=True
    ).astype(jnp.float32)


def tp_gather(share_rows):
    return gathered_copies(share_rows, "tp", 0)


def body(
    tokens,
    cotangent,
    segment_ids,
    first_gain,
    first_shift,
    second_gain,
    second_shift,
    w_qkv,
    qkv_bias,
    w_out,
    w_gate_up,
    w_down,
):
    row_count = tokens.shape[0]
    local_width = w_qkv.shape[2]
    head_count = local_width // HDIM
    context_size = lax.axis_size("ctx")
    own_index = lax.axis_index("ctx")
    share_count = row_count // lax.axis_size("tp")
    share_start = lax.axis_index("tp") * share_count
    row_start = own_index * row_count
    row_last = row_start + row_count - 1
    own_rows = row_start + jnp.arange(row_count, dtype=jnp.int32)
    labels = jnp.arange(DOCS, dtype=jnp.int32)
    starts = jnp.sum((segment_ids[:, None] < labels[None, :]).astype(jnp.int32), axis=0)
    own_segment = lax.dynamic_slice_in_dim(segment_ids, row_start, row_count)
    places = own_rows - jnp.sum(
        jnp.where(own_segment[:, None] == labels[None, :], starts[None, :], 0), axis=1
    )

    def my_share(array):
        return lax.dynamic_slice_in_dim(array, share_start, share_count)

    inputs32 = tokens.astype(jnp.float32)
    normed, first_rows, first_scale = norm_forward(inputs32, first_gain, first_shift)
    normed_low = normed.astype(jnp.bfloat16)
    mixed = (
        jnp.einsum("td,dch->tch", normed_low, w_qkv, preferred_element_type=jnp.float32)
        + qkv_bias[None]
    )
    head_shape = (row_count, head_count, HDIM)
    query_heads = (rotary(mixed[:, 0].reshape(head_shape), places, 1.0) * 0.125).astype(
        jnp.bfloat16
    )
    key_flat = (
        rotary(mixed[:, 1].reshape(head_shape), places, 1.0)
        .astype(jnp.bfloat16)
        .reshape(row_count, local_width)
    )
    value_flat = mixed[:, 2].astype(jnp.bfloat16)
    initial = (
        jnp.full((head_count, row_count), -1e30, jnp.float32),
        jnp.zeros((head_count, row_count), jnp.float32),
        jnp.zeros((head_count, row_count, HDIM), jnp.float32),
    )
    running = initial
    pieces = sent_together((key_flat, value_flat), "ctx", 0, 1)
    sub_rows = min(row_count, pieces[0].shape[0])

    def attend_block(current_state, block_number):
        offset = block_number * sub_rows
        key_block = lax.dynamic_slice_in_dim(pieces[0], offset, sub_rows)
        value_block = lax.dynamic_slice_in_dim(pieces[1], offset, sub_rows)

        def attend_compute(current):
            run_max, run_sum, run_acc = current
            scores = masked_scores(
                query_heads, key_block, segment_ids, own_segment, own_rows, offset
            )
            new_max = jnp.maximum(run_max, jnp.max(scores, axis=-1))
            factor = jnp.exp(run_max - new_max)
            weights = jnp.exp(scores - new_max[..., None])
            value_heads = value_block.reshape(sub_rows, head_count, HDIM)
            update = jnp.einsum(
                "hqk,khd->hqd",
                weights.astype(jnp.bfloat16),
                value_heads,
                preferred_element_type=jnp.float32,
            )
            return (
                new_max,
                run_sum * factor + jnp.sum(weights, axis=-1),
                run_acc * factor[..., None] + update,
            )

        current_state = lax.cond(offset <= row_last, attend_compute, keep_same, current_state)
        return (current_state, None)

    running, unused = lax.scan(attend_block, running, jnp.arange(pieces[0].shape[0] // sub_rows))
    run_max, run_sum, run_acc = running
    attended = jnp.transpose(run_acc / run_sum[..., None], (1, 0, 2))
    log_total = run_max + jnp.log(run_sum)
    attended_low = attended.reshape(row_count, local_width).astype(jnp.bfloat16)
    partial_branch = jnp.dot(attended_low, w_out, preferred_element_type=jnp.float32)
    middle = my_share(inputs32) + tp_share(partial_branch)
    second, second_rows, second_scale = norm_forward(middle, second_gain, second_shift)
    second_low = tp_gather(second.astype(jnp.bfloat16))
    gate_up = jnp.einsum("td,dcf->tcf", second_low, w_gate_up, preferred_element_type=jnp.float32)
    gate_part = gate_up[:, 0]
    up_part = gate_up[:, 1]
    sigmoid_gate = jax.nn.sigmoid(gate_part)
    activated = gate_part * sigmoid_gate
    hidden_low = (activated * up_part).astype(jnp.bfloat16)
    partial_feed = jnp.dot(hidden_low, w_down, preferred_element_type=jnp.float32)
    layer_out = tp_gather((middle + tp_share(partial_feed)).astype(jnp.bfloat16))
    grad_down = jnp.einsum("tf,td->fd", hidden_low, cotangent, preferred_element_type=jnp.float32)
    grad_hidden = jnp.einsum("td,fd->tf", cotangent, w_down, preferred_element_type=jnp.float32)
    grad_gate = grad_hidden * up_part * sigmoid_gate * (1.0 + gate_part * (1.0 - sigmoid_gate))
    grad_gate_up = jnp.stack([grad_gate, grad_hidden * activated], axis=1).astype(jnp.bfloat16)
    grad_feed_weights = jnp.einsum(
        "td,tcf->dcf", second_low, grad_gate_up, preferred_element_type=jnp.float32
    )
    partial_second = jnp.einsum(
        "tcf,dcf->td", grad_gate_up, w_gate_up, preferred_element_type=jnp.float32
    )
    grad_second = tp_share(partial_second)
    cotangent_rows = my_share(cotangent).astype(jnp.float32)
    grad_middle_norm, second_gain_grad, second_shift_grad = norm_backward(
        grad_second, second_rows, second_scale, second_gain
    )
    grad_middle = cotangent_rows + grad_middle_norm
    grad_branch = grad_middle.astype(jnp.bfloat16)
    grad_branch = tp_gather(grad_branch)
    grad_out_weights = jnp.einsum(
        "th,td->hd", attended_low, grad_branch, preferred_element_type=jnp.float32
    )
    grad_attended = (
        jnp.einsum("td,hd->th", grad_branch, w_out, preferred_element_type=jnp.float32)
        .astype(jnp.bfloat16)
        .reshape(head_shape)
    )
    row_dot = jnp.transpose(jnp.sum(grad_attended.astype(jnp.float32) * attended, axis=-1))

    def block_grads(key_block, value_block, key_start):
        scores = masked_scores(
            query_heads, key_block, segment_ids, own_segment, own_rows, key_start
        )
        weights_norm = jnp.exp(scores - log_total[..., None])
        key_heads = key_block.reshape(row_count, head_count, HDIM)
        value_heads = value_block.reshape(row_count, head_count, HDIM)
        grad_weights = jnp.einsum(
            "qhd,khd->hqk", grad_attended, value_heads, preferred_element_type=jnp.float32
        )
        grad_scores = (weights_norm * (grad_weights - row_dot[..., None])).astype(jnp.bfloat16)
        query_term = jnp.einsum(
            "hqk,khd->qhd", grad_scores, key_heads, preferred_element_type=jnp.float32
        )
        key_term = jnp.einsum(
            "hqk,qhd->khd", grad_scores, query_heads, preferred_element_type=jnp.float32
        ).reshape(row_count, local_width)
        value_term = jnp.einsum(
            "hqk,qhd->khd",
            weights_norm.astype(jnp.bfloat16),
            grad_attended,
            preferred_element_type=jnp.float32,
        ).reshape(row_count, local_width)
        return (query_term, key_term, value_term)

    zeros_query = jnp.zeros(head_shape, jnp.float32)
    key_all, value_all = sent_together((key_flat, value_flat), "ctx", 0, 1)

    def local_turn(turn_index, running):
        key_start = turn_index * row_count
        key_block = lax.dynamic_slice_in_dim(key_all, key_start, row_count)
        value_block = lax.dynamic_slice_in_dim(value_all, key_start, row_count)

        def local_compute(current):
            increments = block_grads(key_block, value_block, key_start)
            key_sum = lax.dynamic_slice_in_dim(current[1], key_start, row_count) + increments[1]
            value_sum = lax.dynamic_slice_in_dim(current[2], key_start, row_count) + increments[2]
            return (
                current[0] + increments[0],
                lax.dynamic_update_slice_in_dim(current[1], key_sum, key_start, 0),
                lax.dynamic_update_slice_in_dim(current[2], value_sum, key_start, 0),
            )

        return lax.cond(key_start <= row_last, local_compute, keep_same, running)

    whole_zeros = jnp.zeros((context_size * row_count, local_width), jnp.float32)
    grad_query, key_total, value_total = lax.fori_loop(
        0, context_size, local_turn, (zeros_query, whole_zeros, whole_zeros)
    )
    grad_key, grad_value = tuple(
        (
            part.astype(jnp.float32)
            for part in sent_together_2(
                (key_total.astype(jnp.bfloat16), value_total.astype(jnp.bfloat16)), "ctx", 0, 1
            )
        )
    )
    grad_query_pre = rotary(grad_query * 0.125, places, -1.0).reshape(row_count, local_width)
    grad_key_pre = rotary(grad_key.reshape(head_shape), places, -1.0).reshape(
        row_count, local_width
    )
    grad_mixed = jnp.stack([grad_query_pre, grad_key_pre, grad_value], axis=1).astype(jnp.bfloat16)
    grad_proj_weights = jnp.einsum(
        "td,tch->dch", normed_low, grad_mixed, preferred_element_type=jnp.float32
    )
    grad_bias = jnp.sum(grad_mixed, axis=0, dtype=jnp.float32)
    partial_normed = jnp.einsum(
        "tch,dch->td", grad_mixed, w_qkv, preferred_element_type=jnp.float32
    )
    grad_normed = tp_share(partial_normed)
    grad_inputs, first_gain_grad, first_shift_grad = norm_backward(
        grad_normed, my_share(first_rows), my_share(first_scale), first_gain
    )
    grad_tokens = tp_gather((grad_middle + grad_inputs).astype(jnp.bfloat16))
    norm_parts = (
        of_everyone(first_gain_grad.astype(jnp.bfloat16), "tp").astype(jnp.float32),
        of_everyone(first_shift_grad.astype(jnp.bfloat16), "tp").astype(jnp.float32),
        of_everyone(second_gain_grad.astype(jnp.bfloat16), "tp").astype(jnp.float32),
        of_everyone(second_shift_grad.astype(jnp.bfloat16), "tp").astype(jnp.float32),
    )
    summed = tuple(
        (
            part.astype(jnp.float32)
            for part in sum_packed(
                (
                    grad_proj_weights.astype(jnp.bfloat16),
                    grad_out_weights.astype(jnp.bfloat16),
                    grad_feed_weights.astype(jnp.bfloat16),
                    grad_down.astype(jnp.bfloat16),
                ),
                "ctx",
                (0, 1, 0, 1),
            )
        )
    )
    smaller = (
        of_everyone(norm_parts[0].astype(jnp.bfloat16), "ctx").astype(jnp.float32),
        of_everyone(norm_parts[1].astype(jnp.bfloat16), "ctx").astype(jnp.float32),
        of_everyone(norm_parts[2].astype(jnp.bfloat16), "ctx").astype(jnp.float32),
        of_everyone(norm_parts[3].astype(jnp.bfloat16), "ctx").astype(jnp.float32),
        of_everyone(grad_bias.astype(jnp.bfloat16), "ctx").astype(jnp.float32),
    )
    return (
        layer_out,
        grad_tokens,
        smaller[0],
        smaller[1],
        smaller[2],
        smaller[3],
        summed[0],
        smaller[4],
        summed[1],
        summed[2],
        summed[3],
    )


def solution(mesh):
    placed = (
        P("ctx", None),
        P("ctx", None),
        P(),
        P(),
        P(),
        P(),
        P(),
        P(None, None, "tp"),
        P(None, "tp"),
        P("tp", None),
        P(None, None, "tp"),
        P("tp", None),
    )
    return jax.shard_map(
        body,
        mesh=mesh,
        in_specs=placed,
        out_specs=(
            P("ctx", None),
            P("ctx", None),
            P(),
            P(),
            P(),
            P(),
            P("ctx", None, "tp"),
            P(None, "tp"),
            P("tp", "ctx"),
            P("ctx", None, "tp"),
            P("tp", "ctx"),
        ),
        check_vma=False,
    )
```

profile of v0, /device:TPU:0, one launch (start us, length us, event | category | flops | bytes accessed | tf_op | source)
XLA Modules:
  0.0 1045.5 jit_solution(6516067314813692295)
XLA Ops:
  22.4 77.0 %all-gather.2.cloned.1.call-done = bf16[8192,512]{0,1:T(8,128)(2,1)} async-done(((bf16[512,512]{0,1:T(8,128)(2,1)}), bf16[8192,512]{0,1:T(8,128)(2,1)}) %all-gather.2.cloned.1.call-update) | async-done | bytes 8388624 | tf_op jit(solution)/shard_map/all_gather | solution.py:29
  99.4 6.0 fusion.61
  106.3 26.1 %while.33 = (s32[]{:T(128)}, f32[4,512]{1,0:T(4,128)S(1)}, f32[4,512]{1,0:T(4,128)S(1)}, f32[4,512,64]{1,2,0:T(8,128)}, s32[16]{0:T(128)S(1)}, /*index=5*/s32[]{...) while((s32[]{:T(128)}, f32[4,512]{1,0:T(4,128)S(1)}, ...), condition=%wide.region_9.10_spmd.clone, body=%wide.region_4.9_spmd.clone.sunk | while | flops 277877760 | bytes 20861348 | solution.py:215
  107.5 5.5 conditional.6
  137.6 4.2 convert_element_type.191
  141.8 126.6 %reduce-scatter.7.cloned.1.call-done = bf16[64,2048]{1,0:T(8,128)(2,1)} async-done(((bf16[512,2048]{1,0:T(8,128)(2,1)}), bf16[64,2048]{1,0:T(8,128)(2,1)}) %reduce-scatter.7.cloned.1.call-update) | async-done | bytes 262160 | tf_op jit(solution)/shard_map/reduce_scatter | solution.py:117
  270.9 30.5 %all_to_all.73 = bf16[8,64,2048]{2,1,0:T(8,128)(2,1)S(1)} all-to-all(bf16[8,64,2048]{2,1,0:T(8,128)(2,1)S(1)} %broadcast_in_dim.156), channel_id=1, replica_groups=mesh['ctx'=16,'tp'=8] {'tp'}, dimensions={0} | all-to-all | bytes 4194304 | tf_op jit(solution)/shard_map/all_to_all | solution.py:12
  301.4 6.0 fusion.66
  311.7 4.6 bitcast_convert_fusion.1
  316.4 5.2 convolution_convert_fusion.4
  321.6 46.7 %reduce-scatter.11.cloned.1.call-done = bf16[64,2048]{1,0:T(8,128)(2,1)} async-done(((bf16[512,2048]{1,0:T(8,128)(2,1)}), bf16[64,2048]{1,0:T(8,128)(2,1)}) %reduce-scatter.11.cloned.1.call-update) | async-done | bytes 262160 | tf_op jit(solution)/shard_map/reduce_scatter | solution.py:117
  369.8 53.1 %reduce-scatter.9.cloned.1.call-done = bf16[64,2048]{1,0:T(8,128)(2,1)} async-done(((bf16[512,2048]{1,0:T(8,128)(2,1)}), bf16[64,2048]{1,0:T(8,128)(2,1)}) %reduce-scatter.9.cloned.1.call-update) | async-done | bytes 262160 | tf_op jit(solution)/shard_map/reduce_scatter | solution.py:117
  426.9 4.4 all-to-all-start.2
  431.6 26.8 %all-to-all-done.2 = bf16[8,64,2048]{2,1,0:T(8,128)(2,1)} async-done(((bf16[8,64,2048]{2,1,0:T(8,128)(2,1)}), bf16[8,64,2048]{2,1,0:T(8,128)(2,1)}, u32[]{:S(2)}, u32[]{:S(2)}) %all-to-all-start.2) | async-done | bytes 2097184 | tf_op jit(solution)/shard_map/all_to_all | solution.py:12
  461.8 4.3 broadcast_in_dim.159
  466.1 4.3 broadcast_in_dim.159.clone
  471.3 11.6 %while.34 = (s32[]{:T(128)}, f32[512,4,64]{0,2,1:T(8,128)}, f32[8192,256]{0,1:T(8,128)}, f32[8192,256]{0,1:T(8,128)}, s32[]{:T(128)}, /*index=5*/s32[512]{0:T(51...) while((s32[]{:T(128)}, f32[512,4,64]{0,2,1:T(8,128)}, ...), condition=%wide.region_21.22_spmd.clone, body=%wide.region_18.21_spmd.clone.sunk | while | flops 680657920 | bytes 33075684 | solution.py:306
  471.3 10.9 %conditional.7 = ((f32[512,4,64]{0,2,1:T(8,128)}, f32[8192,256]{0,1:T(8,128)}, f32[8192,256]{0,1:T(8,128)})) conditional(s32[]{:T(128)} %convert_element_type.339, (f32[512,4,64]{0,2,1:T(8,128)}, f32[8192,256]{0,1:T(8,128)}, f32[8192,256]{0,1:T(8,128)}) %tuple.127, (s32[512]{0:T(512)S(1)}, s32[]{:T(128)}, s32[8192]{0:T(1024)S(1)}, s32[]{:T(128)}, ...), branch_computations={%region_19.19_spmd, %region_20.20_spmd} | conditional | flops 680657920 | bytes 33073326 | solution.py:303
  482.9 7.3 copy.100
  490.1 7.3 copy.101
  497.4 7.4 pad_maximum_fusion.1
  505.3 7.6 convolution_convert_fusion
  512.9 16.2 %copy.116 = bf16[2048,2,704]{2,1,0:T(2,128)(2,1)} copy(bf16[2048,2,704]{0,2,1:T(8,128)(2,1)} %convolution_convert_fusion) | data formatting | bytes 11534336 | tf_op jit(solution)/shard_map/convert_element_type | solution.py:347
  529.1 11.5 %reshape_reshape.7 = bf16[16,180224]{1,0:T(8,128)(2,1)} reshape(bf16[2048,2,704]{2,1,0:T(2,128)(2,1)} %copy.116) | data formatting | bytes 11534336 | tf_op jit(solution)/shard_map/reshape;reshape | solution.py:55
  544.9 3.5 copy.145
  554.2 212.7 %reduce-scatter.13.cloned.1.call-done = bf16[512,512]{1,0:T(8,128)(2,1)} async-done(((bf16[8192,512]{1,0:T(8,128)(2,1)}), bf16[512,512]{1,0:T(8,128)(2,1)}) %reduce-scatter.13.cloned.1.call-update) | async-done | bytes 524304 | tf_op jit(solution)/shard_map/reduce_scatter | solution.py:35
  777.9 5.5 convolution_convert_fusion.1
  786.6 6.8 copy.114
  793.3 6.7 reshape_reshape.6
  800.1 16.4 %pad_maximum_fusion = bf16[16,401408]{1,0:T(8,128)(2,1)} fusion(bf16[16,90112]{1,0:T(8,128)(2,1)} %bitcast.159, bf16[16,180224]{1,0:T(8,128)(2,1)} %reshape_reshape.7, bf16[16,32768]{1,0:T(8,128)(2,1)} %bitcast.162, bf16[16,98304]{1,0:T(8,128)(2,1)} %reshape_reshape.6), kind=kLoop, calls=%fused_computation.42 | loop fusion | flops 51380224 | bytes 25690112 | tf_op jit(solution)/shard_map/concatenate | solution.py:55
  816.5 16.8 %reshape.439 = bf16[50176,128]{1,0:T(8,128)(2,1)} reshape(bf16[16,401408]{1,0:T(8,128)(2,1)} %pad_maximum_fusion) | data formatting | bytes 25690112 | tf_op jit(solution)/shard_map/reshape | solution.py:57
  835.4 4.3 all-to-all-start.8
  841.3 5.0 all-to-all-done.8
  851.5 4.3 all-to-all-done.10
  855.9 5.3 all-to-all-start.9
  862.4 6.4 all-to-all-done.9
  868.8 10.2 all_to_all.74
  881.6 4.4 all-to-all-start.1
  886.0 4.2 subtract_multiply_fusion
  890.4 38.2 %all-to-all-done.1 = bf16[8,64,2048]{2,1,0:T(8,128)(2,1)} async-done(((bf16[8,64,2048]{2,1,0:T(8,128)(2,1)}), bf16[8,64,2048]{2,1,0:T(8,128)(2,1)}, u32[]{:S(2)}, u32[]{:S(2)}) %all-to-all-start.1) | async-done | bytes 2097184 | tf_op jit(solution)/shard_map/all_to_all | solution.py:12
  936.1 4.1 all-to-all-done.12
  940.2 3.6 all-to-all-start.4
  955.9 3.8 all-to-all-done.6
  967.0 3.8 all-to-all-done.5
  970.8 4.1 all-to-all-start.7
  976.5 7.0 all-to-all-done.7
  985.0 4.3 all-to-all-start.3
  995.3 21.3 %all-to-all-done.3 = bf16[8,64,2048]{2,1,0:T(8,128)(2,1)} async-done(((bf16[8,64,2048]{2,1,0:T(8,128)(2,1)}), bf16[8,64,2048]{2,1,0:T(8,128)(2,1)}, u32[]{:S(2)}, u32[]{:S(2)}) %all-to-all-start.3) | async-done | bytes 2097184 | tf_op jit(solution)/shard_map/all_to_all | solution.py:12
  (318 shorter events, 158.8 us)
Async XLA Ops:
  7.2 4.5 copy-start
  7.2 4.5 copy-start.26
  7.2 4.5 copy-start.32
  7.2 4.5 copy-start.34
  7.2 92.2 %all-gather.2.cloned.1.call-start = ((), (), s32[]{:S(2)}) async-start(), calls=%async_computation.19 | async-start | bytes 8912896 | tf_op jit(solution)/shard_map/all_gather | solution.py:29
  7.3 4.5 copy-start.1
  11.8 3.2 copy-start.23
  19.5 248.8 %reduce-scatter.7.cloned.1.call-start = ((), (), s32[]{:S(2)}) async-start(), calls=%async_computation.20 | async-start | bytes 2359296 | tf_op jit(solution)/shard_map/reduce_scatter | solution.py:117
  137.5 132.9 %copy-start.24 = (f32[2048]{0:T(1024)S(1)}, f32[2048]{0:T(1024)}, u32[]{:S(2)}) copy-start(f32[2048]{0:T(1024)} %param.25) | copy-start | bytes 24580
  137.5 132.9 %copy-start.28 = (f32[2048]{0:T(1024)S(1)}, f32[2048]{0:T(1024)}, u32[]{:S(2)}) copy-start(f32[2048]{0:T(1024)} %param.26) | copy-start | bytes 24580
  137.5 230.7 %reduce-scatter.11.cloned.1.call-start = ((), (), s32[]{:S(2)}) async-start(), calls=%async_computation.22 | async-start | bytes 2359296 | tf_op jit(solution)/shard_map/reduce_scatter | solution.py:117
  301.4 6.1 copy-start.11
  301.4 6.1 copy-start.27
  301.4 6.1 copy-start.31
  301.4 10.3 slice-start
  307.4 4.2 slice-start.1
  316.3 106.5 %reduce-scatter.9.cloned.1.call-start = ((), (), s32[]{:S(2)}) async-start(), calls=%async_computation.21 | async-start | bytes 2359296 | tf_op jit(solution)/shard_map/reduce_scatter | solution.py:117
  426.9 31.5 %all-to-all-start.2 = ((bf16[8,64,2048]{2,1,0:T(8,128)(2,1)}), bf16[8,64,2048]{2,1,0:T(8,128)(2,1)}, u32[]{:S(2)}, u32[]{:S(2)}) async-start(bf16[8,64,2048]{2,1,0:T(8,128)(2,1)} %broadcast_in_dim.160), calls=%async_computation.5 | async-start | bytes 4194304 | tf_op jit(solution)/shard_map/all_to_all | solution.py:12
  431.3 335.7 %reduce-scatter.13.cloned.1.call-start = ((), (), s32[]{:S(2)}) async-start(), calls=%async_computation.23 | async-start | bytes 8912896 | tf_op jit(solution)/shard_map/reduce_scatter | solution.py:35
  471.3 2.2 copy-start.20
  475.7 5.1 copy-start.4
  504.8 427.9 %reduce-scatter.15.cloned.1.call-start = ((), (), s32[]{:S(2)}) async-start(), calls=%async_computation.24 | async-start | bytes 2359296 | tf_op jit(solution)/shard_map/reduce_scatter | solution.py:117
  544.9 3.6 copy-start.6
  544.9 5.1 copy-start.9
  552.3 218.4 %copy-start.25 = (f32[512,8]{0,1:T(8,128)S(1)}, f32[512,8]{0,1:T(8,128)}, u32[]{:S(2)}) copy-start(f32[512,8]{0,1:T(8,128)} %get-tuple-element.805) | copy-start | bytes 49156
  552.6 225.3 %copy-start.30 = (f32[512]{0:T(512)S(1)}, f32[512]{0:T(512)}, u32[]{:S(2)}) copy-start(f32[512]{0:T(512)} %copy-done.29) | copy-start | bytes 6148
  552.6 225.3 %copy-start.33 = (f32[2048]{0:T(1024)S(1)}, f32[2048]{0:T(1024)}, u32[]{:S(2)}) copy-start(f32[2048]{0:T(1024)} %param.24) | copy-start | bytes 24580
  774.3 9.1 copy-start.13
  777.9 5.5 copy-start.15
  777.9 5.5 copy-start.17
  800.0 216.5 %reduce-scatter.17.cloned.1.call-start = ((), (), s32[]{:S(2)}) async-start(), calls=%async_computation.25 | async-start | bytes 13647872 | tf_op jit(solution)/shard_map/reduce_scatter | solution.py:58
  833.4 6.4 copy-start.10
  835.4 10.9 %all-to-all-start.8 = ((bf16[8,2,1024]{2,1,0:T(2,128)(2,1)}), bf16[8,2,1024]{2,1,0:T(2,128)(2,1)S(1)}, u32[]{:S(2)}, u32[]{:S(2)}) async-start(bf16[8,2,1024]{2,1,0:T(2,128)(2,1)} %reshape.455), calls=%async_computation.13 | async-start | bytes 65536 | tf_op jit(solution)/shard_map/all_to_all | solution.py:12
  846.3 9.5 all-to-all-start.10
  855.9 12.9 %all-to-all-start.9 = ((bf16[16,2,1024]{2,1,0:T(2,128)(2,1)}), bf16[16,2,1024]{2,1,0:T(2,128)(2,1)S(1)}, u32[]{:S(2)}, u32[]{:S(2)}) async-start(bf16[16,2,1024]{2,1,0:T(2,128)(2,1)} %reshape.457), calls=%async_computation.14 | async-start | bytes 131072 | tf_op jit(solution)/shard_map/all_to_all | solution.py:12
  881.6 47.0 %all-to-all-start.1 = ((bf16[8,64,2048]{2,1,0:T(8,128)(2,1)}), bf16[8,64,2048]{2,1,0:T(8,128)(2,1)}, u32[]{:S(2)}, u32[]{:S(2)}) async-start(bf16[8,64,2048]{2,1,0:T(8,128)(2,1)} %broadcast_in_dim.157), calls=%async_computation.3 | async-start | bytes 4194304 | tf_op jit(solution)/shard_map/all_to_all | solution.py:12
  886.0 4.2 copy-start.14
  886.0 4.2 copy-start.16
  886.0 4.2 copy-start.18
  929.2 11.1 %all-to-all-start.12 = ((bf16[16,3,256]{2,1,0:T(4,128)(2,1)}), bf16[16,3,256]{2,1,0:T(4,128)(2,1)S(1)}, u32[]{:S(2)}, u32[]{:S(2)}) async-start(bf16[16,3,256]{2,1,0:T(4,128)(2,1)} %broadcast_in_dim.170), calls=%async_computation.18 | async-start | bytes 65536 | tf_op jit(solution)/shard_map/all_to_all | solution.py:12
  940.2 13.8 %copy-start.22 = (bf16[16,3,256]{2,1,0:T(4,128)(2,1)}, bf16[16,3,256]{2,1,0:T(4,128)(2,1)S(1)}, u32[]{:S(2)}) copy-start(bf16[16,3,256]{2,1,0:T(4,128)(2,1)S(1)} %all-to-all-done.12) | copy-start | bytes 73732
  940.2 9.9 all-to-all-start.4
  950.2 9.5 all-to-all-start.6
  959.7 3.5 copy-start.21
  959.7 11.1 %all-to-all-start.5 = ((bf16[16,2,1024]{2,1,0:T(2,128)(2,1)}), bf16[16,2,1024]{2,1,0:T(2,128)(2,1)S(1)}, u32[]{:S(2)}, u32[]{:S(2)}) async-start(bf16[16,2,1024]{2,1,0:T(2,128)(2,1)} %reshape.449), calls=%async_computation.10 | async-start | bytes 131072 | tf_op jit(solution)/shard_map/all_to_all | solution.py:12
  970.8 4.2 copy-start.19
  970.8 12.6 %all-to-all-start.7 = ((bf16[16,2,1024]{2,1,0:T(2,128)(2,1)}), bf16[16,2,1024]{2,1,0:T(2,128)(2,1)}, u32[]{:S(2)}, u32[]{:S(2)}) async-start(bf16[16,2,1024]{2,1,0:T(2,128)(2,1)} %reshape.453), calls=%async_computation.12 | async-start | bytes 131072 | tf_op jit(solution)/shard_map/all_to_all | solution.py:12
  985.0 31.5 %all-to-all-start.3 = ((bf16[8,64,2048]{2,1,0:T(8,128)(2,1)}), bf16[8,64,2048]{2,1,0:T(8,128)(2,1)}, u32[]{:S(2)}, u32[]{:S(2)}) async-start(bf16[8,64,2048]{2,1,0:T(8,128)(2,1)} %broadcast_in_dim.161), calls=%async_computation.8 | async-start | bytes 4194304 | tf_op jit(solution)/shard_map/all_to_all | solution.py:12
  (9 other events, 9.6 us)
Sparse Core Ops, SparseCore 0:
  19.6 79.6 all-gather.1
  137.6 130.6 reduce-scatter.6
  316.4 51.7 reduce-scatter.10
  371.1 51.7 reduce-scatter.8
  504.9 262.0 reduce-scatter.12
  800.2 51.5 reduce-scatter.14
  856.0 137.1 reduce-scatter.16
where the time goes:
time: 1060 us; the launch traced here: 1050 us
  waiting for transfers between devices  640 us (60%)
  local copies, waits for them, and re-layouts  154 us (15%)
  other arithmetic  82.2 us (8%)
  matrix products  56.5 us (5%)
  starting transfers between devices  45.1 us (4%)
  blocking collectives  40.7 us (4%)
  between operations  15.3 us (1%)
  loops' own time  12.1 us (1%)
    reduce_scatter x4, waiting for transfers between devices, tp_share(): lax.psum_scatter(partial_sum.astype(jnp.bfloat16), 'tp', scatter_dimensio...  226 us
    reduce_scatter x1, waiting for transfers between devices, sent_together_2(): lax.psum_scatter(both, axis, scatter_dimension=dim, tiled=True)  213 us
    all_to_all x11, waiting for transfers between devices, copy_for_each(): return lax.all_to_all(copies, axis, split_axis=0, concat_axis=0, tiled=True)  124 us
    all_gather x1, waiting for transfers between devices, sent_together(): filled = lax.all_gather(both, axis, axis=dim, tiled=True)  77 us
    all_to_all x11, starting transfers between devices, copy_for_each(): return lax.all_to_all(copies, axis, split_axis=0, concat_axis=0, tiled=True)  44.1 us
    all_to_all x2, blocking collectives, copy_for_each(): return lax.all_to_all(copies, axis, split_axis=0, concat_axis=0, tiled=True)  40.7 us
    unnamed x90, local copies, waits for them, and re-layouts  26 us
  transfers between devices with their start and end apart: 18, of which 16 were waited for; matrix products, arithmetic and copies ran while one was open for 13% of the time, Pallas kernels for 0%

commit v1 on v0

v1 whole, which is shorter than its diff:
```python
import functools

import jax
import jax.numpy as jnp
from jax import lax
from jax.experimental import pallas as pl
from jax.experimental.pallas import tpu as pltpu
from jax.sharding import Mesh
from jax.sharding import PartitionSpec as P

HDIM = 64
DOCS = 3
BLOCK = 512
HALF = 256
LOW = jnp.bfloat16
WIDE = jnp.float32
CTX = ("xh", "zh", "zl", "core")
TP = ("y", "xl")
SPREAD = ("xh", "zh")
Z = ("zh", "zl")
VMEM_BYTES = 48 * 1024 * 1024


def kernel_call(body, out_shape, inputs, scalars=(), scratch=(), flops=0, exps=0):
    moved = sum(a.size * a.dtype.itemsize for a in (*inputs, *jax.tree.leaves(out_shape)))
    in_specs = [pl.BlockSpec(memory_space=pltpu.SMEM)] * len(scalars)
    in_specs += [pl.BlockSpec(memory_space=pltpu.VMEM)] * len(inputs)
    return pl.pallas_call(
        body,
        out_shape=out_shape,
        in_specs=in_specs,
        out_specs=jax.tree.map(lambda _: pl.BlockSpec(memory_space=pltpu.VMEM), out_shape),
        scratch_shapes=list(scratch),
        compiler_params=pltpu.CompilerParams(vmem_limit_bytes=VMEM_BYTES),
        cost_estimate=pl.CostEstimate(flops=flops, bytes_accessed=moved, transcendentals=exps),
    )(*scalars, *inputs)


def lane_of(shape):
    return lax.broadcasted_iota(jnp.int32, shape, len(shape) - 1)


def exchange_halves(a, b):
    front = lane_of(a.shape) < HDIM
    return (
        jnp.where(front, a, pltpu.roll(b, HDIM, 1)),
        jnp.where(front, pltpu.roll(a, HDIM, 1), b),
    )


def nt(a, b):
    return lax.dot_general(a, b, (((1,), (1,)), ((), ())), preferred_element_type=WIDE)


def nn(a, b):
    return lax.dot_general(a, b, (((1,), (0,)), ((), ())), preferred_element_type=WIDE)


def turn(x, cosine, sine, sign):
    lane = lax.rem(lane_of(x.shape), HDIM)
    ahead = pltpu.roll(x, x.shape[1] - 8, 1)
    behind = pltpu.roll(x, 8, 1)
    swapped = jnp.where(lane < 8, -ahead, behind) * sign
    return x * cosine + swapped * sine


def project_kernel(tok, gain, shift, w, bias, cosine, sine, normed, mean_out, scale_out, packed):
    rows = 64

    def norm_rows(i, carry):
        at = pl.ds(pl.multiple_of(i * rows, rows), rows)
        x = tok[at, :].astype(WIDE)
        mean = jnp.mean(x, axis=-1, keepdims=True)
        center = x - mean
        scale = lax.rsqrt(jnp.mean(center * center, axis=-1, keepdims=True) + 1e-05)
        normed[at, :] = (center * scale * gain[...] + shift[...]).astype(LOW)
        mean_out[at, :] = mean
        scale_out[at, :] = scale
        return carry

    lax.fori_loop(0, BLOCK // rows, norm_rows, 0)
    mixed = [nn(normed[...], w[c]) + bias[c : c + 1, :] for c in range(3)]
    for pair in range(2):
        lanes = slice(pair * 128, pair * 128 + 128)
        q = turn(mixed[0][:, lanes], cosine[...], sine[...], 1.0) * 0.125
        k = turn(mixed[1][:, lanes], cosine[...], sine[...], 1.0)
        kv = exchange_halves(k, mixed[2][:, lanes])
        qq = exchange_halves(q[:HALF], q[HALF:])
        for one in range(2):
            packed[2 * pair + one, :BLOCK, :] = kv[one].astype(LOW)
            packed[2 * pair + one, BLOCK:, :] = qq[one].astype(LOW)


def padded_queries(q2):
    x = q2.astype(WIDE)
    front = lane_of(x.shape) < HDIM
    return (
        jnp.where(front, x, 0.0).astype(LOW),
        jnp.where(front, pltpu.roll(x, HDIM, 1), 0.0).astype(LOW),
    )


def padded_behind(d2):
    x = d2.astype(WIDE)
    front = lane_of(x.shape) < HDIM
    return (
        jnp.where(front, 0.0, pltpu.roll(x, HDIM, 1)).astype(LOW),
        jnp.where(front, 0.0, x).astype(LOW),
    )


def allowed_keys(key_block, query_block, half, begin):
    shape = (BLOCK, HALF)
    key_at = key_block * BLOCK + lax.broadcasted_iota(jnp.int32, shape, 0)
    query_at = query_block * BLOCK + half * HALF + lax.broadcasted_iota(jnp.int32, shape, 1)
    return (key_at <= query_at) & (key_at >= begin)


def for_key_blocks(query_block, blocks, work):
    def one(key_block, carry):
        edge = (key_block == query_block) | (key_block == 0) | (query_block == blocks - 1)

        @pl.when(edge)
        def _():
            work(key_block, True)

        @pl.when(jnp.logical_not(edge))
        def _():
            work(key_block, False)

        return carry

    lax.fori_loop(0, query_block + 1, one, 0)


def forward_kernel(
    place, begin, kv0, kv1, kv2, kv3, q2, out2, out_t, total, kvs, kvt, queries, most, acc
):
    group = place[0]
    front = lane_of((BLOCK, 128)) < HDIM
    for rel, kv in enumerate((kv0, kv1, kv2, kv3)):
        for j in range(4):
            block = 4 * j + (group ^ rel)
            kvs[block] = kv[j]
            kvt[block] = jnp.where(front, 1.0, kv[j].astype(WIDE)).T.astype(LOW)

    def one_query_block(j, carry):
        query_block = 4 * j + group
        queries[:HALF, :], queries[HALF:, :] = padded_queries(q2[j])
        most[...] = jnp.full((1, BLOCK), -1e30, WIDE)
        acc[...] = jnp.zeros((128, BLOCK), WIDE)

        def work(key_block, masked):
            for half in range(2):
                at = slice(half * HALF, half * HALF + HALF)
                scores = nt(kvs[key_block], queries[at, :])
                if masked:
                    ok = allowed_keys(key_block, query_block, half, begin[j][:, at])
                    scores = jnp.where(ok, scores, -1e30)
                old = most[:, at]
                new = jnp.maximum(old, jnp.max(scores, axis=0, keepdims=True))
                weights = jnp.exp(scores - new).astype(LOW)
                acc[:, at] = acc[:, at] * jnp.exp(old - new) + nn(kvt[key_block], weights)
                most[:, at] = new

        for_key_blocks(query_block, 16, work)
        weight_sum = acc[:1, :]
        done = acc[...] / weight_sum
        out_t[j] = done
        total[j] = most[...] + jnp.log(weight_sum)
        rows = done.T
        x, y = rows[:HALF], rows[HALF:]
        out2[j] = jnp.where(lane_of(x.shape) < HDIM, pltpu.roll(x, HDIM, 1), y).astype(LOW)
        return carry

    lax.fori_loop(0, 4, one_query_block, 0)


def backward_kernel(
    place, begin, kv0, kv1, kv2, kv3, q2, d2, out_t, total,
    dq2, keep, send, kvs, kvt, queries, grads, dot_rows, acc, dkv,
):
    group = place[0]
    for rel, kv in enumerate((kv0, kv1, kv2, kv3)):
        for j in range(4):
            block = 4 * j + (group ^ rel)
            kvs[block] = kv[j]
            kvt[block] = kv[j].astype(WIDE).T.astype(LOW)
    dkv[...] = jnp.zeros(dkv.shape, WIDE)

    def one_query_block(j, carry):
        query_block = 4 * j + group
        queries[:HALF, :], queries[HALF:, :] = padded_queries(q2[j])
        grads[:HALF, :], grads[HALF:, :] = padded_behind(d2[j])
        dot_rows[...] = jnp.sum(grads[...].astype(WIDE).T * out_t[j], axis=0, keepdims=True)
        acc[...] = jnp.zeros((128, BLOCK), WIDE)

        def work(key_block, masked):
            terms = []
            for half in range(2):
                at = slice(half * HALF, half * HALF + HALF)
                scores = nt(kvs[key_block], queries[at, :])
                probs = jnp.exp(scores - total[j][:, at])
                if masked:
                    ok = allowed_keys(key_block, query_block, half, begin[j][:, at])
                    probs = jnp.where(ok, probs, 0.0)
                grad_probs = nt(kvs[key_block], grads[at, :])
                grad_scores = (probs * (grad_probs - dot_rows[:, at])).astype(LOW)
                terms.append(
                    nn(grad_scores, queries[at, :]) + nn(probs.astype(LOW), grads[at, :])
                )
                acc[:, at] += nn(kvt[key_block], grad_scores)
            dkv[key_block] += terms[0] + terms[1]

        for_key_blocks(query_block, 16, work)
        rows = acc[...].T
        x, y = rows[:HALF], rows[HALF:]
        dq2[j] = jnp.where(lane_of(x.shape) < HDIM, x, pltpu.roll(y, HDIM, 1)).astype(LOW)
        return carry

    lax.fori_loop(0, 4, one_query_block, 0)
    for j in range(4):
        for k in range(2):
            keep[k, j] = dkv[4 * j + (group ^ (2 * k))].astype(LOW)
            send[k, j] = dkv[4 * j + (group ^ (2 * k + 1))].astype(LOW)


def branch_kernel(heads2, w, attended, partial):
    for pair in range(2):
        lanes = slice(pair * 128, pair * 128 + 128)
        x, y = exchange_halves(heads2[2 * pair].astype(WIDE), heads2[2 * pair + 1].astype(WIDE))
        attended[:HALF, lanes] = x.astype(LOW)
        attended[HALF:, lanes] = y.astype(LOW)
    for n in range(4):
        at = slice(n * 512, n * 512 + 512)
        partial[:, at] = nn(attended[...], w[:, at]).astype(LOW)


def grad_attended_kernel(grad, w, packed):
    g = nt(grad[...], w[...])
    for pair in range(2):
        lanes = slice(pair * 128, pair * 128 + 128)
        both = exchange_halves(g[:HALF, lanes], g[HALF:, lanes])
        for one in range(2):
            packed[2 * pair + one] = both[one].astype(LOW)


def grad_project_kernel(
    parts, w, cosine, sine, tok, mean, scale, grad_mixed, partial, gain_sum, shift_sum, bias_sum
):
    for pair in range(2):
        lanes = slice(pair * 128, pair * 128 + 128)
        even, odd = parts[2 * pair].astype(WIDE), parts[2 * pair + 1].astype(WIDE)
        k, v = exchange_halves(even[:BLOCK], odd[:BLOCK])
        q = jnp.concatenate(exchange_halves(even[BLOCK:], odd[BLOCK:]), axis=0)
        q = turn(q, cosine[...], sine[...], -1.0) * 0.125
        k = turn(k, cosine[...], sine[...], -1.0)
        for c, part in enumerate((q, k, v)):
            start = c * 256 + pair * 128
            low = part.astype(LOW)
            grad_mixed[:, start : start + 128] = low
            bias_sum[c : c + 1, lanes] = jnp.sum(low.astype(WIDE), axis=0, keepdims=True)
    for n in range(4):
        at = slice(n * 512, n * 512 + 512)
        total = nt(grad_mixed[:, :256], w[0, at, :])
        total += nt(grad_mixed[:, 256:512], w[1, at, :])
        total += nt(grad_mixed[:, 512:], w[2, at, :])
        partial[:, at] = total.astype(LOW)
        normal = (tok[:, at].astype(WIDE) - mean[...]) * scale[...]
        gain_sum[:, at] = jnp.sum(total * normal, axis=0, keepdims=True)
        shift_sum[:, at] = jnp.sum(total, axis=0, keepdims=True)


def weight_kernel(place, left, right, mine, theirs, turned):
    core = place[0]
    turned[...] = left[...].astype(WIDE).T.astype(LOW)

    def one(n, carry):
        both = nn(turned[...], right[:, pl.ds(pl.multiple_of(n * 256, 256), 256)])
        first, second = both[:, :128], both[:, 128:]
        mine[n] = jnp.where(core == 0, first, second).astype(LOW)
        theirs[n] = jnp.where(core == 0, second, first).astype(LOW)
        return carry

    lax.fori_loop(0, 8, one, 0)


def weight_grads(left, right, core):
    width = left.shape[1]
    out = jax.ShapeDtypeStruct((8, width, 128), LOW)
    return kernel_call(
        weight_kernel,
        (out, out),
        (left, right),
        scalars=(core,),
        scratch=(pltpu.VMEM((width, left.shape[0]), LOW),),
        flops=2 * left.size * right.shape[1],
    )


def swapped(x, axis):
    return lax.ppermute(x, axis, [(0, 1), (1, 0)])


def summed_over_ctx(mine, theirs):
    here = (mine.astype(WIDE) + swapped(theirs, "core").astype(WIDE)).astype(LOW)
    rows = here.shape[1]
    here = here.reshape(2, 4, rows, 128)
    z = lax.axis_index(Z)
    total = lax.dynamic_index_in_dim(here, z, 1, False).astype(WIDE)
    for k in range(1, 4):
        part = lax.dynamic_index_in_dim(here, lax.rem(z + k, 4), 1, False)
        total += lax.ppermute(part, Z, [(i, (i + k) % 4) for i in range(4)]).astype(WIDE)
    xh = lax.axis_index("xh")
    other = lax.dynamic_index_in_dim(total, 1 - xh, 0, False).astype(LOW)
    return lax.dynamic_index_in_dim(total, xh, 0, False) + swapped(other, "xh").astype(WIDE)


def everywhere(part, axis):
    copies = jnp.broadcast_to(part, (lax.axis_size(axis), *part.shape))
    return lax.all_to_all(copies, axis, split_axis=0, concat_axis=0, tiled=True)


def tp_share(partial):
    parts = partial.reshape(8, -1, partial.shape[1])
    parts = lax.all_to_all(parts, TP, split_axis=0, concat_axis=0, tiled=True)
    return jnp.sum(parts.astype(WIDE), axis=0)


def tp_gather(share):
    parts = everywhere(share, TP)
    return parts.reshape(-1, share.shape[1])


def norm_forward(values, gain, shift):
    center = values - jnp.mean(values, axis=-1, keepdims=True)
    scaling = lax.rsqrt(jnp.mean(center * center, axis=-1, keepdims=True) + 1e-05)
    normal_rows = center * scaling
    return (normal_rows * gain + shift, normal_rows, scaling)


def norm_backward(grad_out, normal_rows, scaling, gain):
    scaled = grad_out * gain
    return scaling * (
        scaled
        - jnp.mean(scaled, axis=-1, keepdims=True)
        - normal_rows * jnp.mean(scaled * normal_rows, axis=-1, keepdims=True)
    )


def shape_of(*dims, kind=LOW):
    return jax.ShapeDtypeStruct(dims, kind)


def body(
    tokens, cotangent, segment_ids, first_gain, first_shift, second_gain, second_shift,
    w_qkv, qkv_bias, w_out, w_gate_up, w_down,
):
    ctx = lax.axis_index(CTX)
    tp = lax.axis_index(TP)
    group = lax.axis_index(("zl", "core"))
    core = lax.axis_index("core").reshape(1)
    group_here = group.reshape(1)

    def my_share(array):
        return lax.dynamic_slice_in_dim(array, tp * 64, 64)

    labels = jnp.arange(DOCS, dtype=jnp.int32)
    starts = jnp.sum((segment_ids[None, :] < labels[:, None]).astype(jnp.int32), axis=1)
    begins = jnp.sum(
        jnp.where(segment_ids[None, :] == labels[:, None], starts[:, None], 0), axis=0
    )
    begin = lax.dynamic_index_in_dim(begins.reshape(4, 4, 1, BLOCK), group, 1, False)
    own = lax.dynamic_slice_in_dim(begins, ctx * BLOCK, BLOCK)
    places = ctx * BLOCK + jnp.arange(BLOCK, dtype=jnp.int32) - own
    frequency = 10000.0 ** (-jnp.arange(8, dtype=WIDE) / 8.0)
    angles = frequency[:, None] * places.astype(WIDE)[None, :]
    cosine = jnp.cos(angles).T
    sine = jnp.sin(angles).T
    one, zero = jnp.ones((BLOCK, 48), WIDE), jnp.zeros((BLOCK, 48), WIDE)
    cosine = jnp.concatenate([cosine, cosine, one] * 2, axis=1)
    sine = jnp.concatenate([sine, sine, zero] * 2, axis=1)

    w3 = jnp.transpose(w_qkv, (1, 0, 2))
    gain_row, shift_row = first_gain[None], first_shift[None]
    normed_low, mean1, scale1, packed = kernel_call(
        project_kernel,
        (
            shape_of(BLOCK, 2048),
            shape_of(BLOCK, 1, kind=WIDE),
            shape_of(BLOCK, 1, kind=WIDE),
            shape_of(4, 768, 128),
        ),
        (tokens, gain_row, shift_row, w3, qkv_bias, cosine, sine),
        flops=2 * 512 * 2048 * 768,
    )
    spread = lax.all_to_all(packed, SPREAD, split_axis=0, concat_axis=0, tiled=True)
    kv = spread[:, :BLOCK]
    q2 = spread[:, BLOCK:]
    kv_z = swapped(kv, "zl")
    kv_c = swapped(jnp.stack([kv, kv_z]), "core")
    kv_parts = (kv, kv_c[0], kv_z, kv_c[1])
    heads2, out_t, total = kernel_call(
        forward_kernel,
        (shape_of(4, HALF, 128), shape_of(4, 128, BLOCK, kind=WIDE), shape_of(4, 1, BLOCK, kind=WIDE)),
        (begin, *kv_parts, q2),
        scalars=(group_here,),
        scratch=(
            pltpu.VMEM((16, BLOCK, 128), LOW),
            pltpu.VMEM((16, 128, BLOCK), LOW),
            pltpu.VMEM((BLOCK, 128), LOW),
            pltpu.VMEM((1, BLOCK), WIDE),
            pltpu.VMEM((128, BLOCK), WIDE),
        ),
        flops=34 * 4 * BLOCK * BLOCK * 128,
        exps=34 * BLOCK * BLOCK,
    )
    heads2 = lax.all_to_all(heads2, SPREAD, split_axis=0, concat_axis=0, tiled=True)
    attended_low, partial_branch = kernel_call(
        branch_kernel,
        (shape_of(BLOCK, 256), shape_of(BLOCK, 2048)),
        (heads2, w_out),
        flops=2 * 512 * 256 * 2048,
    )
    middle = my_share(tokens).astype(WIDE) + tp_share(partial_branch)
    second, second_rows, second_scale = norm_forward(middle, second_gain, second_shift)
    second_low = tp_gather(second.astype(LOW))

    gate_up = jnp.einsum("td,dcf->tcf", second_low, w_gate_up, preferred_element_type=WIDE)
    gate, up = gate_up[:, 0], gate_up[:, 1]
    sigmoid_gate = jax.nn.sigmoid(gate)
    activated = gate * sigmoid_gate
    hidden_low = (activated * up).astype(LOW)
    grad_hidden = jnp.einsum("td,fd->tf", cotangent, w_down, preferred_element_type=WIDE)
    grad_gate = grad_hidden * up * sigmoid_gate * (1.0 + gate * (1.0 - sigmoid_gate))
    grad_gate = grad_gate.astype(LOW)
    grad_up = (grad_hidden * activated).astype(LOW)
    partial_second = jnp.einsum(
        "tcf,dcf->td", jnp.stack([grad_gate, grad_up], axis=1), w_gate_up, preferred_element_type=WIDE
    ).astype(LOW)
    grad_second = tp_share(partial_second)
    grad_middle = my_share(cotangent).astype(WIDE) + norm_backward(
        grad_second, second_rows, second_scale, second_gain
    )
    grad_branch = tp_gather(grad_middle.astype(LOW))

    partial_feed = jnp.dot(hidden_low, w_down, preferred_element_type=WIDE).astype(LOW)
    layer_out = tp_gather((middle + tp_share(partial_feed)).astype(LOW))

    gate_mine, gate_theirs = weight_grads(grad_gate, second_low, core)
    up_mine, up_theirs = weight_grads(grad_up, second_low, core)
    down_mine, down_theirs = weight_grads(hidden_low, cotangent, core)

    grad2 = kernel_call(
        grad_attended_kernel,
        shape_of(4, HALF, 128),
        (grad_branch, w_out),
        flops=2 * 512 * 256 * 2048,
    )
    grad2 = lax.all_to_all(grad2, SPREAD, split_axis=0, concat_axis=0, tiled=True)
    dq2, keep, send = kernel_call(
        backward_kernel,
        (shape_of(4, HALF, 128), shape_of(2, 4, BLOCK, 128), shape_of(2, 4, BLOCK, 128)),
        (begin, *kv_parts, q2, grad2, out_t, total),
        scalars=(group_here,),
        scratch=(
            pltpu.VMEM((16, BLOCK, 128), LOW),
            pltpu.VMEM((16, 128, BLOCK), LOW),
            pltpu.VMEM((BLOCK, 128), LOW),
            pltpu.VMEM((BLOCK, 128), LOW),
            pltpu.VMEM((1, BLOCK), WIDE),
            pltpu.VMEM((128, BLOCK), WIDE),
            pltpu.VMEM((16, BLOCK, 128), WIDE),
        ),
        flops=34 * 10 * BLOCK * BLOCK * 128,
        exps=34 * BLOCK * BLOCK,
    )
    dkv = keep.astype(WIDE) + swapped(send, "core").astype(WIDE)
    dkv = dkv[0] + swapped(dkv[1].astype(LOW), "zl").astype(WIDE)
    grads = jnp.concatenate([dkv.astype(LOW), dq2], axis=1)
    grads = lax.all_to_all(grads, SPREAD, split_axis=0, concat_axis=0, tiled=True)
    grad_mixed, partial_normed, gain_sum, shift_sum, bias_sum = kernel_call(
        grad_project_kernel,
        (
            shape_of(BLOCK, 768),
            shape_of(BLOCK, 2048),
            shape_of(1, 2048, kind=WIDE),
            shape_of(1, 2048, kind=WIDE),
            shape_of(3, 256, kind=WIDE),
        ),
        (grads, w3, cosine, sine, tokens, mean1, scale1),
        flops=2 * 512 * 2048 * 768,
    )
    grad_normed = tp_share(partial_normed)
    first_rows = (my_share(tokens).astype(WIDE) - my_share(mean1)) * my_share(scale1)
    grad_tokens = grad_middle + norm_backward(grad_normed, first_rows, my_share(scale1), first_gain)
    grad_tokens = tp_gather(grad_tokens.astype(LOW))

    vectors = jnp.concatenate(
        [
            gain_sum,
            shift_sum,
            jnp.sum(grad_second * second_rows, axis=0, keepdims=True),
            jnp.sum(grad_second, axis=0, keepdims=True),
        ],
        axis=0,
    )
    vectors = jnp.sum(everywhere(vectors, TP), axis=0)
    vectors = jnp.concatenate([vectors.reshape(32, 256), bias_sum], axis=0)
    vectors = jnp.sum(everywhere(vectors, CTX), axis=0)
    bias_grad = vectors[32:]
    vectors = vectors[:32].reshape(4, 2048)

    out_mine, out_theirs = weight_grads(attended_low, grad_branch, core)
    qkv_mine, qkv_theirs = weight_grads(grad_mixed, normed_low, core)
    grad_gate_w = summed_over_ctx(gate_mine, gate_theirs)
    grad_up_w = summed_over_ctx(up_mine, up_theirs)
    grad_down_w = summed_over_ctx(down_mine, down_theirs)
    grad_out_w = summed_over_ctx(out_mine, out_theirs)
    grad_qkv_w = summed_over_ctx(qkv_mine, qkv_theirs)
    return (
        layer_out,
        grad_tokens,
        vectors[0],
        vectors[1],
        vectors[2],
        vectors[3],
        jnp.transpose(grad_qkv_w.reshape(3, 256, 128), (2, 0, 1)),
        bias_grad,
        grad_out_w,
        jnp.transpose(jnp.stack([grad_gate_w, grad_up_w]), (2, 0, 1)),
        grad_down_w,
    )


def solution(mesh):
    fine = Mesh(
        mesh.devices.reshape(2, 2, 2, 2, 4, 2), ("xh", "zh", "zl", "core", "y", "xl")
    )
    rows = P(CTX, None)
    return jax.shard_map(
        body,
        mesh=fine,
        in_specs=(
            rows, rows, P(), P(), P(), P(), P(),
            P(None, None, TP), P(None, TP), P(TP, None), P(None, None, TP), P(TP, None),
        ),
        out_specs=(
            rows, rows, P(), P(), P(), P(),
            P(CTX, None, TP), P(None, TP), P(TP, CTX), P(CTX, None, TP), P(TP, CTX),
        ),
        check_vma=False,
    )
```

time: 1060 us -> 552 us (0.52)
  waiting for transfers between devices: 640 us -> 149 us
  local copies, waits for them, and re-layouts: 154 us -> 52.9 us
  Pallas kernels: 0 us -> 86.6 us
  blocking collectives: 40.7 us -> 106 us
  other arithmetic: 82.2 us -> 40 us
  starting transfers between devices: 45.1 us -> 87.1 us
  matrix products: 56.5 us -> 18.6 us
  between operations: 15.3 us -> 2.08 us
  loops' own time: 12.1 us -> 0 us
    reduce_scatter x6 -> x0, waiting for transfers between devices: 439 us -> none  [the longest x4 226 us: tp_share(): lax.psum_scatter(partial_sum.astype(jnp.bfloat16), 'tp', scatter_dimensio...]
    pallas_call x0 -> x11, Pallas kernels: none -> 86.6 us  [kernel_call(): pl.pallas_call(body, out_shape=out_shape, in_specs=in_specs, out_specs=ja...]
    all_gather x1 -> x0, waiting for transfers between devices: 77 us -> none  [sent_together(): filled = lax.all_gather(both, axis, axis=dim, tiled=True)]
    all_to_all x2 -> x5, blocking collectives: 40.7 us -> 106 us  [the longest x2 61.7 us: everywhere(): return lax.all_to_all(copies, axis, split_axis=0, concat_axis=0, tiled=True)]
    ppermute x0 -> x29, waiting for transfers between devices: none -> 55.4 us  [the longest x14 34.1 us: swapped(): return lax.ppermute(x, axis, [(0, 1), (1, 0)])]
    ppermute x0 -> x29, starting transfers between devices: none -> 48.3 us  [the longest x14 29 us: swapped(): return lax.ppermute(x, axis, [(0, 1), (1, 0)])]
    dot_general x19 -> x4, matrix products: 56.5 us -> 18.6 us  [the longest x1 6.33 us: body(): jnp.einsum('td,dcf->tcf', second_low, w_gate_up, preferred_element_type=W...]
    all_to_all x11 -> x9, waiting for transfers between devices: 124 us -> 93.9 us  [the longest x4 71.9 us: tp_share(): parts = lax.all_to_all(parts, TP, split_axis=0, concat_axis=0, tiled=True)]
  transfers between devices with their start and end apart: 18 -> 38, of which waited for: 16 -> 17; matrix products, arithmetic and copies ran while one was open for 13% -> 9% of each run, Pallas kernels for 0% -> 4%
where the time goes in v1:
time: 552 us; the launch traced here: 543 us
  waiting for transfers between devices  149 us (27%)
  blocking collectives  106 us (19%)
  starting transfers between devices  87.1 us (16%)
  Pallas kernels  86.6 us (16%)
  local copies, waits for them, and re-layouts  52.9 us (10%)
  other arithmetic  40 us (7%)
  matrix products  18.6 us (3%)
    pallas_call x11, Pallas kernels, kernel_call(): pl.pallas_call(body, out_shape=out_shape, in_specs=in_specs, out_specs=ja...  86.6 us
    all_to_all x4, waiting for transfers between devices, tp_share(): parts = lax.all_to_all(parts, TP, split_axis=0, concat_axis=0, tiled=True)  71.9 us
    all_to_all x2, blocking collectives, everywhere(): return lax.all_to_all(copies, axis, split_axis=0, concat_axis=0, tiled=True)  61.7 us
    ppermute x14, waiting for transfers between devices, swapped(): return lax.ppermute(x, axis, [(0, 1), (1, 0)])  34.1 us
    unnamed x156, local copies, waits for them, and re-layouts  32 us
    ppermute x14, starting transfers between devices, swapped(): return lax.ppermute(x, axis, [(0, 1), (1, 0)])  29 us
    all_to_all x1, blocking collectives, body(): lax.all_to_all(packed, SPREAD, split_axis=0, concat_axis=0, tiled=True)  21.8 us
    ppermute x15, waiting for transfers between devices, summed_over_ctx(): lax.ppermute(part, Z, [(i, (i + k) % 4) for i in range(4)]).astype(WIDE)  21.3 us
  transfers between devices with their start and end apart: 38, of which 17 were waited for; matrix products, arithmetic and copies ran while one was open for 9% of the time, Pallas kernels for 4%

profile of v1, /device:TPU:0, one launch (start us, length us, event | category | flops | bytes accessed | tf_op | source)
XLA Modules:
  0.0 542.9 jit_solution(3719748467851786493)
XLA Ops:
  11.1 6.4 %shard_map.203 = (bf16[512,2048]{1,0:T(8,128)(2,1)S(1)}, f32[512,1]{1,0:T(8,128)S(1)}, f32[512,1]{1,0:T(8,128)S(1)}, bf16[4,768,128]{2,1,0:T(8,128)(2,1)S(1)}) custom-call(bf16[512,2048]{1,0:T(8,128)(2,1)S(1)} %copy-done.2, f32[1,2048]{1,0:T(1,128)S(1)} %bitcast.174, f32[1,2048]{1,0:T(1,128)S(1)} %bitcast.175, bf16[3,2048,256]{2,1,0:T(8,128)(2,1)} %bitcast.186, ...), custom_call_target="tpu_custom_call" | custom-call | flops 1610612736 | bytes 8674304 | tf_op jit(solution)/shard_map/pallas_call | solution.py:28
  17.5 21.8 %all_to_all.70 = bf16[4,768,128]{2,1,0:T(8,128)(2,1)S(1)} all-to-all(bf16[4,768,128]{2,1,0:T(8,128)(2,1)S(1)} %get-tuple-element.38), channel_id=1, replica_groups=mesh['xh'=2,'zh'=2,'zl'=2,'core'=2,'y'=4,'xl'=2] {'xh','zh'}, dimensions={0} | all-to-all | bytes 1572864 | tf_op jit(solution)/shard_map/all_to_all | solution.py:397
  41.4 10.3 %collective-permute-done.kv2 = bf16[4,512,128]{2,1,0:T(8,128)(2,1)S(1)} collective-permute-done((bf16[4,512,128]{2,1,0:T(8,128)(2,1)S(1)}, bf16[4,512,128]{2,1,0:T(8,128)(2,1)S(1)}, u32[]{:S(2)}, u32[]{:S(2)}) %collective-permute-start) | collective-permute-done | bytes 524320 | tf_op jit(solution)/shard_map/ppermute | solution.py:302
  57.9 28.5 %shard_map.204 = (bf16[4,256,128]{2,1,0:T(8,128)(2,1)S(1)}, f32[4,128,512]{2,1,0:T(8,128)S(1)}, f32[4,1,512]{2,1,0:T(1,128)S(1)}) custom-call(s32[1]{0:T(128)} %bitcast.place, s32[4,1,512]{2,1,0:T(1,128)S(1)} %fusion.32.begin, bf16[4,512,128]{2,1,0:T(8,128)(2,1)S(1)} %copy-done.17, bf16[4,512,128]{2,1,0:T(8,128)(2,1)S(1)} %get-tuple-element.136.kv1, ...), custom_call_target="tpu_custom_call" | custom-call | flops 4563402752 | bytes 3686400 | tf_op jit(solution)/shard_map/pallas_call | solution.py:28
  87.5 11.2 %all_to_all.71.heads2 = bf16[4,256,128]{2,1,0:T(8,128)(2,1)S(1)} all-to-all(bf16[4,256,128]{2,1,0:T(8,128)(2,1)S(1)} %get-tuple-element.39), channel_id=1, replica_groups=mesh['xh'=2,'zh'=2,'zl'=2,'core'=2,'y'=4,'xl'=2] {'xh','zh'}, dimensions={0} | all-to-all | bytes 524288 | tf_op jit(solution)/shard_map/all_to_all | solution.py:418
  101.5 4.5 all-to-all-start.2
  106.0 26.9 %all-to-all-done.2 = bf16[8,64,2048]{2,1,0:T(8,128)(2,1)} async-done(((bf16[8,64,2048]{2,1,0:T(8,128)(2,1)}), bf16[8,64,2048]{2,1,0:T(8,128)(2,1)}, u32[]{:S(2)}, u32[]{:S(2)}) %all-to-all-start.2) | async-done | bytes 2097184 | tf_op jit(solution)/shard_map/all_to_all | solution.py:326
  137.3 31.6 %all_to_all.72 = bf16[8,64,2048]{2,1,0:T(8,128)(2,1)S(1)} all-to-all(bf16[8,64,2048]{2,1,0:T(8,128)(2,1)S(1)} %broadcast_in_dim.71), channel_id=1, replica_groups=mesh['xh'=2,'zh'=2,'zl'=2,'core'=2,'y'=4,'xl'=2] {'y','xl'}, dimensions={0} | all-to-all | bytes 4194304 | tf_op jit(solution)/shard_map/all_to_all | solution.py:321
  168.9 6.3 %fusion.36 = f32[512,2,704]{2,0,1:T(8,128)S(1)} fusion(bf16[512,2048,1]{1,0,2:T(8,128)(2,1)S(1)} %bitcast.169, bf16[2048,2,704]{0,2,1:T(8,128)(2,1)} %param.22), kind=kOutput, calls=%fused_computation.127 | convolution fusion | flops 2952790016 | bytes 10747904 | tf_op jit(solution)/shard_map/td,dcf->tcf/dot_general | solution.py:429
  175.3 3.3 multiply_convert_fusion.1
  178.6 4.7 bitcast_convert_fusion
  183.3 4.4 all-to-all-start.6
  187.7 4.3 convolution_convert_fusion
  192.0 21.9 %all-to-all-done.6 = bf16[8,64,2048]{2,1,0:T(8,128)(2,1)} async-done(((bf16[8,64,2048]{2,1,0:T(8,128)(2,1)}), bf16[8,64,2048]{2,1,0:T(8,128)(2,1)}, u32[]{:S(2)}, u32[]{:S(2)}) %all-to-all-start.6) | async-done | bytes 2097184 | tf_op jit(solution)/shard_map/all_to_all | solution.py:326
  213.8 3.6 all-to-all-start.4
  220.6 23.1 %all-to-all-done.4 = bf16[8,64,2048]{2,1,0:T(8,128)(2,1)S(1)} async-done(((bf16[8,64,2048]{2,1,0:T(8,128)(2,1)}), bf16[8,64,2048]{2,1,0:T(8,128)(2,1)S(1)}, u32[]{:S(2)}, u32[]{:S(2)}) %all-to-all-start.4) | async-done | bytes 2097184 | tf_op jit(solution)/shard_map/all_to_all | solution.py:326
  247.2 30.0 %all_to_all.73 = bf16[8,64,2048]{2,1,0:T(8,128)(2,1)S(1)} all-to-all(bf16[8,64,2048]{2,1,0:T(8,128)(2,1)S(1)} %broadcast_in_dim.73), channel_id=1, replica_groups=mesh['xh'=2,'zh'=2,'zl'=2,'core'=2,'y'=4,'xl'=2] {'y','xl'}, dimensions={0} | all-to-all | bytes 4194304 | tf_op jit(solution)/shard_map/all_to_all | solution.py:321
  278.1 11.6 %all_to_all.74.d2 = bf16[4,256,128]{2,1,0:T(8,128)(2,1)S(1)} all-to-all(bf16[4,256,128]{2,1,0:T(8,128)(2,1)S(1)} %shard_map.206), channel_id=1, replica_groups=mesh['xh'=2,'zh'=2,'zl'=2,'core'=2,'y'=4,'xl'=2] {'xh','zh'}, dimensions={0} | all-to-all | bytes 524288 | tf_op jit(solution)/shard_map/all_to_all | solution.py:460
  289.7 25.8 %shard_map.207 = (bf16[4,256,128]{2,1,0:T(8,128)(2,1)S(1)}, bf16[2,4,512,128]{3,2,1,0:T(8,128)(2,1)S(1)}, bf16[2,4,512,128]{3,2,1,0:T(8,128)(2,1)S(1)}) custom-call(s32[1]{0:T(128)} %bitcast.place, s32[4,1,512]{2,1,0:T(1,128)S(1)} %fusion.32.begin, bf16[4,512,128]{2,1,0:T(8,128)(2,1)S(1)} %copy-done.18, bf16[4,512,128]{2,1,0:T(8,128)(2,1)S(1)} %copy-done.25, ...), custom_call_target="tpu_custom_call" | custom-call | flops 11408506880 | bytes 6045696 | tf_op jit(solution)/shard_map/pallas_call | solution.py:28
  318.7 15.8 %collective-permute-start.3 = (bf16[4,512,128]{2,1,0:T(8,128)(2,1)S(1)}, bf16[4,512,128]{2,1,0:T(8,128)(2,1)S(1)}, u32[]{:S(2)}, u32[]{:S(2)}) collective-permute-start(bf16[4,512,128]{2,1,0:T(8,128)(2,1)S(1)} %fusion.22), channel_id=1, source_target_pairs={{0,16},{16,0},{1,17},{17,1},{2,18},{18,2},{3,19},{19,3},{4,20},{20... | collective-permute-start | bytes 1572872 | tf_op jit(solution)/shard_map/ppermute | solution.py:302
  334.6 4.3 shard_map.213
  339.0 4.3 shard_map.211
  348.1 3.5 all-to-all-start.9
  354.3 4.3 shard_map.212
  361.1 3.0 all-to-all-done.9.parts
  366.0 5.1 shard_map.208
  374.1 3.4 all-to-all-start.12
  383.3 3.6 collective-permute-start.26
  388.1 5.6 %all-to-all-start.10 = ((bf16[8,64,2048]{2,1,0:T(8,128)(2,1)}), bf16[8,64,2048]{2,1,0:T(8,128)(2,1)}, u32[]{:S(2)}, u32[]{:S(2)}) async-start(bf16[8,64,2048]{2,1,0:T(8,128)(2,1)} %bitcast.168), calls=%async_computation.10 | async-start | bytes 4194304 | tf_op jit(solution)/shard_map/all_to_all | solution.py:326
  399.7 2.8 collective-permute-start.17
  408.5 8.1 %collective-permute-done.15 = bf16[2,704,128]{2,1,0:T(8,128)(2,1)S(1)} collective-permute-done((bf16[2,704,128]{2,1,0:T(8,128)(2,1)S(1)}, bf16[2,704,128]{2,1,0:T(8,128)(2,1)S(1)}, u32[]{:S(2)}, u32[]{:S(2)}) %collective-permute-start.15) | collective-permute-done | bytes 360480 | tf_op jit(solution)/shard_map/ppermute | solution.py:313
  416.6 3.0 collective-permute-done.16
  421.2 2.9 collective-permute-start.18
  424.1 3.1 collective-permute-done.20
  427.2 5.4 collective-permute-done.21
  433.6 3.2 collective-permute-start.23
  441.5 4.9 all-to-all-start.5
  455.1 2.9 collective-permute-start.11
  458.4 4.4 shard_map.209
  467.5 6.6 %all-to-all-done.5 = bf16[8,64,2048]{2,1,0:T(8,128)(2,1)} async-done(((bf16[8,64,2048]{2,1,0:T(8,128)(2,1)}), bf16[8,64,2048]{2,1,0:T(8,128)(2,1)}, u32[]{:S(2)}, u32[]{:S(2)}) %all-to-all-start.5) | async-done | bytes 2097184 | tf_op jit(solution)/shard_map/all_to_all | solution.py:321
  475.0 4.5 all-to-all-start.13
  480.7 12.5 %all-to-all-done.13 = f32[16,35,256]{2,1,0:T(8,128)S(1)} async-done(((f32[16,35,256]{2,1,0:T(8,128)}), f32[16,35,256]{2,1,0:T(8,128)S(1)}, u32[]{:S(2)}, u32[]{:S(2)}) %all-to-all-start.13) | async-done | bytes 573472 | tf_op jit(solution)/shard_map/all_to_all | solution.py:321
  494.8 4.5 all-to-all-start.11
  509.8 14.9 %collective-permute-done.13 = bf16[256,128]{1,0:T(8,128)(2,1)S(1)} collective-permute-done((bf16[256,128]{1,0:T(8,128)(2,1)S(1)}, bf16[256,128]{1,0:T(8,128)(2,1)S(1)}, u32[]{:S(2)}, u32[]{:S(2)}) %collective-permute-start.13) | collective-permute-done | bytes 65568 | tf_op jit(solution)/shard_map/ppermute | solution.py:302
  527.4 2.6 collective-permute-start.8
  532.4 2.6 collective-permute-done.8
  536.0 3.3 copy.102
  539.3 3.2 copy.103
  (279 shorter events, 112.5 us)
Async XLA Ops:
  0.6 174.7 %copy-start = (bf16[704,2048]{1,0:T(8,128)(2,1)S(1)}, bf16[704,2048]{1,0:T(8,128)(2,1)}, u32[]{:S(2)}) copy-start(bf16[704,2048]{1,0:T(8,128)(2,1)} %param.23) | copy-start | bytes 8650756
  17.5 35.3 %copy-start.26 = (f32[512,1]{1,0:T(8,128)}, f32[512,1]{1,0:T(8,128)S(1)}, u32[]{:S(2)}) copy-start(f32[512,1]{1,0:T(8,128)S(1)} %get-tuple-element.47.mean) | copy-start | bytes 6148
  17.5 35.3 %copy-start.28 = (f32[512,1]{1,0:T(8,128)}, f32[512,1]{1,0:T(8,128)S(1)}, u32[]{:S(2)}) copy-start(f32[512,1]{1,0:T(8,128)S(1)} %get-tuple-element.41.scale) | copy-start | bytes 6148
  17.5 35.3 %copy-start.45 = (bf16[512,2048]{1,0:T(8,128)(2,1)}, bf16[512,2048]{1,0:T(8,128)(2,1)S(1)}, u32[]{:S(2)}) copy-start(bf16[512,2048]{1,0:T(8,128)(2,1)S(1)} %get-tuple-element.53.right) | copy-start | bytes 6291460
  39.5 12.2 %collective-permute-start = (bf16[4,512,128]{2,1,0:T(8,128)(2,1)S(1)}, bf16[4,512,128]{2,1,0:T(8,128)(2,1)S(1)}, u32[]{:S(2)}, u32[]{:S(2)}) collective-permute-start(bf16[4,512,128]{2,1,0:T(8,128)(2,1)S(1)} %get-tuple-element.138.kv0), channel_id=1, source_target_pairs={{0,16},{16,0},{1,17},{17,1},{2,18},{18,2},{3,19},{19,3},{4,20},{20... | collective-permute-start | bytes 1572872 | tf_op jit(solution)/shard_map/ppermute | solution.py:302
  53.5 3.0 collective-permute-start.1
  54.7 31.7 %copy-start.32 = (bf16[4,256,128]{2,1,0:T(8,128)(2,1)}, bf16[4,256,128]{2,1,0:T(8,128)(2,1)S(1)}, u32[]{:S(2)}) copy-start(bf16[4,256,128]{2,1,0:T(8,128)(2,1)S(1)} %slice.65.q2) | copy-start | bytes 786436
  57.9 40.8 %copy-start.14 = (bf16[256,2048]{1,0:T(8,128)(2,1)S(1)}, bf16[256,2048]{1,0:T(8,128)(2,1)}, u32[]{:S(2)}) copy-start(bf16[256,2048]{1,0:T(8,128)(2,1)} %w.3) | copy-start | bytes 3145732
  101.5 31.5 %all-to-all-start.2 = ((bf16[8,64,2048]{2,1,0:T(8,128)(2,1)}), bf16[8,64,2048]{2,1,0:T(8,128)(2,1)}, u32[]{:S(2)}, u32[]{:S(2)}) async-start(bf16[8,64,2048]{2,1,0:T(8,128)(2,1)} %bitcast.172), calls=%async_computation.2 | async-start | bytes 4194304 | tf_op jit(solution)/shard_map/all_to_all | solution.py:326
  106.0 30.9 %copy-start.69 = (f32[2048]{0:T(1024)S(1)}, f32[2048]{0:T(1024)}, u32[]{:S(2)}) copy-start(f32[2048]{0:T(1024)} %param.17) | copy-start | bytes 24580
  106.0 30.9 %copy-start.70 = (f32[2048]{0:T(1024)S(1)}, f32[2048]{0:T(1024)}, u32[]{:S(2)}) copy-start(f32[2048]{0:T(1024)} %param.18) | copy-start | bytes 24580
  137.3 41.3 %slice-start = ((s8[5767168]{0:T(1024)(128)(4,1)}), s8[4194304]{0:T(1024)(128)(4,1)S(1)}, s32[]{:S(2)}) async-start(s8[5767168]{0:T(1024)(128)(4,1)} %bitcast.199), calls=%async_computation.14 | async-start | bytes 8388608
  183.3 30.5 %all-to-all-start.6 = ((bf16[8,64,2048]{2,1,0:T(8,128)(2,1)}), bf16[8,64,2048]{2,1,0:T(8,128)(2,1)}, u32[]{:S(2)}, u32[]{:S(2)}) async-start(bf16[8,64,2048]{2,1,0:T(8,128)(2,1)} %bitcast.191), calls=%async_computation.6 | async-start | bytes 4194304 | tf_op jit(solution)/shard_map/all_to_all | solution.py:326
  213.8 29.8 %all-to-all-start.4 = ((bf16[8,64,2048]{2,1,0:T(8,128)(2,1)}), bf16[8,64,2048]{2,1,0:T(8,128)(2,1)S(1)}, u32[]{:S(2)}, u32[]{:S(2)}) async-start(bf16[8,64,2048]{2,1,0:T(8,128)(2,1)} %bitcast.190), calls=%async_computation.4 | async-start | bytes 4194304 | tf_op jit(solution)/shard_map/all_to_all | solution.py:326
  247.2 30.1 %copy-start.15 = (bf16[256,2048]{1,0:T(8,128)(2,1)S(1)}, bf16[256,2048]{1,0:T(8,128)(2,1)}, u32[]{:S(2)}) copy-start(bf16[256,2048]{1,0:T(8,128)(2,1)} %w.3) | copy-start | bytes 3145732
  315.5 3.0 collective-permute-start.2
  318.7 28.3 %collective-permute-start.3 = (bf16[4,512,128]{2,1,0:T(8,128)(2,1)S(1)}, bf16[4,512,128]{2,1,0:T(8,128)(2,1)S(1)}, u32[]{:S(2)}, u32[]{:S(2)}) collective-permute-start(bf16[4,512,128]{2,1,0:T(8,128)(2,1)S(1)} %fusion.22), channel_id=1, source_target_pairs={{0,16},{16,0},{1,17},{17,1},{2,18},{18,2},{3,19},{19,3},{4,20},{20... | collective-permute-start | bytes 1572872 | tf_op jit(solution)/shard_map/ppermute | solution.py:302
  338.9 38.6 %collective-permute-start.24 = (bf16[8,704,128]{2,1,0:T(8,128)(2,1)}, bf16[8,704,128]{2,1,0:T(8,128)(2,1)}, u32[]{:S(2)}, u32[]{:S(2)}) collective-permute-start(bf16[8,704,128]{2,1,0:T(8,128)(2,1)} %get-tuple-element.64), channel_id=1, source_target_pairs={{0,8},{8,0},{1,9},{9,1},{2,10},{10,2},{3,11},{11,3},{4,12},{12,4},... | collective-permute-start | bytes 4325384 | tf_op jit(solution)/shard_map/ppermute | solution.py:302
  344.4 49.3 %collective-permute-start.14 = (bf16[8,704,128]{2,1,0:T(8,128)(2,1)}, bf16[8,704,128]{2,1,0:T(8,128)(2,1)}, u32[]{:S(2)}, u32[]{:S(2)}) collective-permute-start(bf16[8,704,128]{2,1,0:T(8,128)(2,1)} %get-tuple-element.60), channel_id=1, source_target_pairs={{0,8},{8,0},{1,9},{9,1},{2,10},{10,2},{3,11},{11,3},{4,12},{12,4},... | collective-permute-start | bytes 4325384 | tf_op jit(solution)/shard_map/ppermute | solution.py:302
  348.1 16.0 %all-to-all-start.9 = ((bf16[4,768,128]{2,1,0:T(8,128)(2,1)}), bf16[4,768,128]{2,1,0:T(8,128)(2,1)S(1)}, u32[]{:S(2)}, u32[]{:S(2)}) async-start(bf16[4,768,128]{2,1,0:T(8,128)(2,1)} %pad_maximum_fusion.1), calls=%async_computation.9 | async-start | bytes 1572864 | tf_op jit(solution)/shard_map/all_to_all | solution.py:481
  359.7 38.2 %collective-permute-start.19 = (bf16[8,704,128]{2,1,0:T(8,128)(2,1)}, bf16[8,704,128]{2,1,0:T(8,128)(2,1)}, u32[]{:S(2)}, u32[]{:S(2)}) collective-permute-start(bf16[8,704,128]{2,1,0:T(8,128)(2,1)} %get-tuple-element.62), channel_id=1, source_target_pairs={{0,8},{8,0},{1,9},{9,1},{2,10},{10,2},{3,11},{11,3},{4,12},{12,4},... | collective-permute-start | bytes 4325384 | tf_op jit(solution)/shard_map/ppermute | solution.py:302
  374.1 13.3 %all-to-all-start.12 = ((f32[8,4,2048]{2,1,0:T(4,128)}), f32[8,4,2048]{2,1,0:T(4,128)S(1)}, u32[]{:S(2)}, u32[]{:S(2)}) async-start(f32[8,4,2048]{2,1,0:T(4,128)} %broadcast_in_dim.77), calls=%async_computation.12 | async-start | bytes 524288 | tf_op jit(solution)/shard_map/all_to_all | solution.py:321
  381.8 17.9 %collective-permute-start.25 = (bf16[2,704,128]{2,1,0:T(8,128)(2,1)}, bf16[2,704,128]{2,1,0:T(8,128)(2,1)S(1)}, u32[]{:S(2)}, u32[]{:S(2)}) collective-permute-start(bf16[2,704,128]{2,1,0:T(8,128)(2,1)} %get-tuple-element.126), channel_id=1, source_target_pairs={{0,16},{16,32},{32,48},{48,0},{1,17},{17,33},{33,49},{49,1},{2,18}... | collective-permute-start | bytes 1081352 | tf_op jit(solution)/shard_map/ppermute | solution.py:313
  383.3 20.9 %collective-permute-start.26 = (bf16[2,704,128]{2,1,0:T(8,128)(2,1)}, bf16[2,704,128]{2,1,0:T(8,128)(2,1)S(1)}, u32[]{:S(2)}, u32[]{:S(2)}) collective-permute-start(bf16[2,704,128]{2,1,0:T(8,128)(2,1)} %get-tuple-element.128), channel_id=1, source_target_pairs={{0,32},{16,48},{32,0},{48,16},{1,33},{17,49},{33,1},{49,17},{2,34}... | collective-permute-start | bytes 1081352 | tf_op jit(solution)/shard_map/ppermute | solution.py:313
  386.9 17.3 %collective-permute-start.27 = (bf16[2,704,128]{2,1,0:T(8,128)(2,1)}, bf16[2,704,128]{2,1,0:T(8,128)(2,1)}, u32[]{:S(2)}, u32[]{:S(2)}) collective-permute-start(bf16[2,704,128]{2,1,0:T(8,128)(2,1)} %get-tuple-element.127), channel_id=1, source_target_pairs={{0,48},{16,0},{32,16},{48,32},{1,49},{17,1},{33,17},{49,33},{2,50}... | collective-permute-start | bytes 1081352 | tf_op jit(solution)/shard_map/ppermute | solution.py:313
  388.1 50.8 %all-to-all-start.10 = ((bf16[8,64,2048]{2,1,0:T(8,128)(2,1)}), bf16[8,64,2048]{2,1,0:T(8,128)(2,1)}, u32[]{:S(2)}, u32[]{:S(2)}) async-start(bf16[8,64,2048]{2,1,0:T(8,128)(2,1)} %bitcast.168), calls=%async_computation.10 | async-start | bytes 4194304 | tf_op jit(solution)/shard_map/all_to_all | solution.py:326
  396.0 20.6 %collective-permute-start.15 = (bf16[2,704,128]{2,1,0:T(8,128)(2,1)S(1)}, bf16[2,704,128]{2,1,0:T(8,128)(2,1)S(1)}, u32[]{:S(2)}, u32[]{:S(2)}) collective-permute-start(bf16[2,704,128]{2,1,0:T(8,128)(2,1)S(1)} %get-tuple-element.129), channel_id=1, source_target_pairs={{0,16},{16,32},{32,48},{48,0},{1,17},{17,33},{33,49},{49,1},{2,18}... | collective-permute-start | bytes 1081352 | tf_op jit(solution)/shard_map/ppermute | solution.py:313
  397.8 21.8 %collective-permute-start.16 = (bf16[2,704,128]{2,1,0:T(8,128)(2,1)S(1)}, bf16[2,704,128]{2,1,0:T(8,128)(2,1)S(1)}, u32[]{:S(2)}, u32[]{:S(2)}) collective-permute-start(bf16[2,704,128]{2,1,0:T(8,128)(2,1)S(1)} %get-tuple-element.131), channel_id=1, source_target_pairs={{0,32},{16,48},{32,0},{48,16},{1,33},{17,49},{33,1},{49,17},{2,34}... | collective-permute-start | bytes 1081352 | tf_op jit(solution)/shard_map/ppermute | solution.py:313
  399.7 20.5 %collective-permute-start.17 = (bf16[2,704,128]{2,1,0:T(8,128)(2,1)S(1)}, bf16[2,704,128]{2,1,0:T(8,128)(2,1)S(1)}, u32[]{:S(2)}, u32[]{:S(2)}) collective-permute-start(bf16[2,704,128]{2,1,0:T(8,128)(2,1)S(1)} %get-tuple-element.130), channel_id=1, source_target_pairs={{0,48},{16,0},{32,16},{48,32},{1,49},{17,1},{33,17},{49,33},{2,50}... | collective-permute-start | bytes 1081352 | tf_op jit(solution)/shard_map/ppermute | solution.py:313
  404.1 23.1 %collective-permute-start.20 = (bf16[2,704,128]{2,1,0:T(8,128)(2,1)S(1)}, bf16[2,704,128]{2,1,0:T(8,128)(2,1)S(1)}, u32[]{:S(2)}, u32[]{:S(2)}) collective-permute-start(bf16[2,704,128]{2,1,0:T(8,128)(2,1)S(1)} %get-tuple-element.132), channel_id=1, source_target_pairs={{0,16},{16,32},{32,48},{48,0},{1,17},{17,33},{33,49},{49,1},{2,18}... | collective-permute-start | bytes 1081352 | tf_op jit(solution)/shard_map/ppermute | solution.py:313
  404.9 27.8 %collective-permute-start.21 = (bf16[2,704,128]{2,1,0:T(8,128)(2,1)S(1)}, bf16[2,704,128]{2,1,0:T(8,128)(2,1)S(1)}, u32[]{:S(2)}, u32[]{:S(2)}) collective-permute-start(bf16[2,704,128]{2,1,0:T(8,128)(2,1)S(1)} %get-tuple-element.134), channel_id=1, source_target_pairs={{0,32},{16,48},{32,0},{48,16},{1,33},{17,49},{33,1},{49,17},{2,34}... | collective-permute-start | bytes 1081352 | tf_op jit(solution)/shard_map/ppermute | solution.py:313
  416.6 16.0 %collective-permute-start.22 = (bf16[2,704,128]{2,1,0:T(8,128)(2,1)S(1)}, bf16[2,704,128]{2,1,0:T(8,128)(2,1)S(1)}, u32[]{:S(2)}, u32[]{:S(2)}) collective-permute-start(bf16[2,704,128]{2,1,0:T(8,128)(2,1)S(1)} %get-tuple-element.133), channel_id=1, source_target_pairs={{0,48},{16,0},{32,16},{48,32},{1,49},{17,1},{33,17},{49,33},{2,50}... | collective-permute-start | bytes 1081352 | tf_op jit(solution)/shard_map/ppermute | solution.py:313
  419.6 26.7 %collective-permute-start.28 = (bf16[704,128]{1,0:T(8,128)(2,1)}, bf16[704,128]{1,0:T(8,128)(2,1)}, u32[]{:S(2)}, u32[]{:S(2)}) collective-permute-start(bf16[704,128]{1,0:T(8,128)(2,1)} %fusion.30), channel_id=1, source_target_pairs={{0,64},{64,0},{1,65},{65,1},{2,66},{66,2},{3,67},{67,3},{4,68},{68... | collective-permute-start | bytes 540680 | tf_op jit(solution)/shard_map/ppermute | solution.py:302
  421.2 26.8 %collective-permute-start.18 = (bf16[704,128]{1,0:T(8,128)(2,1)}, bf16[704,128]{1,0:T(8,128)(2,1)}, u32[]{:S(2)}, u32[]{:S(2)}) collective-permute-start(bf16[704,128]{1,0:T(8,128)(2,1)} %fusion.28), channel_id=1, source_target_pairs={{0,64},{64,0},{1,65},{65,1},{2,66},{66,2},{3,67},{67,3},{4,68},{68... | collective-permute-start | bytes 540680 | tf_op jit(solution)/shard_map/ppermute | solution.py:302
  433.6 16.4 %collective-permute-start.23 = (bf16[704,128]{1,0:T(8,128)(2,1)}, bf16[704,128]{1,0:T(8,128)(2,1)}, u32[]{:S(2)}, u32[]{:S(2)}) collective-permute-start(bf16[704,128]{1,0:T(8,128)(2,1)} %fusion.29), channel_id=1, source_target_pairs={{0,64},{64,0},{1,65},{65,1},{2,66},{66,2},{3,67},{67,3},{4,68},{68... | collective-permute-start | bytes 540680 | tf_op jit(solution)/shard_map/ppermute | solution.py:302
  438.8 13.1 %collective-permute-start.9 = (bf16[8,256,128]{2,1,0:T(8,128)(2,1)S(1)}, bf16[8,256,128]{2,1,0:T(8,128)(2,1)}, u32[]{:S(2)}, u32[]{:S(2)}) collective-permute-start(bf16[8,256,128]{2,1,0:T(8,128)(2,1)S(1)} %get-tuple-element.58), channel_id=1, source_target_pairs={{0,8},{8,0},{1,9},{9,1},{2,10},{10,2},{3,11},{11,3},{4,12},{12,4},... | collective-permute-start | bytes 1572872 | tf_op jit(solution)/shard_map/ppermute | solution.py:302
  441.5 32.6 %all-to-all-start.5 = ((bf16[8,64,2048]{2,1,0:T(8,128)(2,1)}), bf16[8,64,2048]{2,1,0:T(8,128)(2,1)}, u32[]{:S(2)}, u32[]{:S(2)}) async-start(bf16[8,64,2048]{2,1,0:T(8,128)(2,1)} %broadcast_in_dim.72), calls=%async_computation.5 | async-start | bytes 4194304 | tf_op jit(solution)/shard_map/all_to_all | solution.py:321
  454.0 45.3 %collective-permute-start.10 = (bf16[2,256,128]{2,1,0:T(8,128)(2,1)}, bf16[2,256,128]{2,1,0:T(8,128)(2,1)S(1)}, u32[]{:S(2)}, u32[]{:S(2)}) collective-permute-start(bf16[2,256,128]{2,1,0:T(8,128)(2,1)} %get-tuple-element.139), channel_id=1, source_target_pairs={{0,16},{16,32},{32,48},{48,0},{1,17},{17,33},{33,49},{49,1},{2,18}... | collective-permute-start | bytes 393224 | tf_op jit(solution)/shard_map/ppermute | solution.py:313
  455.1 44.2 %collective-permute-start.11 = (bf16[2,256,128]{2,1,0:T(8,128)(2,1)}, bf16[2,256,128]{2,1,0:T(8,128)(2,1)}, u32[]{:S(2)}, u32[]{:S(2)}) collective-permute-start(bf16[2,256,128]{2,1,0:T(8,128)(2,1)} %get-tuple-element.141), channel_id=1, source_target_pairs={{0,32},{16,48},{32,0},{48,16},{1,33},{17,49},{33,1},{49,17},{2,34}... | collective-permute-start | bytes 393224 | tf_op jit(solution)/shard_map/ppermute | solution.py:313
  458.0 41.3 %collective-permute-start.12 = (bf16[2,256,128]{2,1,0:T(8,128)(2,1)}, bf16[2,256,128]{2,1,0:T(8,128)(2,1)}, u32[]{:S(2)}, u32[]{:S(2)}) collective-permute-start(bf16[2,256,128]{2,1,0:T(8,128)(2,1)} %get-tuple-element.140), channel_id=1, source_target_pairs={{0,48},{16,0},{32,16},{48,32},{1,49},{17,1},{33,17},{49,33},{2,50}... | collective-permute-start | bytes 393224 | tf_op jit(solution)/shard_map/ppermute | solution.py:313
  464.1 36.3 %collective-permute-start.4 = (bf16[8,768,128]{2,1,0:T(8,128)(2,1)}, bf16[8,768,128]{2,1,0:T(8,128)(2,1)}, u32[]{:S(2)}, u32[]{:S(2)}) collective-permute-start(bf16[8,768,128]{2,1,0:T(8,128)(2,1)} %get-tuple-element.55), channel_id=1, source_target_pairs={{0,8},{8,0},{1,9},{9,1},{2,10},{10,2},{3,11},{11,3},{4,12},{12,4},... | collective-permute-start | bytes 4718600 | tf_op jit(solution)/shard_map/ppermute | solution.py:302
  475.0 18.2 %all-to-all-start.13 = ((f32[16,35,256]{2,1,0:T(8,128)}), f32[16,35,256]{2,1,0:T(8,128)S(1)}, u32[]{:S(2)}, u32[]{:S(2)}) async-start(f32[16,35,256]{2,1,0:T(8,128)} %broadcast_in_dim.78), calls=%async_computation.13 | async-start | bytes 1310720 | tf_op jit(solution)/shard_map/all_to_all | solution.py:321
  494.8 41.2 %all-to-all-start.11 = ((bf16[8,64,2048]{2,1,0:T(8,128)(2,1)}), bf16[8,64,2048]{2,1,0:T(8,128)(2,1)}, u32[]{:S(2)}, u32[]{:S(2)}) async-start(bf16[8,64,2048]{2,1,0:T(8,128)(2,1)} %broadcast_in_dim.74), calls=%async_computation.11 | async-start | bytes 4194304 | tf_op jit(solution)/shard_map/all_to_all | solution.py:321
  504.2 21.8 %collective-permute-start.5 = (bf16[2,768,128]{2,1,0:T(8,128)(2,1)}, bf16[2,768,128]{2,1,0:T(8,128)(2,1)S(1)}, u32[]{:S(2)}, u32[]{:S(2)}) collective-permute-start(bf16[2,768,128]{2,1,0:T(8,128)(2,1)} %get-tuple-element.123), channel_id=1, source_target_pairs={{0,16},{16,32},{32,48},{48,0},{1,17},{17,33},{33,49},{49,1},{2,18}... | collective-permute-start | bytes 1179656 | tf_op jit(solution)/shard_map/ppermute | solution.py:313
  504.2 21.8 %collective-permute-start.6 = (bf16[2,768,128]{2,1,0:T(8,128)(2,1)S(1)}, bf16[2,768,128]{2,1,0:T(8,128)(2,1)S(1)}, u32[]{:S(2)}, u32[]{:S(2)}) collective-permute-start(bf16[2,768,128]{2,1,0:T(8,128)(2,1)S(1)} %get-tuple-element.125), channel_id=1, source_target_pairs={{0,32},{16,48},{32,0},{48,16},{1,33},{17,49},{33,1},{49,17},{2,34}... | collective-permute-start | bytes 1179656 | tf_op jit(solution)/shard_map/ppermute | solution.py:313
  506.7 19.4 %collective-permute-start.7 = (bf16[2,768,128]{2,1,0:T(8,128)(2,1)S(1)}, bf16[2,768,128]{2,1,0:T(8,128)(2,1)}, u32[]{:S(2)}, u32[]{:S(2)}) collective-permute-start(bf16[2,768,128]{2,1,0:T(8,128)(2,1)S(1)} %get-tuple-element.124), channel_id=1, source_target_pairs={{0,48},{16,0},{32,16},{48,32},{1,49},{17,1},{33,17},{49,33},{2,50}... | collective-permute-start | bytes 1179656 | tf_op jit(solution)/shard_map/ppermute | solution.py:313
  507.5 17.2 %collective-permute-start.13 = (bf16[256,128]{1,0:T(8,128)(2,1)S(1)}, bf16[256,128]{1,0:T(8,128)(2,1)S(1)}, u32[]{:S(2)}, u32[]{:S(2)}) collective-permute-start(bf16[256,128]{1,0:T(8,128)(2,1)S(1)} %fusion.31), channel_id=1, source_target_pairs={{0,64},{64,0},{1,65},{65,1},{2,66},{66,2},{3,67},{67,3},{4,68},{68... | collective-permute-start | bytes 196616 | tf_op jit(solution)/shard_map/ppermute | solution.py:302
  527.4 7.7 %collective-permute-start.8 = (bf16[768,128]{1,0:T(8,128)(2,1)S(1)}, bf16[768,128]{1,0:T(8,128)(2,1)S(1)}, u32[]{:S(2)}, u32[]{:S(2)}) collective-permute-start(bf16[768,128]{1,0:T(8,128)(2,1)S(1)} %fusion.27), channel_id=1, source_target_pairs={{0,64},{64,0},{1,65},{65,1},{2,66},{66,2},{3,67},{67,3},{4,68},{68... | collective-permute-start | bytes 589832 | tf_op jit(solution)/shard_map/ppermute | solution.py:302
  (64 other events, 410.8 us)

commit v2 on v1

v2 whole, which is shorter than its diff:
```python
import functools

import jax
import jax.numpy as jnp
from jax import lax
from jax.experimental import pallas as pl
from jax.experimental.pallas import tpu as pltpu
from jax.sharding import Mesh
from jax.sharding import PartitionSpec as P

HDIM = 64
DOCS = 3
BLOCK = 512
HALF = 256
LOW = jnp.bfloat16
WIDE = jnp.float32
CTX = ("xh", "zh", "zl", "core")
TP = ("y", "xl")
SPREAD = ("xh", "zh")
Z = ("zh", "zl")


def kernel_call(body, out_shape, inputs, scalars=(), scratch=(), flops=0, exps=0, mib=16, far=()):
    operands = (*inputs, *far)
    moved = sum(a.size * a.dtype.itemsize for a in (*operands, *jax.tree.leaves(out_shape)))
    in_specs = [pl.BlockSpec(memory_space=pltpu.SMEM)] * len(scalars)
    in_specs += [pl.BlockSpec(memory_space=pltpu.VMEM)] * len(inputs)
    in_specs += [pl.BlockSpec(memory_space=pl.ANY)] * len(far)
    return pl.pallas_call(
        body,
        out_shape=out_shape,
        in_specs=in_specs,
        out_specs=jax.tree.map(lambda _: pl.BlockSpec(memory_space=pltpu.VMEM), out_shape),
        scratch_shapes=list(scratch),
        compiler_params=pltpu.CompilerParams(vmem_limit_bytes=mib * 1024 * 1024),
        cost_estimate=pl.CostEstimate(flops=flops, bytes_accessed=moved, transcendentals=exps),
    )(*scalars, *operands)


def lane_of(shape):
    return lax.broadcasted_iota(jnp.int32, shape, len(shape) - 1)


def exchange_halves(a, b):
    front = lane_of(a.shape) < HDIM
    return (
        jnp.where(front, a, pltpu.roll(b, HDIM, 1)),
        jnp.where(front, pltpu.roll(a, HDIM, 1), b),
    )


def nt(a, b):
    return lax.dot_general(a, b, (((1,), (1,)), ((), ())), preferred_element_type=WIDE)


def nn(a, b):
    return lax.dot_general(a, b, (((1,), (0,)), ((), ())), preferred_element_type=WIDE)


def turn(x, cosine, sine, sign):
    lane = lax.rem(lane_of(x.shape), HDIM)
    ahead = pltpu.roll(x, x.shape[1] - 8, 1)
    behind = pltpu.roll(x, 8, 1)
    swapped = jnp.where(lane < 8, -ahead, behind) * sign
    return x * cosine + swapped * sine


def rotation_table(angles_table):
    tokens = angles_table.shape[1]
    rest = jnp.zeros((112, tokens), WIDE)
    x = jnp.concatenate([angles_table, rest], axis=0).T
    lane = lane_of(x.shape)
    c = jnp.where(lane < 8, x, 0.0)
    c = c + pltpu.roll(c, 8, 1)
    c = c + pltpu.roll(c, HDIM, 1) + jnp.where(lax.rem(lane, HDIM) < 16, 0.0, 1.0)
    s = jnp.where((lane >= 8) & (lane < 16), x, 0.0)
    s = s + pltpu.roll(s, 120, 1)
    s = s + pltpu.roll(s, HDIM, 1)
    return c, s


def project_kernel(
    place, tok, gain, shift, w, bias, table,
    normed, mean_out, scale_out, kv_out, q0, q1, q2, q3, cosine_out, sine_out, kept,
):
    rows = 64

    def norm_rows(i, carry):
        at = pl.ds(pl.multiple_of(i * rows, rows), rows)
        x = tok[at, :].astype(WIDE)
        mean = jnp.mean(x, axis=-1, keepdims=True)
        center = x - mean
        scale = lax.rsqrt(jnp.mean(center * center, axis=-1, keepdims=True) + 1e-05)
        normed[at, :] = (center * scale * gain[...] + shift[...]).astype(LOW)
        mean_out[at, :] = mean
        scale_out[at, :] = scale
        return carry

    lax.fori_loop(0, BLOCK // rows, norm_rows, 0)
    cosine, sine = rotation_table(table[...])
    cosine_out[...] = cosine
    sine_out[...] = sine
    mixed = [nn(normed[...], w[c]) + bias[c : c + 1, :] for c in range(3)]
    for pair in range(2):
        lanes = slice(pair * 128, pair * 128 + 128)
        q = turn(mixed[0][:, lanes], cosine, sine, 1.0) * 0.125
        k = turn(mixed[1][:, lanes], cosine, sine, 1.0)
        kv = exchange_halves(k, mixed[2][:, lanes])
        qq = exchange_halves(q[:HALF], q[HALF:])
        for one in range(2):
            kv_out[2 * pair + one] = kv[one].astype(LOW)
            kept[2 * pair + one] = qq[one].astype(LOW)
    for k, out in enumerate((q0, q1, q2, q3)):
        out[...] = kept[place[1] ^ k]


def padded_queries(q2):
    x = q2.astype(WIDE)
    front = lane_of(x.shape) < HDIM
    return (
        jnp.where(front, x, 0.0).astype(LOW),
        jnp.where(front, pltpu.roll(x, HDIM, 1), 0.0).astype(LOW),
    )


def padded_behind(d2):
    x = d2.astype(WIDE)
    front = lane_of(x.shape) < HDIM
    return (
        jnp.where(front, 0.0, pltpu.roll(x, HDIM, 1)).astype(LOW),
        jnp.where(front, 0.0, x).astype(LOW),
    )


def allowed_keys(key_block, first_query, begin):
    shape = (BLOCK, begin.shape[1])
    key_at = key_block * BLOCK + lax.broadcasted_iota(jnp.int32, shape, 0)
    query_at = first_query + lax.broadcasted_iota(jnp.int32, shape, 1)
    return (key_at <= query_at) & (key_at >= begin)


def forward_kernel(
    place, begin, kv0, kv1, kv2, kv3, q0, q1, q2, q3,
    o0, o1, o2, o3, out_t, total, kvs, kvt, queries, peak, acc, kept_q, kept_o,
):
    group, me = place[0], place[1]
    front = lane_of((BLOCK, 128)) < HDIM
    for k, q in enumerate((q0, q1, q2, q3)):
        kept_q[me ^ k] = q[...]
    for rel, kv in enumerate((kv0, kv1, kv2, kv3)):
        for j in range(4):
            block = 4 * j + (group ^ rel)
            kvs[block] = kv[j]
            kvt[block] = jnp.where(front, 1.0, kv[j].astype(WIDE)).T.astype(LOW)

    def one_query_block(j, carry):
        query_block = 4 * j + group
        queries[:HALF, :], queries[HALF:, :] = padded_queries(kept_q[j])
        peak[...] = jnp.full((1, BLOCK), -1e30, WIDE)
        acc[...] = jnp.zeros((128, BLOCK), WIDE)

        def four_blocks(t, carry):
            scores = []
            for key_block in [4 * t + k for k in range(4)]:
                ok = allowed_keys(key_block, query_block * BLOCK, begin[j])
                scores.append(jnp.where(ok, nt(kvs[key_block], queries[...]), -1e30))
            old = peak[...]
            new = old
            for one in scores:
                new = jnp.maximum(new, jnp.max(one, axis=0, keepdims=True))
            total_now = acc[...] * jnp.exp(old - new)
            for k in range(4):
                weights = jnp.exp(scores[k] - new).astype(LOW)
                total_now += nn(kvt[4 * t + k], weights)
            acc[...] = total_now
            peak[...] = new
            return carry

        lax.fori_loop(0, j + 1, four_blocks, 0)
        weight_sum = acc[:1, :]
        done = acc[...] / weight_sum
        out_t[j] = done
        total[j] = peak[...] + jnp.log(weight_sum)
        rows = done.T
        x, y = rows[:HALF], rows[HALF:]
        kept_o[j] = jnp.where(lane_of(x.shape) < HDIM, pltpu.roll(x, HDIM, 1), y).astype(LOW)
        return carry

    lax.fori_loop(0, 4, one_query_block, 0)
    for k, out in enumerate((o0, o1, o2, o3)):
        out[...] = kept_o[me ^ k]


def backward_kernel(
    place, begin, kv0, kv1, kv2, kv3, q0, q1, q2, q3, d0, d1, d2, d3, out_t, total,
    g0, g1, g2, g3, keep0, keep1, send0, send1,
    kvs, kvt, queries, grads, dot_rows, acc, dkv, kept_q, kept_d, kept_g,
):
    group, me = place[0], place[1]
    for k in range(4):
        kept_q[me ^ k] = (q0, q1, q2, q3)[k][...]
        kept_d[me ^ k] = (d0, d1, d2, d3)[k][...]
    for rel, kv in enumerate((kv0, kv1, kv2, kv3)):
        for j in range(4):
            block = 4 * j + (group ^ rel)
            kvs[block] = kv[j]
            kvt[block] = kv[j].astype(WIDE).T.astype(LOW)
    dkv[...] = jnp.zeros(dkv.shape, WIDE)

    def one_query_block(j, carry):
        query_block = 4 * j + group
        queries[:HALF, :], queries[HALF:, :] = padded_queries(kept_q[j])
        grads[:HALF, :], grads[HALF:, :] = padded_behind(kept_d[j])
        dot_rows[...] = jnp.sum(grads[...].astype(WIDE).T * out_t[j], axis=0, keepdims=True)
        acc[...] = jnp.zeros((128, BLOCK), WIDE)

        def four_blocks(t, carry):
            for key_block in [4 * t + k for k in range(4)]:
                term = 0.0
                for half in range(2):
                    at = slice(half * HALF, half * HALF + HALF)
                    ok = allowed_keys(key_block, query_block * BLOCK + half * HALF, begin[j][:, at])
                    scores = nt(kvs[key_block], queries[at, :])
                    probs = jnp.where(ok, jnp.exp(scores - total[j][:, at]), 0.0)
                    grad_probs = nt(kvs[key_block], grads[at, :])
                    grad_scores = (probs * (grad_probs - dot_rows[:, at])).astype(LOW)
                    term += nn(grad_scores, queries[at, :]) + nn(probs.astype(LOW), grads[at, :])
                    acc[:, at] += nn(kvt[key_block], grad_scores)
                dkv[key_block] += term
            return carry

        lax.fori_loop(0, j + 1, four_blocks, 0)
        rows = acc[...].T
        x, y = rows[:HALF], rows[HALF:]
        kept_g[j] = jnp.where(lane_of(x.shape) < HDIM, x, pltpu.roll(y, HDIM, 1)).astype(LOW)
        return carry

    lax.fori_loop(0, 4, one_query_block, 0)
    for k, out in enumerate((g0, g1, g2, g3)):
        out[...] = kept_g[me ^ k]
    for rel, out in enumerate((keep0, send0, keep1, send1)):
        for k in range(4):
            out[k] = dkv[4 * (me ^ k) + (group ^ rel)].astype(LOW)


def branch_kernel(place, h0, h1, h2, h3, w, attended, partial, kept):
    for k, h in enumerate((h0, h1, h2, h3)):
        kept[place[1] ^ k] = h[...]
    for pair in range(2):
        lanes = slice(pair * 128, pair * 128 + 128)
        x, y = exchange_halves(kept[2 * pair].astype(WIDE), kept[2 * pair + 1].astype(WIDE))
        attended[:HALF, lanes] = x.astype(LOW)
        attended[HALF:, lanes] = y.astype(LOW)
    for n in range(4):
        at = slice(n * 512, n * 512 + 512)
        partial[:, at] = nn(attended[...], w[:, at]).astype(LOW)


def grad_attended_kernel(place, grad, w, d0, d1, d2, d3, kept):
    g = nt(grad[...], w[...])
    for pair in range(2):
        lanes = slice(pair * 128, pair * 128 + 128)
        both = exchange_halves(g[:HALF, lanes], g[HALF:, lanes])
        for one in range(2):
            kept[2 * pair + one] = both[one].astype(LOW)
    for k, out in enumerate((d0, d1, d2, d3)):
        out[...] = kept[place[1] ^ k]


def grad_project_kernel(
    place, w, cosine, sine, tok, mean, scale, p0, p1, p2, p3, g0, g1, g2, g3,
    grad_mixed, partial, gain_sum, shift_sum, bias_sum, parts, kept, sems,
):
    moves = []
    for k in range(4):
        at = place[1] ^ k
        moves.append(pltpu.make_async_copy((p0, p1, p2, p3)[k], parts.at[at], sems.at[k]))
        moves.append(pltpu.make_async_copy((g0, g1, g2, g3)[k], kept.at[at], sems.at[4 + k]))
    for move in moves:
        move.start()
    for move in moves:
        move.wait()
    for pair in range(2):
        lanes = slice(pair * 128, pair * 128 + 128)
        k, v = exchange_halves(parts[2 * pair].astype(WIDE), parts[2 * pair + 1].astype(WIDE))
        q = exchange_halves(kept[2 * pair].astype(WIDE), kept[2 * pair + 1].astype(WIDE))
        q = jnp.concatenate(q, axis=0)
        q = turn(q, cosine[...], sine[...], -1.0) * 0.125
        k = turn(k, cosine[...], sine[...], -1.0)
        for c, part in enumerate((q, k, v)):
            start = c * 256 + pair * 128
            low = part.astype(LOW)
            grad_mixed[:, start : start + 128] = low
            bias_sum[c : c + 1, lanes] = jnp.sum(low.astype(WIDE), axis=0, keepdims=True)
    for n in range(4):
        at = slice(n * 512, n * 512 + 512)
        total = nt(grad_mixed[:, :256], w[0, at, :])
        total += nt(grad_mixed[:, 256:512], w[1, at, :])
        total += nt(grad_mixed[:, 512:], w[2, at, :])
        partial[:, at] = total.astype(LOW)
        normal = (tok[:, at].astype(WIDE) - mean[...]) * scale[...]
        gain_sum[:, at] = jnp.sum(total * normal, axis=0, keepdims=True)
        shift_sum[:, at] = jnp.sum(total, axis=0, keepdims=True)


def for_rows(work):
    rows = 16

    def one(i, carry):
        work(pl.ds(pl.multiple_of(i * rows, rows), rows))
        return carry

    lax.fori_loop(0, 64 // rows, one, 0)


def summed(parts, at):
    total = parts[0, at, :].astype(WIDE)
    for k in range(1, 8):
        total += parts[k, at, :].astype(WIDE)
    return total


def copy_out(copies, at, value):
    low = value.astype(LOW)
    for k in range(8):
        copies[k, at, :] = low


def second_norm_kernel(parts, tok, gain, shift, copies, middle, normal, scale_out):
    def work(at):
        x = tok[at, :].astype(WIDE) + summed(parts, at)
        center = x - jnp.mean(x, axis=-1, keepdims=True)
        scale = lax.rsqrt(jnp.mean(center * center, axis=-1, keepdims=True) + 1e-05)
        rows = center * scale
        copy_out(copies, at, rows * gain[...] + shift[...])
        middle[at, :] = x
        normal[at, :] = rows
        scale_out[at, :] = scale

    for_rows(work)


def norm_gradient(grad, rows, scale, gain):
    scaled = grad * gain
    return scale * (
        scaled
        - jnp.mean(scaled, axis=-1, keepdims=True)
        - rows * jnp.mean(scaled * rows, axis=-1, keepdims=True)
    )


def second_gradient_kernel(parts, cot, normal, scale, gain, copies, grad_middle, sums):
    sums[...] = jnp.zeros(sums.shape, WIDE)

    def work(at):
        grad, rows = summed(parts, at), normal[at, :]
        done = cot[at, :].astype(WIDE) + norm_gradient(grad, rows, scale[at, :], gain[...])
        copy_out(copies, at, done)
        grad_middle[at, :] = done
        sums[0:1, :] += jnp.sum(grad * rows, axis=0, keepdims=True)
        sums[1:2, :] += jnp.sum(grad, axis=0, keepdims=True)

    for_rows(work)


def layer_out_kernel(parts, middle, copies):
    for_rows(lambda at: copy_out(copies, at, middle[at, :] + summed(parts, at)))


def first_gradient_kernel(parts, grad_middle, tok, mean, scale, gain, copies):
    def work(at):
        rows = (tok[at, :].astype(WIDE) - mean[at, :]) * scale[at, :]
        done = norm_gradient(summed(parts, at), rows, scale[at, :], gain[...])
        copy_out(copies, at, grad_middle[at, :] + done)

    for_rows(work)


def weight_kernel(widths, place, *refs):
    count = len(widths)
    lefts, rights = refs[:count], refs[count : 2 * count]
    mine, theirs, turned = refs[2 * count :]
    first_core = place[2] == 0
    start = 0
    for left, right, width in zip(lefts, rights, widths):
        turned[:width, :] = left[...].astype(WIDE).T.astype(LOW)

        def one(n, carry, start=start, right=right, width=width):
            columns = right[:, pl.ds(pl.multiple_of(n * 256, 256), 256)]
            both = nn(turned[:width, :], columns)
            first, second = both[:, :128], both[:, 128:]
            at = pl.ds(start, width)
            mine[n, at, :] = jnp.where(first_core, first, second).astype(LOW)
            theirs[n, at, :] = jnp.where(first_core, second, first).astype(LOW)
            return carry

        lax.fori_loop(0, 8, one, 0, unroll=4)
        start += width


def weight_grads(pairs, place):
    lefts, rights = [a for a, _ in pairs], [b for _, b in pairs]
    widths = tuple(a.shape[1] for a in lefts)
    out = jax.ShapeDtypeStruct((8, sum(widths), 128), LOW)
    return kernel_call(
        functools.partial(weight_kernel, widths),
        (out, out),
        (*lefts, *rights),
        scalars=(place,),
        scratch=(pltpu.VMEM((max(widths), BLOCK), LOW),),
        flops=2 * sum(widths) * BLOCK * 2048,
    )


def swapped(x, axis):
    return lax.ppermute(x, axis, [(0, 1), (1, 0)])


def across(pieces):
    moved = [
        lax.ppermute(pieces[k], SPREAD, [(i, i ^ k) for i in range(4)]) for k in range(1, 4)
    ]
    return (pieces[0], *moved)


def z_parts(mine, received):
    rows = mine.shape[1]
    mine, received = mine.reshape(2, 4, rows, 128), received.reshape(2, 4, rows, 128)
    z = lax.axis_index(Z)
    done = []
    for k in range(4):
        at = lax.rem(z + k, 4)
        a, b = (lax.dynamic_index_in_dim(x, at, 1, False).astype(WIDE) for x in (mine, received))
        done.append((a + b).astype(LOW))
    return done


def z_permute(part, distance):
    return lax.ppermute(part, Z, [(i, (i + distance) % 4) for i in range(4)])


def xh_halves(moved):
    xh = lax.axis_index("xh")

    def added(at):
        return sum(lax.dynamic_index_in_dim(x, at, 0, False).astype(WIDE) for x in moved)

    return added(xh), added(1 - xh).astype(LOW)


def settled_kernel(x, out, sem):
    move = pltpu.make_async_copy(x, out, sem)
    move.start()
    move.wait()


def settled(x):
    return pl.pallas_call(
        settled_kernel,
        out_shape=jax.ShapeDtypeStruct(x.shape, x.dtype),
        in_specs=[pl.BlockSpec(memory_space=pl.ANY)],
        out_specs=pl.BlockSpec(memory_space=pl.ANY),
        scratch_shapes=[pltpu.SemaphoreType.DMA],
        cost_estimate=pl.CostEstimate(flops=0, bytes_accessed=2 * x.size * 2, transcendentals=0),
    )(x)


def tp_parts(partial):
    parts = partial.reshape(8, -1, partial.shape[1])
    return lax.all_to_all(parts, TP, split_axis=0, concat_axis=0, tiled=True)


def tp_rows(copies):
    rows = lax.all_to_all(copies, TP, split_axis=0, concat_axis=0, tiled=True)
    return rows.reshape(-1, copies.shape[2])


def summed_by_pairs(x, pairs):
    for axis, size, distance in pairs:
        x = x + lax.ppermute(x, axis, [(i, i ^ distance) for i in range(size)])
    return x


def shape_of(*dims, kind=LOW):
    return jax.ShapeDtypeStruct(dims, kind)


def body(
    tokens, cotangent, segment_ids, first_gain, first_shift, second_gain, second_shift,
    w_qkv, qkv_bias, w_out, w_gate_up, w_down,
):
    ctx = lax.axis_index(CTX)
    tp = lax.axis_index(TP)
    group = lax.axis_index(("zl", "core"))
    place = jnp.stack([group, lax.axis_index(SPREAD), lax.axis_index("core")])

    def my_share(array):
        return lax.dynamic_slice_in_dim(array, tp * 64, 64)

    labels = jnp.arange(DOCS, dtype=jnp.int32)
    starts = jnp.sum((segment_ids[None, :] < labels[:, None]).astype(jnp.int32), axis=1)
    begins = jnp.sum(
        jnp.where(segment_ids[None, :] == labels[:, None], starts[:, None], 0), axis=0
    )
    begin = lax.dynamic_index_in_dim(begins.reshape(4, 4, 1, BLOCK), group, 1, False)
    own = lax.dynamic_slice_in_dim(begins, ctx * BLOCK, BLOCK)
    places = ctx * BLOCK + jnp.arange(BLOCK, dtype=jnp.int32) - own
    frequency = 10000.0 ** (-jnp.arange(8, dtype=WIDE) / 8.0)
    angles = frequency[:, None] * places.astype(WIDE)[None, :]
    table = jnp.concatenate([jnp.cos(angles), jnp.sin(angles)], axis=0)

    w3 = jnp.transpose(w_qkv, (1, 0, 2))
    quarter = shape_of(HALF, 128)
    normed_low, mean1, scale1, kv, *queries, cosine, sine = kernel_call(
        project_kernel,
        (
            shape_of(BLOCK, 2048),
            shape_of(BLOCK, 1, kind=WIDE),
            shape_of(BLOCK, 1, kind=WIDE),
            shape_of(4, BLOCK, 128),
            *[quarter] * 4,
            shape_of(BLOCK, 128, kind=WIDE),
            shape_of(BLOCK, 128, kind=WIDE),
        ),
        (tokens, first_gain[None], first_shift[None], w3, qkv_bias, table),
        scalars=(place,),
        scratch=(pltpu.VMEM((4, HALF, 128), LOW),),
        flops=2 * 512 * 2048 * 768,
    )
    kv = lax.all_to_all(kv, SPREAD, split_axis=0, concat_axis=0, tiled=True)
    queries = across(queries)
    kv_z, *queries = lax.optimization_barrier((swapped(kv, "zl"), *queries))
    kv_parts = (kv, swapped(kv, "core"), kv_z, swapped(kv_z, "core"))
    *heads, out_t, total = kernel_call(
        forward_kernel,
        (*[quarter] * 4, shape_of(4, 128, BLOCK, kind=WIDE), shape_of(4, 1, BLOCK, kind=WIDE)),
        (begin, *kv_parts, *queries),
        scalars=(place,),
        scratch=(
            pltpu.VMEM((16, BLOCK, 128), LOW),
            pltpu.VMEM((16, 128, BLOCK), LOW),
            pltpu.VMEM((BLOCK, 128), LOW),
            pltpu.VMEM((1, BLOCK), WIDE),
            pltpu.VMEM((128, BLOCK), WIDE),
            pltpu.VMEM((4, HALF, 128), LOW),
            pltpu.VMEM((4, HALF, 128), LOW),
        ),
        flops=40 * 4 * BLOCK * BLOCK * 128,
        mib=32,
        exps=40 * BLOCK * BLOCK,
    )
    heads = across(heads)
    attended_low, partial_branch = kernel_call(
        branch_kernel,
        (shape_of(BLOCK, 256), shape_of(BLOCK, 2048)),
        (*heads, w_out),
        scalars=(place,),
        scratch=(pltpu.VMEM((4, HALF, 128), LOW),),
        flops=2 * 512 * 256 * 2048,
    )
    share = shape_of(64, 2048, kind=WIDE)
    copies = shape_of(8, 64, 2048)
    copies2, middle, second_rows, second_scale = kernel_call(
        second_norm_kernel,
        (copies, share, share, shape_of(64, 1, kind=WIDE)),
        (tp_parts(partial_branch), my_share(tokens), second_gain[None], second_shift[None]),
    )
    second_low, cot_share = lax.optimization_barrier((tp_rows(copies2), my_share(cotangent)))

    gate_up = jnp.einsum("td,dcf->tcf", second_low, w_gate_up, preferred_element_type=WIDE)
    gate, up = gate_up[:, 0], gate_up[:, 1]
    sigmoid_gate = jax.nn.sigmoid(gate)
    activated = gate * sigmoid_gate
    hidden_low = (activated * up).astype(LOW)
    grad_hidden = jnp.einsum("td,fd->tf", cotangent, w_down, preferred_element_type=WIDE)
    grad_gate = grad_hidden * up * sigmoid_gate * (1.0 + gate * (1.0 - sigmoid_gate))
    grad_gate = grad_gate.astype(LOW)
    grad_up = (grad_hidden * activated).astype(LOW)
    partial_second = jnp.einsum(
        "tcf,dcf->td", jnp.stack([grad_gate, grad_up], axis=1), w_gate_up, preferred_element_type=WIDE
    ).astype(LOW)
    grad_gate, partial_second = lax.optimization_barrier((grad_gate, partial_second))
    second_parts = tp_parts(partial_second)

    feed_mine, feed_theirs = weight_grads(
        ((grad_gate, second_low), (grad_up, second_low), (hidden_low, cotangent)), place
    )
    second_parts, feed_mine, feed_theirs = lax.optimization_barrier(
        (second_parts, feed_mine, feed_theirs)
    )
    copies3, grad_middle, second_sums = kernel_call(
        second_gradient_kernel,
        (copies, share, shape_of(2, 2048, kind=WIDE)),
        (second_parts, cot_share, second_rows, second_scale, second_gain[None]),
    )
    grad_branch = tp_rows(copies3)
    feed_received = swapped(feed_theirs, "core")
    feed_z = z_parts(feed_mine, feed_received)
    feed_1, feed_3 = z_permute(feed_z[1], 1), z_permute(feed_z[3], 3)

    grads = kernel_call(
        grad_attended_kernel,
        (*[quarter] * 4,),
        (grad_branch, w_out),
        scalars=(place,),
        scratch=(pltpu.VMEM((4, HALF, 128), LOW),),
        flops=2 * 512 * 256 * 2048,
    )
    hidden_low, feed_1, feed_3, *grads = lax.optimization_barrier(
        (hidden_low, feed_1, feed_3, *grads)
    )
    partial_feed = jnp.dot(hidden_low, w_down, preferred_element_type=WIDE).astype(LOW)
    *grads, partial_feed, feed_2 = lax.optimization_barrier(
        (*across(grads), partial_feed, feed_z[2])
    )
    feed_parts = tp_parts(partial_feed)
    feed_2 = z_permute(feed_2, 2)
    backward = kernel_call(
        backward_kernel,
        (*[quarter] * 4, *[shape_of(4, BLOCK, 128)] * 4),
        (begin, *kv_parts, *queries, *grads, out_t, total),
        scalars=(place,),
        scratch=(
            pltpu.VMEM((16, BLOCK, 128), LOW),
            pltpu.VMEM((16, 128, BLOCK), LOW),
            pltpu.VMEM((BLOCK, 128), LOW),
            pltpu.VMEM((BLOCK, 128), LOW),
            pltpu.VMEM((1, BLOCK), WIDE),
            pltpu.VMEM((128, BLOCK), WIDE),
            pltpu.VMEM((16, BLOCK, 128), WIDE),
            *[pltpu.VMEM((4, HALF, 128), LOW)] * 3,
        ),
        flops=40 * 10 * BLOCK * BLOCK * 128,
        mib=32,
        exps=40 * BLOCK * BLOCK,
    )
    *backward, feed_parts, feed_2 = lax.optimization_barrier((*backward, feed_parts, feed_2))
    *grad_queries, keep0, keep1, send0, send1 = backward
    feed_keep, feed_send = xh_halves([feed_z[0], feed_1, feed_2, feed_3])
    far, feed_send = lax.optimization_barrier((swapped(send1, "core"), feed_send))
    feed_received = swapped(feed_send, "xh")
    far = (keep1.astype(WIDE) + far.astype(WIDE)).astype(LOW)
    far, send0 = lax.optimization_barrier((far, send0))
    near = keep0.astype(WIDE) + swapped(send0, "core").astype(WIDE)
    near, feed_parts = lax.optimization_barrier((near, feed_parts))
    copies4 = kernel_call(layer_out_kernel, copies, (feed_parts, middle))
    layer_out = tp_rows(copies4)
    far, *grad_queries = lax.optimization_barrier((swapped(far, "zl"), *across(grad_queries)))
    grad_kv = across([(near[k] + far[k].astype(WIDE)).astype(LOW) for k in range(4)])
    layer_out, feed_received, *grad_kv = lax.optimization_barrier(
        (layer_out, feed_received, *grad_kv)
    )
    layer_out = settled(layer_out)
    grad_mixed, partial_normed, gain_sum, shift_sum, bias_sum = kernel_call(
        grad_project_kernel,
        (
            shape_of(BLOCK, 768),
            shape_of(BLOCK, 2048),
            shape_of(1, 2048, kind=WIDE),
            shape_of(1, 2048, kind=WIDE),
            shape_of(3, 256, kind=WIDE),
        ),
        (w3, cosine, sine, tokens, mean1, scale1),
        far=(*grad_kv, *grad_queries),
        scalars=(place,),
        scratch=(
            pltpu.VMEM((4, BLOCK, 128), LOW),
            pltpu.VMEM((4, HALF, 128), LOW),
            pltpu.SemaphoreType.DMA((8,)),
        ),
        flops=2 * 512 * 2048 * 768,
    )
    grad_mixed, partial_normed = lax.optimization_barrier((grad_mixed, partial_normed))
    normed_parts = tp_parts(partial_normed)

    rest_mine, rest_theirs = weight_grads(
        ((grad_mixed, normed_low), (attended_low, grad_branch)), place
    )
    vectors = jnp.concatenate([gain_sum, shift_sum, second_sums], axis=0).reshape(32, 256)
    vectors = jnp.concatenate([vectors, bias_sum], axis=0)
    normed_parts, rest_mine, vectors = lax.optimization_barrier((normed_parts, rest_mine, vectors))
    rest_received = swapped(rest_theirs, "core")
    vectors = summed_by_pairs(
        vectors, (("core", 2, 1), ("zl", 2, 1), ("zh", 2, 1), ("xh", 2, 1))
    )
    bias_grad = vectors[32:]
    rest_z = z_parts(rest_mine, rest_received)

    copies5 = kernel_call(
        first_gradient_kernel,
        copies,
        (
            normed_parts,
            grad_middle,
            my_share(tokens),
            my_share(mean1),
            my_share(scale1),
            first_gain[None],
        ),
    )
    grad_tokens = settled(tp_rows(copies5))

    vectors = vectors[:32].reshape(4, 2048)
    vectors = summed_by_pairs(vectors, (("y", 4, 1), ("y", 4, 2), ("xl", 2, 1)))
    rest_keep, rest_send = xh_halves(
        [rest_z[0], *[z_permute(rest_z[k], k) for k in range(1, 4)]]
    )
    rest_w = rest_keep + swapped(rest_send, "xh").astype(WIDE)
    feed_w = feed_keep + feed_received.astype(WIDE)
    return (
        layer_out,
        grad_tokens,
        vectors[0],
        vectors[1],
        vectors[2],
        vectors[3],
        jnp.transpose(rest_w[:768].reshape(3, 256, 128), (2, 0, 1)),
        bias_grad,
        rest_w[768:],
        jnp.transpose(feed_w[:1408].reshape(2, 704, 128), (2, 0, 1)),
        feed_w[1408:],
    )


def solution(mesh):
    fine = Mesh(
        mesh.devices.reshape(2, 2, 2, 2, 4, 2), ("xh", "zh", "zl", "core", "y", "xl")
    )
    rows = P(CTX, None)
    return jax.shard_map(
        body,
        mesh=fine,
        in_specs=(
            rows, rows, P(), P(), P(), P(), P(),
            P(None, None, TP), P(None, TP), P(TP, None), P(None, None, TP), P(TP, None),
        ),
        out_specs=(
            rows, rows, P(), P(), P(), P(),
            P(CTX, None, TP), P(None, TP), P(TP, CTX), P(CTX, None, TP), P(TP, CTX),
        ),
        check_vma=False,
    )
```

time: 552 us -> 642 us (1.16)
  Pallas kernels: 86.6 us -> 219 us
  blocking collectives: 106 us -> 19.1 us
  waiting for transfers between devices: 149 us -> 179 us
  other arithmetic: 40 us -> 23.2 us
  starting transfers between devices: 87.1 us -> 103 us
  local copies, waits for them, and re-layouts: 52.9 us -> 66.4 us
    pallas_call x0 -> x2, Pallas kernels: none -> 129 us  [settled(): pl.pallas_call(settled_kernel, out_shape=jax.ShapeDtypeStruct(x.shape, x....]
    all_to_all x5 -> x1, blocking collectives: 106 us -> 19.1 us  [body(): kv = lax.all_to_all(kv, SPREAD, split_axis=0, concat_axis=0, tiled=True)]
    ppermute x15 -> x28, waiting for transfers between devices: 21.3 us -> 81.8 us  [the longest x15 51.5 us: across(): lax.ppermute(pieces[k], SPREAD, [(i, i ^ k) for i in range(4)])]
    ppermute x15 -> x28, starting transfers between devices: 19.3 us -> 56.5 us  [the longest x15 33.1 us: across(): lax.ppermute(pieces[k], SPREAD, [(i, i ^ k) for i in range(4)])]
    unnamed x156 -> x190, local copies, waits for them, and re-layouts: 32 us -> 59.1 us
    ppermute x14 -> x10, waiting for transfers between devices: 34.1 us -> 8.14 us  [swapped(): return lax.ppermute(x, axis, [(0, 1), (1, 0)])]
    ppermute x14 -> x10, starting transfers between devices: 29 us -> 7.59 us  [swapped(): return lax.ppermute(x, axis, [(0, 1), (1, 0)])]
    reduce_sum x10 -> x0, other arithmetic: 9.68 us -> none  [the longest x3 4.4 us: tp_share(): return jnp.sum(parts.astype(WIDE), axis=0)]
  transfers between devices with their start and end apart: 38 -> 46, of which waited for: 17 -> 23; matrix products, arithmetic and copies ran while one was open for 9% -> 4% of each run, Pallas kernels for 4% -> 19%
where the time goes in v2:
time: 642 us; the launch traced here: 633 us
  Pallas kernels  219 us (34%)
  waiting for transfers between devices  179 us (28%)
  starting transfers between devices  103 us (16%)
  local copies, waits for them, and re-layouts  66.4 us (10%)
  other arithmetic  23.2 us (4%)
  matrix products  20.5 us (3%)
  blocking collectives  19.1 us (3%)
    pallas_call x2, Pallas kernels, settled(): pl.pallas_call(settled_kernel, out_shape=jax.ShapeDtypeStruct(x.shape, x....  129 us
    pallas_call x12, Pallas kernels, kernel_call(): pl.pallas_call(body, out_shape=out_shape, in_specs=in_specs, out_specs=ja...  90.2 us
    unnamed x190, local copies, waits for them, and re-layouts  59.1 us
    ppermute x15, waiting for transfers between devices, across(): lax.ppermute(pieces[k], SPREAD, [(i, i ^ k) for i in range(4)])  51.5 us
    all_to_all x4, waiting for transfers between devices, tp_parts(): return lax.all_to_all(parts, TP, split_axis=0, concat_axis=0, tiled=True)  46.6 us
    all_to_all x4, waiting for transfers between devices, tp_rows(): rows = lax.all_to_all(copies, TP, split_axis=0, concat_axis=0, tiled=True)  42.9 us
    ppermute x15, starting transfers between devices, across(): lax.ppermute(pieces[k], SPREAD, [(i, i ^ k) for i in range(4)])  33.1 us
    ppermute x7, waiting for transfers between devices, summed_by_pairs(): x = x + lax.ppermute(x, axis, [(i, i ^ distance) for i in range(size)])  27.8 us
  transfers between devices with their start and end apart: 46, of which 23 were waited for; matrix products, arithmetic and copies ran while one was open for 4% of the time, Pallas kernels for 19%

profile of v2, /device:TPU:0, one launch (start us, length us, event | category | flops | bytes accessed | tf_op | source)
XLA Modules:
  0.0 632.9 jit_solution(15151003512646579537)
XLA Ops:
  8.6 5.0 shard_map.203
  15.0 19.1 %all_to_all.45.kv0 = bf16[4,512,128]{2,1,0:T(8,128)(2,1)} all-to-all(bf16[4,512,128]{2,1,0:T(8,128)(2,1)S(1)} %get-tuple-element.114), channel_id=1, replica_groups=mesh['xh'=2,'zh'=2,'zl'=2,'core'=2,'y'=4,'xl'=2] {'xh','zh'}, dimensions={0} | all-to-all | bytes 1048576 | tf_op jit(solution)/shard_map/all_to_all | solution.py:530
  37.2 4.4 collective-permute-start.4
  41.6 8.5 %collective-permute-done.2.q1 = bf16[256,128]{1,0:T(8,128)(2,1)S(1)} collective-permute-done((bf16[256,128]{1,0:T(8,128)(2,1)S(1)}, bf16[256,128]{1,0:T(8,128)(2,1)S(1)}, u32[]{:S(2)}, u32[]{:S(2)}) %collective-permute-start.2) | collective-permute-done | bytes 65568 | tf_op jit(solution)/shard_map/ppermute | solution.py:421
  52.5 20.9 %shard_map.204 = (bf16[256,128]{1,0:T(8,128)(2,1)S(1)}, bf16[256,128]{1,0:T(8,128)(2,1)S(1)}, bf16[256,128]{1,0:T(8,128)(2,1)S(1)}, bf16[256,128]{1,0:T(8,128)(2...) custom-call(s32[3]{0:T(128)S(1)} %pad_add_fusion.place, s32[4,1,512]{2,1,0:T(1,128)S(1)} %fusion.32.begin, ...), custom_call_target="tpu_custom_call" | custom-call | flops 5368709120 | bytes 3686400 | tf_op jit(solution)/shard_map/pallas_call | solution.py:29
  76.5 3.5 collective-permute-start.8
  81.3 3.4 collective-permute-done.8.h3
  88.0 4.5 all-to-all-start.1
  93.5 24.7 %all-to-all-done.1.parts = bf16[8,64,2048]{2,1,0:T(8,128)(2,1)} async-done(((bf16[8,64,2048]{2,1,0:T(8,128)(2,1)}), bf16[8,64,2048]{2,1,0:T(8,128)(2,1)}, u32[]{:S(2)}, u32[]{:S(2)}) %all-to-all-start.1) | async-done | bytes 2097184 | tf_op jit(solution)/shard_map/all_to_all | solution.py:470
  118.2 2.8 shard_map.206
  123.9 4.5 all-to-all-start.2
  129.4 24.6 %all-to-all-done.2 = bf16[8,64,2048]{2,1,0:T(8,128)(2,1)} async-done(((bf16[8,64,2048]{2,1,0:T(8,128)(2,1)}), bf16[8,64,2048]{2,1,0:T(8,128)(2,1)}, u32[]{:S(2)}, u32[]{:S(2)}) %all-to-all-start.2) | async-done | bytes 2097184 | tf_op jit(solution)/shard_map/all_to_all | solution.py:474
  154.0 6.3 fusion
  160.3 3.3 multiply_convert_fusion
  163.6 7.8 %bitcast_convert_fusion = bf16[512,2048]{1,0:T(8,128)(2,1)} fusion(bf16[2048,2,704]{0,2,1:T(8,128)(2,1)} %param.22, bf16[512,1,704]{2,0,1:T(8,128)(2,1)S(1)} %bitcast.116, bf16[512,1,704]{2,0,1:T(8,128)(2,1)S(1)} %bitcast.117), kind=kOutput, calls=%fused_computation | convolution fusion | flops 2954559488 | bytes 9306112 | tf_op jit(solution)/shard_map/tcf,dcf->td/dot_general | solution.py:579
  171.4 4.3 all-to-all-start.3
  180.8 8.6 %shard_map.207 = (bf16[8,2112,128]{2,1,0:T(8,128)(2,1)S(1)}, bf16[8,2112,128]{2,1,0:T(8,128)(2,1)S(1)}) custom-call(s32[3]{0:T(128)S(1)} %pad_add_fusion.place, bf16[512,704]{1,0:T(8,128)(2,1)S(1)} %copy-done.80, bf16[512,704]{1,0:T(8,128)(2,1)S(1)} %copy-done.78, bf16[512,704]{1,0:T(8,128)(2,1)S(1)} %copy-done.87, ...), custom_call_target="tpu_custom_call" | custom-call | flops 4429185024 | bytes 17104896 | tf_op jit(solution)/shard_map/pallas_call | solution.py:29
  193.5 7.9 %all-to-all-done.3.parts = bf16[8,64,2048]{2,1,0:T(8,128)(2,1)} async-done(((bf16[8,64,2048]{2,1,0:T(8,128)(2,1)}), bf16[8,64,2048]{2,1,0:T(8,128)(2,1)}, u32[]{:S(2)}, u32[]{:S(2)}) %all-to-all-start.3) | async-done | bytes 2097184 | tf_op jit(solution)/shard_map/all_to_all | solution.py:470
  207.0 4.3 all-to-all-start.4
  211.4 6.3 %add_convert_fusion = (bf16[2,1,2112,128]{3,2,1,0:T(8,128)(2,1)}, bf16[2,2112,128]{2,1,0:T(8,128)(2,1)}, bf16[2,2112,128]{2,1,0:T(8,128)(2,1)}, bf16[2,2112,128]{2,1,0:T(8,128)(2,1)}) fusion(bf16[2,4,2112,128]{3,2,1,0:T(8,128)(2,1)} %bitcast.19, s32[]{:T(128)S(6)} %select_n.73, bf16[2,4,2112,128]{3,2,1,0:T(8,128)(2,1)} %bitcast.104, s32[]{:T(128)S(6)} %select_n.72, ...), kind=kLoop, calls=%fused_computation.2 | loop fusion | flops 8650752 | bytes 12976144 | tf_op jit(solution)/shard_map/convert_element_type | solution.py:434
  221.0 18.3 %all-to-all-done.4 = bf16[8,64,2048]{2,1,0:T(8,128)(2,1)} async-done(((bf16[8,64,2048]{2,1,0:T(8,128)(2,1)}), bf16[8,64,2048]{2,1,0:T(8,128)(2,1)}, u32[]{:S(2)}, u32[]{:S(2)}) %all-to-all-start.4) | async-done | bytes 2097184 | tf_op jit(solution)/shard_map/all_to_all | solution.py:474
  240.5 2.5 shard_map.209
  247.0 3.0 collective-permute-start.13
  252.2 3.2 convolution_convert_fusion
  258.8 4.8 all-to-all-start.5
  268.6 33.5 %shard_map.210 = (bf16[256,128]{1,0:T(8,128)(2,1)S(1)}, bf16[256,128]{1,0:T(8,128)(2,1)S(1)}, bf16[256,128]{1,0:T(8,128)(2,1)S(1)}, bf16[256,128]{1,0:T(8,128)(2...) custom-call(s32[3]{0:T(128)S(1)} %pad_add_fusion.place, ...), custom_call_target="tpu_custom_call" | custom-call | flops 13421772800 | bytes 6045696 | tf_op jit(solution)/shard_map/pallas_call | solution.py:29
  306.1 2.7 fusion.16
  315.6 5.7 all-to-all-start.6
  321.8 2.7 collective-permute-start.18
  324.4 3.3 collective-permute-start.20
  330.9 8.4 %collective-permute-done.20.g1 = bf16[256,128]{1,0:T(8,128)(2,1)S(1)} collective-permute-done((bf16[256,128]{1,0:T(8,128)(2,1)S(1)}, bf16[256,128]{1,0:T(8,128)(2,1)S(1)}, u32[]{:S(2)}, u32[]{:S(2)}) %collective-permute-start.20) | collective-permute-done | bytes 65568 | tf_op jit(solution)/shard_map/ppermute | solution.py:421
  339.3 21.4 %collective-permute-done.21.g2 = bf16[256,128]{1,0:T(8,128)(2,1)S(1)} collective-permute-done((bf16[256,128]{1,0:T(8,128)(2,1)S(1)}, bf16[256,128]{1,0:T(8,128)(2,1)S(1)}, u32[]{:S(2)}, u32[]{:S(2)}) %collective-permute-start.21) | collective-permute-done | bytes 65568 | tf_op jit(solution)/shard_map/ppermute | solution.py:421
  367.6 3.0 collective-permute-start.25
  373.8 2.9 collective-permute-done.25.p3
  391.7 4.1 shard_map.213
  399.0 5.9 all-to-all-start.7
  407.5 6.3 %shard_map.214 = (bf16[8,1024,128]{2,1,0:T(8,128)(2,1)S(1)}, bf16[8,1024,128]{2,1,0:T(8,128)(2,1)}) custom-call(s32[3]{0:T(128)S(1)} %copy-done.60, bf16[512,768]{1,0:T(8,128)(2,1)S(1)} %get-tuple-element.203.refs_0_, bf16[512,256]{1,0:T(8,128)(2,1)S(1)} %copy-done.84, bf16[512,2048]{1,0:T(8,128)(2,1)S(1)} %copy-done.82, bf16[512,2048]{1,0:T(8,128)(2,1)} %bitcast.22.grad.refs_3_), custom_call_target="tpu_custom_call" | custom-call | flops 2147483648 | bytes 9437184 | tf_op jit(solution)/shard_map/pallas_call | solution.py:29
  415.3 14.0 %all-to-all-done.7.parts = bf16[8,64,2048]{2,1,0:T(8,128)(2,1)S(1)} async-done(((bf16[8,64,2048]{2,1,0:T(8,128)(2,1)}), bf16[8,64,2048]{2,1,0:T(8,128)(2,1)S(1)}, u32[]{:S(2)}, u32[]{:S(2)}) %all-to-all-start.7) | async-done | bytes 2097184 | tf_op jit(solution)/shard_map/all_to_all | solution.py:470
  436.2 4.5 all-to-all-start.8
  440.7 2.8 collective-permute-start.28
  443.5 2.8 collective-permute-done.28
  448.3 18.9 %collective-permute-done.29 = f32[35,256]{1,0:T(8,128)S(1)} collective-permute-done((f32[35,256]{1,0:T(8,128)S(1)}, f32[35,256]{1,0:T(8,128)S(1)}, u32[]{:S(2)}, u32[]{:S(2)}) %collective-permute-start.29) | collective-permute-done | bytes 35872 | tf_op jit(solution)/shard_map/ppermute | solution.py:480
  471.2 3.1 collective-permute-start.31
  478.5 3.2 add_convert_fusion.7
  490.5 64.6 %shard_map.212 = bf16[512,2048]{1,0:T(8,128)(2,1)} custom-call(bf16[512,2048]{1,0:T(8,128)(2,1)} %bitcast.118), custom_call_target="tpu_custom_call" | custom-call | bytes 4194304 | tf_op jit(solution)/shard_map/pallas_call | solution.py:458
  557.0 2.9 collective-permute-start.37
  560.5 4.4 collective-permute-done.37
  567.7 64.6 %shard_map.216 = bf16[512,2048]{1,0:T(8,128)(2,1)} custom-call(bf16[512,2048]{1,0:T(8,128)(2,1)} %bitcast.33.x), custom_call_target="tpu_custom_call" | custom-call | bytes 4194304 | tf_op jit(solution)/shard_map/pallas_call | solution.py:458
  (293 shorter events, 138.3 us)
Async XLA Ops:
  0.6 159.7 %copy-start = (bf16[704,2048]{1,0:T(8,128)(2,1)S(1)}, bf16[704,2048]{1,0:T(8,128)(2,1)}, u32[]{:S(2)}) copy-start(bf16[704,2048]{1,0:T(8,128)(2,1)} %param.23) | copy-start | bytes 8650756
  3.0 262.7 %copy-start.58 = (s32[3]{0:T(128)}, s32[3]{0:T(128)S(1)}, u32[]{:S(2)}) copy-start(s32[3]{0:T(128)S(1)} %pad_add_fusion.place) | copy-start | bytes 40
  34.1 16.0 %collective-permute-start.1 = (bf16[4,512,128]{2,1,0:T(8,128)(2,1)}, bf16[4,512,128]{2,1,0:T(8,128)(2,1)}, u32[]{:S(2)}, u32[]{:S(2)}) collective-permute-start(bf16[4,512,128]{2,1,0:T(8,128)(2,1)} %all_to_all.45.kv0), channel_id=1, source_target_pairs={{0,16},{16,0},{1,17},{17,1},{2,18},{18,2},{3,19},{19,3},{4,20},{20... | collective-permute-start | bytes 1572872 | tf_op jit(solution)/shard_map/ppermute | solution.py:416
  35.1 15.0 %collective-permute-start.2 = (bf16[256,128]{1,0:T(8,128)(2,1)S(1)}, bf16[256,128]{1,0:T(8,128)(2,1)S(1)}, u32[]{:S(2)}, u32[]{:S(2)}) collective-permute-start(bf16[256,128]{1,0:T(8,128)(2,1)S(1)} %get-tuple-element.116), channel_id=1, source_target_pairs={{0,32},{32,0},{64,96},{96,64},{1,33},{33,1},{65,97},{97,65},{2,34}... | collective-permute-start | bytes 196616 | tf_op jit(solution)/shard_map/ppermute | solution.py:421
  36.6 13.5 %collective-permute-start.3 = (bf16[256,128]{1,0:T(8,128)(2,1)S(1)}, bf16[256,128]{1,0:T(8,128)(2,1)S(1)}, u32[]{:S(2)}, u32[]{:S(2)}) collective-permute-start(bf16[256,128]{1,0:T(8,128)(2,1)S(1)} %get-tuple-element.117), channel_id=1, source_target_pairs={{0,64},{32,96},{64,0},{96,32},{1,65},{33,97},{65,1},{97,33},{2,66}... | collective-permute-start | bytes 196616 | tf_op jit(solution)/shard_map/ppermute | solution.py:421
  37.2 12.9 %collective-permute-start.4 = (bf16[256,128]{1,0:T(8,128)(2,1)S(1)}, bf16[256,128]{1,0:T(8,128)(2,1)S(1)}, u32[]{:S(2)}, u32[]{:S(2)}) collective-permute-start(bf16[256,128]{1,0:T(8,128)(2,1)S(1)} %get-tuple-element.118), channel_id=1, source_target_pairs={{0,96},{32,64},{64,32},{96,0},{1,97},{33,65},{65,33},{97,1},{2,98}... | collective-permute-start | bytes 196616 | tf_op jit(solution)/shard_map/ppermute | solution.py:421
  41.6 8.7 %collective-permute-start = (bf16[4,512,128]{2,1,0:T(8,128)(2,1)}, bf16[4,512,128]{2,1,0:T(8,128)(2,1)}, u32[]{:S(2)}, u32[]{:S(2)}) collective-permute-start(bf16[4,512,128]{2,1,0:T(8,128)(2,1)} %all_to_all.45.kv0), channel_id=1, source_target_pairs={{0,8},{8,0},{1,9},{9,1},{2,10},{10,2},{3,11},{11,3},{4,12},{12,4},... | collective-permute-start | bytes 1572872 | tf_op jit(solution)/shard_map/ppermute | solution.py:416
  50.1 2.3 collective-permute-start.5
  73.4 6.6 %collective-permute-start.6 = (bf16[256,128]{1,0:T(8,128)(2,1)S(1)}, bf16[256,128]{1,0:T(8,128)(2,1)S(1)}, u32[]{:S(2)}, u32[]{:S(2)}) collective-permute-start(bf16[256,128]{1,0:T(8,128)(2,1)S(1)} %get-tuple-element.125), channel_id=1, source_target_pairs={{0,32},{32,0},{64,96},{96,64},{1,33},{33,1},{65,97},{97,65},{2,34}... | collective-permute-start | bytes 196616 | tf_op jit(solution)/shard_map/ppermute | solution.py:421
  75.2 6.1 collective-permute-start.7
  76.5 8.2 %collective-permute-start.8 = (bf16[256,128]{1,0:T(8,128)(2,1)S(1)}, bf16[256,128]{1,0:T(8,128)(2,1)S(1)}, u32[]{:S(2)}, u32[]{:S(2)}) collective-permute-start(bf16[256,128]{1,0:T(8,128)(2,1)S(1)} %get-tuple-element.127), channel_id=1, source_target_pairs={{0,96},{32,64},{64,32},{96,0},{1,97},{33,65},{65,33},{97,1},{2,98}... | collective-permute-start | bytes 196616 | tf_op jit(solution)/shard_map/ppermute | solution.py:421
  88.0 30.2 %all-to-all-start.1 = ((bf16[8,64,2048]{2,1,0:T(8,128)(2,1)}), bf16[8,64,2048]{2,1,0:T(8,128)(2,1)}, u32[]{:S(2)}, u32[]{:S(2)}) async-start(bf16[8,64,2048]{2,1,0:T(8,128)(2,1)} %bitcast.109), calls=%async_computation.1 | async-start | bytes 4194304 | tf_op jit(solution)/shard_map/all_to_all | solution.py:470
  123.9 30.1 %all-to-all-start.2 = ((bf16[8,64,2048]{2,1,0:T(8,128)(2,1)}), bf16[8,64,2048]{2,1,0:T(8,128)(2,1)}, u32[]{:S(2)}, u32[]{:S(2)}) async-start(bf16[8,64,2048]{2,1,0:T(8,128)(2,1)} %copy-done.13), calls=%async_computation.2 | async-start | bytes 4194304 | tf_op jit(solution)/shard_map/all_to_all | solution.py:474
  171.4 30.0 %all-to-all-start.3 = ((bf16[8,64,2048]{2,1,0:T(8,128)(2,1)}), bf16[8,64,2048]{2,1,0:T(8,128)(2,1)}, u32[]{:S(2)}, u32[]{:S(2)}) async-start(bf16[8,64,2048]{2,1,0:T(8,128)(2,1)} %bitcast.120), calls=%async_computation.3 | async-start | bytes 4194304 | tf_op jit(solution)/shard_map/all_to_all | solution.py:470
  201.4 10.0 %collective-permute-start.9 = (bf16[8,2112,128]{2,1,0:T(8,128)(2,1)}, bf16[8,2112,128]{2,1,0:T(8,128)(2,1)}, u32[]{:S(2)}, u32[]{:S(2)}) collective-permute-start(bf16[8,2112,128]{2,1,0:T(8,128)(2,1)} %copy-done.63), channel_id=1, source_target_pairs={{0,8},{8,0},{1,9},{9,1},{2,10},{10,2},{3,11},{11,3},{4,12},{12,4},... | collective-permute-start | bytes 12976136 | tf_op jit(solution)/shard_map/ppermute | solution.py:416
  207.0 32.3 %all-to-all-start.4 = ((bf16[8,64,2048]{2,1,0:T(8,128)(2,1)}), bf16[8,64,2048]{2,1,0:T(8,128)(2,1)}, u32[]{:S(2)}, u32[]{:S(2)}) async-start(bf16[8,64,2048]{2,1,0:T(8,128)(2,1)} %copy-done.10), calls=%async_computation.4 | async-start | bytes 4194304 | tf_op jit(solution)/shard_map/all_to_all | solution.py:474
  217.7 27.8 %collective-permute-start.10 = (bf16[2,2112,128]{2,1,0:T(8,128)(2,1)}, bf16[2,2112,128]{2,1,0:T(8,128)(2,1)}, u32[]{:S(2)}, u32[]{:S(2)}) collective-permute-start(bf16[2,2112,128]{2,1,0:T(8,128)(2,1)} %get-tuple-element.220), channel_id=1, source_target_pairs={{0,16},{16,32},{32,48},{48,0},{1,17},{17,33},{33,49},{49,1},{2,18}... | collective-permute-start | bytes 3244040 | tf_op jit(solution)/shard_map/ppermute | solution.py:439
  218.8 26.8 %collective-permute-start.11 = (bf16[2,2112,128]{2,1,0:T(8,128)(2,1)}, bf16[2,2112,128]{2,1,0:T(8,128)(2,1)}, u32[]{:S(2)}, u32[]{:S(2)}) collective-permute-start(bf16[2,2112,128]{2,1,0:T(8,128)(2,1)} %get-tuple-element.219), channel_id=1, source_target_pairs={{0,48},{16,0},{32,16},{48,32},{1,49},{17,1},{33,17},{49,33},{2,50}... | collective-permute-start | bytes 3244040 | tf_op jit(solution)/shard_map/ppermute | solution.py:439
  245.5 9.9 %collective-permute-start.12 = (bf16[256,128]{1,0:T(8,128)(2,1)S(1)}, bf16[256,128]{1,0:T(8,128)(2,1)S(1)}, u32[]{:S(2)}, u32[]{:S(2)}) collective-permute-start(bf16[256,128]{1,0:T(8,128)(2,1)S(1)} %get-tuple-element.147), channel_id=1, source_target_pairs={{0,32},{32,0},{64,96},{96,64},{1,33},{33,1},{65,97},{97,65},{2,34}... | collective-permute-start | bytes 196616 | tf_op jit(solution)/shard_map/ppermute | solution.py:421
  247.0 8.4 %collective-permute-start.13 = (bf16[256,128]{1,0:T(8,128)(2,1)S(1)}, bf16[256,128]{1,0:T(8,128)(2,1)S(1)}, u32[]{:S(2)}, u32[]{:S(2)}) collective-permute-start(bf16[256,128]{1,0:T(8,128)(2,1)S(1)} %get-tuple-element.148), channel_id=1, source_target_pairs={{0,64},{32,96},{64,0},{96,32},{1,65},{33,97},{65,1},{97,33},{2,66}... | collective-permute-start | bytes 196616 | tf_op jit(solution)/shard_map/ppermute | solution.py:421
  250.0 8.2 %collective-permute-start.14 = (bf16[256,128]{1,0:T(8,128)(2,1)S(1)}, bf16[256,128]{1,0:T(8,128)(2,1)S(1)}, u32[]{:S(2)}, u32[]{:S(2)}) collective-permute-start(bf16[256,128]{1,0:T(8,128)(2,1)S(1)} %get-tuple-element.149), channel_id=1, source_target_pairs={{0,96},{32,64},{64,32},{96,0},{1,97},{33,65},{65,33},{97,1},{2,98}... | collective-permute-start | bytes 196616 | tf_op jit(solution)/shard_map/ppermute | solution.py:421
  258.8 47.2 %all-to-all-start.5 = ((bf16[8,64,2048]{2,1,0:T(8,128)(2,1)}), bf16[8,64,2048]{2,1,0:T(8,128)(2,1)S(1)}, u32[]{:S(2)}, u32[]{:S(2)}) async-start(bf16[8,64,2048]{2,1,0:T(8,128)(2,1)} %bitcast.119), calls=%async_computation.5 | async-start | bytes 4194304 | tf_op jit(solution)/shard_map/all_to_all | solution.py:470
  263.6 42.4 %collective-permute-start.15 = (bf16[2,2112,128]{2,1,0:T(8,128)(2,1)}, bf16[2,2112,128]{2,1,0:T(8,128)(2,1)}, u32[]{:S(2)}, u32[]{:S(2)}) collective-permute-start(bf16[2,2112,128]{2,1,0:T(8,128)(2,1)} %get-tuple-element.166), channel_id=1, source_target_pairs={{0,32},{16,48},{32,0},{48,16},{1,33},{17,49},{33,1},{49,17},{2,34}... | collective-permute-start | bytes 3244040 | tf_op jit(solution)/shard_map/ppermute | solution.py:439
  306.0 2.8 collective-permute-start.16
  310.9 2.0 collective-permute-start.17
  315.6 61.7 %all-to-all-start.6 = ((bf16[8,64,2048]{2,1,0:T(8,128)(2,1)}), bf16[8,64,2048]{2,1,0:T(8,128)(2,1)S(1)}, u32[]{:S(2)}, u32[]{:S(2)}) async-start(bf16[8,64,2048]{2,1,0:T(8,128)(2,1)} %copy-done.2), calls=%async_computation.6 | async-start | bytes 4194304 | tf_op jit(solution)/shard_map/all_to_all | solution.py:474
  321.3 41.1 %collective-permute-start.19 = (bf16[4,512,128]{2,1,0:T(8,128)(2,1)}, bf16[4,512,128]{2,1,0:T(8,128)(2,1)S(1)}, u32[]{:S(2)}, u32[]{:S(2)}) collective-permute-start(bf16[4,512,128]{2,1,0:T(8,128)(2,1)} %add_convert_fusion.8), channel_id=1, source_target_pairs={{0,16},{16,0},{1,17},{17,1},{2,18},{18,2},{3,19},{19,3},{4,20},{20... | collective-permute-start | bytes 1572872 | tf_op jit(solution)/shard_map/ppermute | solution.py:416
  321.8 48.9 %collective-permute-start.18 = (bf16[2112,128]{1,0:T(8,128)(2,1)}, bf16[2112,128]{1,0:T(8,128)(2,1)S(1)}, u32[]{:S(2)}, u32[]{:S(2)}) collective-permute-start(bf16[2112,128]{1,0:T(8,128)(2,1)} %fusion.16), channel_id=1, source_target_pairs={{0,64},{64,0},{1,65},{65,1},{2,66},{66,2},{3,67},{67,3},{4,68},{68... | collective-permute-start | bytes 1622024 | tf_op jit(solution)/shard_map/ppermute | solution.py:416
  324.4 14.9 %collective-permute-start.20 = (bf16[256,128]{1,0:T(8,128)(2,1)S(1)}, bf16[256,128]{1,0:T(8,128)(2,1)S(1)}, u32[]{:S(2)}, u32[]{:S(2)}) collective-permute-start(bf16[256,128]{1,0:T(8,128)(2,1)S(1)} %get-tuple-element.183), channel_id=1, source_target_pairs={{0,32},{32,0},{64,96},{96,64},{1,33},{33,1},{65,97},{97,65},{2,34}... | collective-permute-start | bytes 196616 | tf_op jit(solution)/shard_map/ppermute | solution.py:421
  327.8 33.0 %collective-permute-start.21 = (bf16[256,128]{1,0:T(8,128)(2,1)S(1)}, bf16[256,128]{1,0:T(8,128)(2,1)S(1)}, u32[]{:S(2)}, u32[]{:S(2)}) collective-permute-start(bf16[256,128]{1,0:T(8,128)(2,1)S(1)} %get-tuple-element.184), channel_id=1, source_target_pairs={{0,64},{32,96},{64,0},{96,32},{1,65},{33,97},{65,1},{97,33},{2,66}... | collective-permute-start | bytes 196616 | tf_op jit(solution)/shard_map/ppermute | solution.py:421
  329.4 33.1 %collective-permute-start.22 = (bf16[256,128]{1,0:T(8,128)(2,1)S(1)}, bf16[256,128]{1,0:T(8,128)(2,1)S(1)}, u32[]{:S(2)}, u32[]{:S(2)}) collective-permute-start(bf16[256,128]{1,0:T(8,128)(2,1)S(1)} %get-tuple-element.185), channel_id=1, source_target_pairs={{0,96},{32,64},{64,32},{96,0},{1,97},{33,65},{65,33},{97,1},{2,98}... | collective-permute-start | bytes 196616 | tf_op jit(solution)/shard_map/ppermute | solution.py:421
  363.8 6.8 %collective-permute-start.23 = (bf16[512,128]{1,0:T(8,128)(2,1)S(1)}, bf16[512,128]{1,0:T(8,128)(2,1)S(1)}, u32[]{:S(2)}, u32[]{:S(2)}) collective-permute-start(bf16[512,128]{1,0:T(8,128)(2,1)S(1)} %get-tuple-element.230), channel_id=1, source_target_pairs={{0,32},{32,0},{64,96},{96,64},{1,33},{33,1},{65,97},{97,65},{2,34}... | collective-permute-start | bytes 393224 | tf_op jit(solution)/shard_map/ppermute | solution.py:421
  366.0 7.1 %collective-permute-start.24 = (bf16[512,128]{1,0:T(8,128)(2,1)S(1)}, bf16[512,128]{1,0:T(8,128)(2,1)S(1)}, u32[]{:S(2)}, u32[]{:S(2)}) collective-permute-start(bf16[512,128]{1,0:T(8,128)(2,1)S(1)} %get-tuple-element.229), channel_id=1, source_target_pairs={{0,64},{32,96},{64,0},{96,32},{1,65},{33,97},{65,1},{97,33},{2,66}... | collective-permute-start | bytes 393224 | tf_op jit(solution)/shard_map/ppermute | solution.py:421
  367.6 9.1 %collective-permute-start.25 = (bf16[512,128]{1,0:T(8,128)(2,1)S(1)}, bf16[512,128]{1,0:T(8,128)(2,1)S(1)}, u32[]{:S(2)}, u32[]{:S(2)}) collective-permute-start(bf16[512,128]{1,0:T(8,128)(2,1)S(1)} %get-tuple-element.228), channel_id=1, source_target_pairs={{0,96},{32,64},{64,32},{96,0},{1,97},{33,65},{65,33},{97,1},{2,98}... | collective-permute-start | bytes 393224 | tf_op jit(solution)/shard_map/ppermute | solution.py:421
  399.0 30.3 %all-to-all-start.7 = ((bf16[8,64,2048]{2,1,0:T(8,128)(2,1)}), bf16[8,64,2048]{2,1,0:T(8,128)(2,1)S(1)}, u32[]{:S(2)}, u32[]{:S(2)}) async-start(bf16[8,64,2048]{2,1,0:T(8,128)(2,1)} %bitcast.108), calls=%async_computation.7 | async-start | bytes 4194304 | tf_op jit(solution)/shard_map/all_to_all | solution.py:470
  415.2 63.4 %collective-permute-start.33 = (bf16[8,1024,128]{2,1,0:T(8,128)(2,1)}, bf16[8,1024,128]{2,1,0:T(8,128)(2,1)}, u32[]{:S(2)}, u32[]{:S(2)}) collective-permute-start(bf16[8,1024,128]{2,1,0:T(8,128)(2,1)} %get-tuple-element.215), channel_id=1, source_target_pairs={{0,8},{8,0},{1,9},{9,1},{2,10},{10,2},{3,11},{11,3},{4,12},{12,4},... | collective-permute-start | bytes 6291464 | tf_op jit(solution)/shard_map/ppermute | solution.py:416
  429.3 1.2 collective-permute-start.26
  430.5 10.2 %collective-permute-start.27 = (f32[35,256]{1,0:T(8,128)S(1)}, f32[35,256]{1,0:T(8,128)S(1)}, u32[]{:S(2)}, u32[]{:S(2)}) collective-permute-start(f32[35,256]{1,0:T(8,128)S(1)} %add.279), channel_id=1, source_target_pairs={{0,16},{16,0},{1,17},{17,1},{2,18},{18,2},{3,19},{19,3},{4,20},{20... | collective-permute-start | bytes 107528 | tf_op jit(solution)/shard_map/ppermute | solution.py:480
  436.2 131.5 %all-to-all-start.8 = ((bf16[8,64,2048]{2,1,0:T(8,128)(2,1)}), bf16[8,64,2048]{2,1,0:T(8,128)(2,1)}, u32[]{:S(2)}, u32[]{:S(2)}) async-start(bf16[8,64,2048]{2,1,0:T(8,128)(2,1)} %shard_map.215), calls=%async_computation.8 | async-start | bytes 4194304 | tf_op jit(solution)/shard_map/all_to_all | solution.py:474
  440.7 5.6 collective-permute-start.28
  446.3 20.8 %collective-permute-start.29 = (f32[35,256]{1,0:T(8,128)S(1)}, f32[35,256]{1,0:T(8,128)S(1)}, u32[]{:S(2)}, u32[]{:S(2)}) collective-permute-start(f32[35,256]{1,0:T(8,128)S(1)} %add.281), channel_id=1, source_target_pairs={{0,64},{64,0},{1,65},{65,1},{2,66},{66,2},{3,67},{67,3},{4,68},{68... | collective-permute-start | bytes 107528 | tf_op jit(solution)/shard_map/ppermute | solution.py:480
  467.2 4.0 collective-permute-start.30
  471.2 5.5 collective-permute-start.31
  476.7 79.0 %collective-permute-start.32 = (f32[4,2048]{1,0:T(4,128)S(1)}, f32[4,2048]{1,0:T(4,128)S(1)}, u32[]{:S(2)}, u32[]{:S(2)}) collective-permute-start(f32[4,2048]{1,0:T(4,128)S(1)} %add.284), channel_id=1, source_target_pairs={{0,1},{1,0},{2,3},{3,2},{4,5},{5,4},{6,7},{7,6},{8,9},{9,8},{10,11... | collective-permute-start | bytes 98312 | tf_op jit(solution)/shard_map/ppermute | solution.py:480
  481.8 74.0 %collective-permute-start.34 = (bf16[2,1024,128]{2,1,0:T(8,128)(2,1)}, bf16[2,1024,128]{2,1,0:T(8,128)(2,1)S(1)}, u32[]{:S(2)}, u32[]{:S(2)}) collective-permute-start(bf16[2,1024,128]{2,1,0:T(8,128)(2,1)} %get-tuple-element.226), channel_id=1, source_target_pairs={{0,16},{16,32},{32,48},{48,0},{1,17},{17,33},{33,49},{49,1},{2,18}... | collective-permute-start | bytes 1572872 | tf_op jit(solution)/shard_map/ppermute | solution.py:439
  483.0 72.8 %collective-permute-start.35 = (bf16[2,1024,128]{2,1,0:T(8,128)(2,1)}, bf16[2,1024,128]{2,1,0:T(8,128)(2,1)}, u32[]{:S(2)}, u32[]{:S(2)}) collective-permute-start(bf16[2,1024,128]{2,1,0:T(8,128)(2,1)} %get-tuple-element.225), channel_id=1, source_target_pairs={{0,32},{16,48},{32,0},{48,16},{1,33},{17,49},{33,1},{49,17},{2,34}... | collective-permute-start | bytes 1572872 | tf_op jit(solution)/shard_map/ppermute | solution.py:439
  484.8 71.0 %collective-permute-start.36 = (bf16[2,1024,128]{2,1,0:T(8,128)(2,1)S(1)}, bf16[2,1024,128]{2,1,0:T(8,128)(2,1)}, u32[]{:S(2)}, u32[]{:S(2)}) collective-permute-start(bf16[2,1024,128]{2,1,0:T(8,128)(2,1)S(1)} %get-tuple-element.224), channel_id=1, source_target_pairs={{0,48},{16,0},{32,16},{48,32},{1,49},{17,1},{33,17},{49,33},{2,50}... | collective-permute-start | bytes 1572872 | tf_op jit(solution)/shard_map/ppermute | solution.py:439
  557.0 8.0 %collective-permute-start.37 = (bf16[1024,128]{1,0:T(8,128)(2,1)S(1)}, bf16[1024,128]{1,0:T(8,128)(2,1)S(1)}, u32[]{:S(2)}, u32[]{:S(2)}) collective-permute-start(bf16[1024,128]{1,0:T(8,128)(2,1)S(1)} %fusion.27), channel_id=1, source_target_pairs={{0,64},{64,0},{1,65},{65,1},{2,66},{66,2},{3,67},{67,3},{4,68},{68... | collective-permute-start | bytes 786440 | tf_op jit(solution)/shard_map/ppermute | solution.py:416
  (93 other events, 712.5 us)

commit v3 on v2

v3 whole, which is shorter than its diff:
```python
import functools

import jax
import jax.numpy as jnp
from jax import lax
from jax.experimental import pallas as pl
from jax.experimental.pallas import tpu as pltpu
from jax.sharding import Mesh
from jax.sharding import PartitionSpec as P

HDIM = 64
DOCS = 3
BLOCK = 512
HALF = 256
LOW = jnp.bfloat16
WIDE = jnp.float32
CTX = ("xh", "zh", "zl", "core")
TP = ("y", "xl")
SPREAD = ("xh", "zh")
Z = ("zh", "zl")


def size_of(a):
    return a.size * jnp.dtype(a.dtype).itemsize


def kernel_call(
    body, outs, inputs, *, small=(), small_outs=(), scalars=(), scratch=(), late=0, flops=0, exps=0, mib=12
):
    counts = [len(x) for x in (scalars, inputs, small, outs, small_outs, inputs, outs)]

    def run(*refs):
        groups, at = [], 0
        for n in counts:
            groups.append(refs[at : at + n])
            at += n
        scalar_refs, far_in, near_in, far_out, near_out, held_in, held_out = groups
        arrived, left, *rest = refs[at:]
        moves = [
            pltpu.make_async_copy(a, b, arrived.at[k]) for k, (a, b) in enumerate(zip(far_in, held_in))
        ]
        for move in moves:
            move.start()
        early = len(moves) - late
        for move in moves[:early]:
            move.wait()

        def arrive():
            for move in moves[early:]:
                move.wait()

        body(
            *([arrive] if late else []),
            *scalar_refs, *held_in, *near_in, *held_out, *near_out, *rest,
        )
        moves = [
            pltpu.make_async_copy(a, b, left.at[k]) for k, (a, b) in enumerate(zip(held_out, far_out))
        ]
        for move in moves:
            move.start()
        for move in moves:
            move.wait()

    vmem, hbm = pl.BlockSpec(memory_space=pltpu.VMEM), pl.BlockSpec(memory_space=pltpu.HBM)
    held = [pltpu.VMEM(a.shape, a.dtype) for a in (*inputs, *outs)]
    limit = sum(size_of(a) for a in (*inputs, *outs, *small, *small_outs)) + mib * 1024 * 1024
    return pl.pallas_call(
        run,
        out_shape=(*outs, *small_outs),
        in_specs=[pl.BlockSpec(memory_space=pltpu.SMEM)] * len(scalars)
        + [hbm] * len(inputs)
        + [vmem] * len(small),
        out_specs=(*[hbm] * len(outs), *[vmem] * len(small_outs)),
        scratch_shapes=[
            *held,
            pltpu.SemaphoreType.DMA((len(inputs),)),
            pltpu.SemaphoreType.DMA((max(1, len(outs)),)),
            *scratch,
        ],
        compiler_params=pltpu.CompilerParams(vmem_limit_bytes=limit),
        cost_estimate=pl.CostEstimate(
            flops=flops,
            bytes_accessed=sum(size_of(a) for a in (*inputs, *outs)),
            transcendentals=exps,
        ),
    )(*scalars, *inputs, *small)


def lane_of(shape):
    return lax.broadcasted_iota(jnp.int32, shape, len(shape) - 1)


def exchange_halves(a, b):
    front = lane_of(a.shape) < HDIM
    return (
        jnp.where(front, a, pltpu.roll(b, HDIM, 1)),
        jnp.where(front, pltpu.roll(a, HDIM, 1), b),
    )


def nt(a, b):
    return lax.dot_general(a, b, (((1,), (1,)), ((), ())), preferred_element_type=WIDE)


def nn(a, b):
    return lax.dot_general(a, b, (((1,), (0,)), ((), ())), preferred_element_type=WIDE)


def turn(x, cosine, sine, sign):
    lane = lax.rem(lane_of(x.shape), HDIM)
    ahead = pltpu.roll(x, x.shape[1] - 8, 1)
    behind = pltpu.roll(x, 8, 1)
    swapped = jnp.where(lane < 8, -ahead, behind) * sign
    return x * cosine + swapped * sine


def rotation_table(angles_table):
    tokens = angles_table.shape[1]
    rest = jnp.zeros((112, tokens), WIDE)
    x = jnp.concatenate([angles_table, rest], axis=0).T
    lane = lane_of(x.shape)
    c = jnp.where(lane < 8, x, 0.0)
    c = c + pltpu.roll(c, 8, 1)
    c = c + pltpu.roll(c, HDIM, 1) + jnp.where(lax.rem(lane, HDIM) < 16, 0.0, 1.0)
    s = jnp.where((lane >= 8) & (lane < 16), x, 0.0)
    s = s + pltpu.roll(s, 120, 1)
    s = s + pltpu.roll(s, HDIM, 1)
    return c, s


def project_kernel(
    arrive, place, tok, table, w, gain, shift, bias,
    normed, stats, kv0, kv1, kv2, kv3, q0, q1, q2, q3, cosine_out, sine_out, kept_kv, kept_q,
):
    rows = 64

    def norm_rows(i, carry):
        at = pl.ds(pl.multiple_of(i * rows, rows), rows)
        x = tok[at, :].astype(WIDE)
        mean = jnp.mean(x, axis=-1, keepdims=True)
        center = x - mean
        scale = lax.rsqrt(jnp.mean(center * center, axis=-1, keepdims=True) + 1e-05)
        normed[at, :] = (center * scale * gain[...] + shift[...]).astype(LOW)
        stats[at, :] = jnp.where(lane_of((rows, 128)) < HDIM, mean, scale)
        return carry

    lax.fori_loop(0, BLOCK // rows, norm_rows, 0)
    cosine, sine = rotation_table(table[...])
    cosine_out[...] = cosine
    sine_out[...] = sine
    arrive()
    mixed = [nn(normed[...], w[c]) + bias[c : c + 1, :] for c in range(3)]
    for pair in range(2):
        lanes = slice(pair * 128, pair * 128 + 128)
        q = turn(mixed[0][:, lanes], cosine, sine, 1.0) * 0.125
        k = turn(mixed[1][:, lanes], cosine, sine, 1.0)
        kv = exchange_halves(k, mixed[2][:, lanes])
        qq = exchange_halves(q[:HALF], q[HALF:])
        for one in range(2):
            kept_kv[2 * pair + one] = kv[one].astype(LOW)
            kept_q[2 * pair + one] = qq[one].astype(LOW)
    for k in range(4):
        (kv0, kv1, kv2, kv3)[k][...] = kept_kv[place[1] ^ k]
        (q0, q1, q2, q3)[k][...] = kept_q[place[1] ^ k]


def padded_queries(q2):
    x = q2.astype(WIDE)
    front = lane_of(x.shape) < HDIM
    return (
        jnp.where(front, x, 0.0).astype(LOW),
        jnp.where(front, pltpu.roll(x, HDIM, 1), 0.0).astype(LOW),
    )


def padded_behind(d2):
    x = d2.astype(WIDE)
    front = lane_of(x.shape) < HDIM
    return (
        jnp.where(front, 0.0, pltpu.roll(x, HDIM, 1)).astype(LOW),
        jnp.where(front, 0.0, x).astype(LOW),
    )


def allowed_keys(key_block, first_query, begin):
    shape = (BLOCK, begin.shape[1])
    key_at = key_block * BLOCK + lax.broadcasted_iota(jnp.int32, shape, 0)
    query_at = first_query + lax.broadcasted_iota(jnp.int32, shape, 1)
    return (key_at <= query_at) & (key_at >= begin)


def key_blocks(place, rels, t):
    return [4 * t + (place[0] ^ rel) for rel in rels], place[1] ^ t


def forward_kernel(rels, first, last, *refs):
    place, kv0, kv1, q0, q1, q2, q3, begin = refs[:8]
    if first:
        acc_out, peak_out, kvt, queries, kept_q = refs[8:]
    else:
        acc_in, peak_in, o0, o1, o2, o3, out_t, total, kvt, queries, kept_q, kept_o = refs[8:]
        acc_out, peak_out = out_t, total
    me = place[1]
    front = lane_of((BLOCK, 128)) < HDIM
    for k, q in enumerate((q0, q1, q2, q3)):
        kept_q[me ^ k] = q[...]
    for i, kv in enumerate((kv0, kv1)):
        for t in range(4):
            kvt[i, t] = jnp.where(front, 1.0, kv[t].astype(WIDE)).T.astype(LOW)

    def one_query_block(j, carry):
        first_query = (4 * j + place[0]) * BLOCK
        queries[:HALF, :], queries[HALF:, :] = padded_queries(kept_q[j])
        if first:
            peak_out[j] = jnp.full((8, BLOCK), -1e30, WIDE)
            acc_out[j] = jnp.zeros((128, BLOCK), WIDE)
        else:
            peak_out[j] = peak_in[j]
            acc_out[j] = acc_in[j]

        def two_blocks(t, carry):
            blocks, at = key_blocks(place, rels, t)
            scores = []
            for i, kv in enumerate((kv0, kv1)):
                ok = allowed_keys(blocks[i], first_query, begin[j, :1])
                scores.append(jnp.where(ok, nt(kv[at], queries[...]), -1e30))
            old = peak_out[j, :1]
            new = old
            for one in scores:
                new = jnp.maximum(new, jnp.max(one, axis=0, keepdims=True))
            done = acc_out[j] * jnp.exp(old - new)
            for i in range(2):
                done += nn(kvt[i, at], jnp.exp(scores[i] - new).astype(LOW))
            acc_out[j] = done
            peak_out[j, :1] = new
            return carry

        lax.fori_loop(0, j + 1, two_blocks, 0)
        if last:
            weight_sum = acc_out[j, :1]
            done = acc_out[j] / weight_sum
            out_t[j] = done
            total[j, :1] = peak_out[j, :1] + jnp.log(weight_sum)
            rows = done.T
            x, y = rows[:HALF], rows[HALF:]
            kept_o[j] = jnp.where(lane_of(x.shape) < HDIM, pltpu.roll(x, HDIM, 1), y).astype(LOW)
        return carry

    lax.fori_loop(0, 4, one_query_block, 0)
    if last:
        for k, out in enumerate((o0, o1, o2, o3)):
            out[...] = kept_o[me ^ k]


def backward_kernel(rels, first, *refs):
    place, kv0, kv1, q0, q1, q2, q3, d0, d1, d2, d3, out_t, total, begin = refs[:14]
    if first:
        acc, keep, send, kvt, queries, grads, dot_rows, dkv, kept_q, kept_d = refs[14:]
    else:
        (
            acc_in, g0, g1, g2, g3, keep, send,
            kvt, queries, grads, dot_rows, dkv, kept_q, kept_d, acc, kept_g,
        ) = refs[14:]
    me = place[1]
    for k in range(4):
        kept_q[me ^ k] = (q0, q1, q2, q3)[k][...]
        kept_d[me ^ k] = (d0, d1, d2, d3)[k][...]
    for i, kv in enumerate((kv0, kv1)):
        for t in range(4):
            kvt[i, t] = kv[t].astype(WIDE).T.astype(LOW)
    dkv[...] = jnp.zeros(dkv.shape, WIDE)

    def one_query_block(j, carry):
        first_query = (4 * j + place[0]) * BLOCK
        queries[:HALF, :], queries[HALF:, :] = padded_queries(kept_q[j])
        grads[:HALF, :], grads[HALF:, :] = padded_behind(kept_d[j])
        dot_rows[...] = jnp.sum(grads[...].astype(WIDE).T * out_t[j], axis=0, keepdims=True)
        acc[j] = jnp.zeros((128, BLOCK), WIDE) if first else acc_in[j]

        def two_blocks(t, carry):
            blocks, at = key_blocks(place, rels, t)
            for i, kv in enumerate((kv0, kv1)):
                term = 0.0
                for half in range(2):
                    some = slice(half * HALF, half * HALF + HALF)
                    ok = allowed_keys(blocks[i], first_query + half * HALF, begin[j, :1, some])
                    scores = nt(kv[at], queries[some, :])
                    probs = jnp.where(ok, jnp.exp(scores - total[j, :1, some]), 0.0)
                    grad_probs = nt(kv[at], grads[some, :])
                    grad_scores = (probs * (grad_probs - dot_rows[:, some])).astype(LOW)
                    term += nn(grad_scores, queries[some, :]) + nn(probs.astype(LOW), grads[some, :])
                    acc[j, :, some] += nn(kvt[i, at], grad_scores)
                dkv[i, at] += term
            return carry

        lax.fori_loop(0, j + 1, two_blocks, 0)
        if not first:
            rows = acc[j].T
            x, y = rows[:HALF], rows[HALF:]
            kept_g[j] = jnp.where(lane_of(x.shape) < HDIM, x, pltpu.roll(y, HDIM, 1)).astype(LOW)
        return carry

    lax.fori_loop(0, 4, one_query_block, 0)
    if not first:
        for k, out in enumerate((g0, g1, g2, g3)):
            out[...] = kept_g[me ^ k]
    for t in range(4):
        keep[t] = dkv[0, t].astype(LOW)
        send[t] = dkv[1, t].astype(LOW)


def branch_kernel(arrive, place, h0, h1, h2, h3, w, attended, partial, kept):
    for k, h in enumerate((h0, h1, h2, h3)):
        kept[place[1] ^ k] = h[...]
    for pair in range(2):
        lanes = slice(pair * 128, pair * 128 + 128)
        x, y = exchange_halves(kept[2 * pair].astype(WIDE), kept[2 * pair + 1].astype(WIDE))
        attended[:HALF, lanes] = x.astype(LOW)
        attended[HALF:, lanes] = y.astype(LOW)
    arrive()
    for n in range(4):
        at = slice(n * 512, n * 512 + 512)
        partial[:, at] = nn(attended[...], w[:, at]).astype(LOW)


def grad_attended_kernel(place, grad, w, d0, d1, d2, d3, kept):
    g = nt(grad[...], w[...])
    for pair in range(2):
        lanes = slice(pair * 128, pair * 128 + 128)
        both = exchange_halves(g[:HALF, lanes], g[HALF:, lanes])
        for one in range(2):
            kept[2 * pair + one] = both[one].astype(LOW)
    for k, out in enumerate((d0, d1, d2, d3)):
        out[...] = kept[place[1] ^ k]


def grad_project_kernel(
    arrive, place, p0, p1, p2, p3, g0, g1, g2, g3, cosine, sine, tok, stats, w,
    grad_mixed, partial, gain_sum, shift_sum, bias_sum, parts, kept,
):
    for k in range(4):
        parts[place[1] ^ k] = (p0, p1, p2, p3)[k][...]
        kept[place[1] ^ k] = (g0, g1, g2, g3)[k][...]
    for pair in range(2):
        lanes = slice(pair * 128, pair * 128 + 128)
        k, v = exchange_halves(parts[2 * pair].astype(WIDE), parts[2 * pair + 1].astype(WIDE))
        q = exchange_halves(kept[2 * pair].astype(WIDE), kept[2 * pair + 1].astype(WIDE))
        q = jnp.concatenate(q, axis=0)
        q = turn(q, cosine[...], sine[...], -1.0) * 0.125
        k = turn(k, cosine[...], sine[...], -1.0)
        for c, part in enumerate((q, k, v)):
            start = c * 256 + pair * 128
            low = part.astype(LOW)
            grad_mixed[:, start : start + 128] = low
            bias_sum[c : c + 1, lanes] = jnp.sum(low.astype(WIDE), axis=0, keepdims=True)
    arrive()
    mean, scale = stats[:, 0:1], stats[:, 64:65]
    for n in range(4):
        at = slice(n * 512, n * 512 + 512)
        total = nt(grad_mixed[:, :256], w[0, at, :])
        total += nt(grad_mixed[:, 256:512], w[1, at, :])
        total += nt(grad_mixed[:, 512:], w[2, at, :])
        partial[:, at] = total.astype(LOW)
        normal = (tok[:, at].astype(WIDE) - mean) * scale
        gain_sum[:, at] = jnp.sum(total * normal, axis=0, keepdims=True)
        shift_sum[:, at] = jnp.sum(total, axis=0, keepdims=True)


def hidden_gradient_kernel(cot, w, grad_hidden):
    grad_hidden[...] = nt(cot[...], w[...])


def feed_kernel(arrive, second, w_gate, w_up, grad_hidden, hidden, grad_gate, grad_up, partial):
    gate = nt(second[...], w_gate[0])
    arrive()
    up = nt(second[...], w_up[0])
    sigmoid = 1.0 / (1.0 + jnp.exp(-gate))
    activated = gate * sigmoid
    hidden[...] = (activated * up).astype(LOW)
    grad = grad_hidden[...]
    grad_up[...] = (grad * activated).astype(LOW)
    grad_gate[...] = (grad * up * sigmoid * (1.0 + gate * (1.0 - sigmoid))).astype(LOW)
    for n in range(4):
        at = slice(n * 512, n * 512 + 512)
        partial[:, at] = (nn(grad_gate[...], w_gate[0, :, at]) + nn(grad_up[...], w_up[0, :, at])).astype(LOW)


def for_rows(work):
    rows = 16

    def one(i, carry):
        work(pl.ds(pl.multiple_of(i * rows, rows), rows))
        return carry

    lax.fori_loop(0, 64 // rows, one, 0)


def summed(parts, at):
    total = parts[0, at, :].astype(WIDE)
    for k in range(1, 8):
        total += parts[k, at, :].astype(WIDE)
    return total


def copy_out(copies, at, value):
    low = value.astype(LOW)
    for k in range(8):
        copies[k, at, :] = low


def second_norm_kernel(parts, tok, gain, shift, copies, middle, normal, stats):
    def work(at):
        x = tok[at, :].astype(WIDE) + summed(parts, at)
        center = x - jnp.mean(x, axis=-1, keepdims=True)
        scale = lax.rsqrt(jnp.mean(center * center, axis=-1, keepdims=True) + 1e-05)
        rows = center * scale
        copy_out(copies, at, rows * gain[...] + shift[...])
        middle[at, :] = x
        normal[at, :] = rows
        stats[at, :] = jnp.broadcast_to(scale, (scale.shape[0], 128))

    for_rows(work)


def norm_gradient(grad, rows, scale, gain):
    scaled = grad * gain
    return scale * (
        scaled
        - jnp.mean(scaled, axis=-1, keepdims=True)
        - rows * jnp.mean(scaled * rows, axis=-1, keepdims=True)
    )


def second_gradient_kernel(parts, cot, normal, stats, gain, copies, grad_middle, sums):
    sums[...] = jnp.zeros(sums.shape, WIDE)

    def work(at):
        grad, rows = summed(parts, at), normal[at, :]
        done = cot[at, :].astype(WIDE) + norm_gradient(grad, rows, stats[at, 0:1], gain[...])
        copy_out(copies, at, done)
        grad_middle[at, :] = done
        sums[0:1, :] += jnp.sum(grad * rows, axis=0, keepdims=True)
        sums[1:2, :] += jnp.sum(grad, axis=0, keepdims=True)

    for_rows(work)


def feed_sum_kernel(place, parts, middle, out):
    rows = 16
    mine = place[3]

    def one(i, carry):
        at = pl.ds(pl.multiple_of(i * rows, rows), rows)
        total = parts[0, at, :].astype(WIDE)
        for k in range(1, 4):
            total += parts[k, at, :].astype(WIDE)
        here = i * rows - mine * 64
        own = pl.ds(pl.multiple_of(jnp.clip(here, 0, 64 - rows), rows), rows)
        inside = (here >= 0) & (here < 64)
        out[at, :] = (total + jnp.where(inside, middle[own, :], 0.0)).astype(LOW)
        return carry

    lax.fori_loop(0, 128 // rows, one, 0)


def layer_out_kernel(a, b, copies):
    rows = 16

    def one(i, carry):
        at = pl.ds(pl.multiple_of(i * rows, rows), rows)
        low = (a[at, :].astype(WIDE) + b[at, :].astype(WIDE)).astype(LOW)
        for k in range(4):
            copies[k, at, :] = low
        return carry

    lax.fori_loop(0, 128 // rows, one, 0)


def first_gradient_kernel(parts, grad_middle, tok, stats, gain, copies):
    def work(at):
        mean, scale = stats[at, 0:1], stats[at, 64:65]
        rows = (tok[at, :].astype(WIDE) - mean) * scale
        done = norm_gradient(summed(parts, at), rows, scale, gain[...])
        copy_out(copies, at, grad_middle[at, :] + done)

    for_rows(work)


def weight_kernel(widths, place, *refs):
    count = len(widths)
    lefts, rights = refs[:count], refs[count : 2 * count]
    mine, theirs, turned = refs[2 * count :]
    first_core = place[2] == 0
    start = 0
    for left, right, width in zip(lefts, rights, widths):
        turned[:width, :] = left[...].astype(WIDE).T.astype(LOW)

        def one(n, carry, start=start, right=right, width=width):
            columns = right[:, pl.ds(pl.multiple_of(n * 256, 256), 256)]
            both = nn(turned[:width, :], columns)
            first, second = both[:, :128], both[:, 128:]
            at = pl.ds(start, width)
            mine[n, at, :] = jnp.where(first_core, first, second).astype(LOW)
            theirs[n, at, :] = jnp.where(first_core, second, first).astype(LOW)
            return carry

        lax.fori_loop(0, 8, one, 0, unroll=4)
        start += width


def weight_grads(pairs, place):
    lefts, rights = [a for a, _ in pairs], [b for _, b in pairs]
    widths = tuple(a.shape[1] for a in lefts)
    out = jax.ShapeDtypeStruct((8, sum(widths), 128), LOW)
    return kernel_call(
        functools.partial(weight_kernel, widths),
        (out, out),
        (*lefts, *rights),
        scalars=(place,),
        scratch=(pltpu.VMEM((max(widths), BLOCK), LOW),),
        flops=2 * sum(widths) * BLOCK * 2048,
    )


def swapped(x, axis):
    return lax.ppermute(x, axis, [(0, 1), (1, 0)])


def across(pieces):
    moved = [
        lax.ppermute(pieces[k], SPREAD, [(i, i ^ k) for i in range(4)]) for k in range(1, 4)
    ]
    return (pieces[0], *moved)


def z_parts(mine, received):
    rows = mine.shape[1]
    mine, received = mine.reshape(2, 4, rows, 128), received.reshape(2, 4, rows, 128)
    z = lax.axis_index(Z)
    done = []
    for k in range(4):
        at = lax.rem(z + k, 4)
        a, b = (lax.dynamic_index_in_dim(x, at, 1, False).astype(WIDE) for x in (mine, received))
        done.append((a + b).astype(LOW))
    return done


def z_permute(part, distance):
    return lax.ppermute(part, Z, [(i, (i + distance) % 4) for i in range(4)])


def xh_halves(moved):
    xh = lax.axis_index("xh")

    def added(at):
        return sum(lax.dynamic_index_in_dim(x, at, 0, False).astype(WIDE) for x in moved)

    return added(xh), added(1 - xh).astype(LOW)


def dealt(x, axis):
    return lax.all_to_all(x, axis, split_axis=0, concat_axis=0, tiled=True)


def tp_parts(partial):
    return dealt(partial.reshape(8, -1, partial.shape[1]), TP)


def tp_rows(copies):
    return dealt(copies, TP).reshape(-1, copies.shape[2])


def summed_by_pairs(x, pairs):
    for axis, size, distance in pairs:
        x = x + lax.ppermute(x, axis, [(i, i ^ distance) for i in range(size)])
    return x


def shape_of(*dims, kind=LOW):
    return jax.ShapeDtypeStruct(dims, kind)


def body(
    tokens, cotangent, segment_ids, first_gain, first_shift, second_gain, second_shift,
    w_qkv, qkv_bias, w_out, w_gate_up, w_down,
):
    ctx = lax.axis_index(CTX)
    tp = lax.axis_index(TP)
    group = lax.axis_index(("zl", "core"))
    place = jnp.stack(
        [group, lax.axis_index(SPREAD), lax.axis_index("core"), lax.axis_index("xl")]
    )
    tied = lax.optimization_barrier

    def my_share(array):
        return lax.dynamic_slice_in_dim(array, tp * 64, 64)

    labels = jnp.arange(DOCS, dtype=jnp.int32)
    starts = jnp.sum((segment_ids[None, :] < labels[:, None]).astype(jnp.int32), axis=1)
    begins = jnp.sum(
        jnp.where(segment_ids[None, :] == labels[:, None], starts[:, None], 0), axis=0
    )
    begin = lax.dynamic_index_in_dim(begins.reshape(4, 4, 1, BLOCK), group, 1, False)
    begin = jnp.broadcast_to(begin, (4, 8, BLOCK))
    own = lax.dynamic_slice_in_dim(begins, ctx * BLOCK, BLOCK)
    places = ctx * BLOCK + jnp.arange(BLOCK, dtype=jnp.int32) - own
    frequency = 10000.0 ** (-jnp.arange(8, dtype=WIDE) / 8.0)
    angles = frequency[:, None] * places.astype(WIDE)[None, :]
    table = jnp.concatenate([jnp.cos(angles), jnp.sin(angles)], axis=0)

    w3 = jnp.transpose(w_qkv, (1, 0, 2))
    w2 = jnp.transpose(w_gate_up, (1, 2, 0))
    quarter, block = shape_of(HALF, 128), shape_of(BLOCK, 128)
    wide_block = shape_of(BLOCK, 128, kind=WIDE)
    four = pltpu.VMEM((4, HALF, 128), LOW)
    normed_low, stats1, *packed, cosine, sine = kernel_call(
        project_kernel,
        (shape_of(BLOCK, 2048), wide_block, *[block] * 4, *[quarter] * 4, wide_block, wide_block),
        (tokens, table, w3),
        small=(first_gain[None], first_shift[None], qkv_bias),
        scalars=(place,),
        scratch=(pltpu.VMEM((4, BLOCK, 128), LOW), four),
        late=1,
        flops=2 * 512 * 2048 * 768,
    )
    kv = jnp.stack(across(packed[:4]))
    queries = across(packed[4:])
    kv_c = swapped(kv, "core")
    state = (shape_of(4, 128, BLOCK, kind=WIDE), shape_of(4, 8, BLOCK, kind=WIDE))
    acc, peak = kernel_call(
        functools.partial(forward_kernel, (0, 1), True, False),
        state,
        (kv, kv_c, *queries, begin),
        scalars=(place,),
        scratch=(pltpu.VMEM((2, 4, 128, BLOCK), LOW), pltpu.VMEM((BLOCK, 128), LOW), four),
        flops=20 * 4 * BLOCK * BLOCK * 128,
        exps=20 * BLOCK * BLOCK,
        mib=24,
    )
    acc, peak, kv_z = tied((acc, peak, swapped(kv, "zl")))
    kv_zc = swapped(kv_z, "core")
    *heads, out_t, total = kernel_call(
        functools.partial(forward_kernel, (2, 3), False, True),
        (*[quarter] * 4, *state),
        (kv_z, kv_zc, *queries, begin, acc, peak),
        scalars=(place,),
        scratch=(pltpu.VMEM((2, 4, 128, BLOCK), LOW), pltpu.VMEM((BLOCK, 128), LOW), four, four),
        flops=20 * 4 * BLOCK * BLOCK * 128,
        exps=20 * BLOCK * BLOCK,
        mib=24,
    )
    heads = across(heads)
    attended_low, partial_branch = kernel_call(
        branch_kernel,
        (shape_of(BLOCK, 256), shape_of(BLOCK, 2048)),
        (*heads, w_out),
        scalars=(place,),
        scratch=(four,),
        late=1,
        flops=2 * 512 * 256 * 2048,
    )
    share = shape_of(64, 2048, kind=WIDE)
    copies = shape_of(8, 64, 2048)
    branch_parts, tok_share, cot_share = tied(
        (tp_parts(partial_branch), my_share(tokens), my_share(cotangent))
    )
    copies2, middle, second_rows, stats2 = kernel_call(
        second_norm_kernel,
        (copies, share, share, shape_of(64, 128, kind=WIDE)),
        (branch_parts, tok_share),
        small=(second_gain[None], second_shift[None]),
    )
    (grad_hidden,) = kernel_call(
        hidden_gradient_kernel,
        (shape_of(BLOCK, 704, kind=WIDE),),
        (tied((cotangent, copies2))[0], w_down),
        flops=2 * 512 * 2048 * 704,
    )
    second_low, grad_hidden = tied((tp_rows(copies2), grad_hidden))
    strip = shape_of(BLOCK, 704)
    hidden_low, grad_gate, grad_up, partial_second = kernel_call(
        feed_kernel,
        (strip, strip, strip, shape_of(BLOCK, 2048)),
        (second_low, w2[:1], w2[1:], grad_hidden),
        late=2,
        flops=8 * 512 * 2048 * 704,
        mib=24,
    )
    second_parts = tp_parts(partial_second)

    feed_mine, feed_theirs = weight_grads(
        ((grad_gate, second_low), (grad_up, second_low), (hidden_low, cotangent)), place
    )
    second_parts, feed_mine, feed_theirs = tied((second_parts, feed_mine, feed_theirs))
    copies3, grad_middle, second_sums = kernel_call(
        second_gradient_kernel,
        (copies, share),
        (second_parts, cot_share, second_rows, stats2),
        small=(second_gain[None],),
        small_outs=(shape_of(2, 2048, kind=WIDE),),
    )
    grad_branch = tp_rows(copies3)
    partial_feed = jnp.dot(hidden_low, w_down, preferred_element_type=WIDE).astype(LOW)
    grad_branch, partial_feed = tied((grad_branch, partial_feed))
    feed_received = swapped(feed_theirs, "core")
    feed_z = z_parts(feed_mine, feed_received)
    feed_1, feed_3 = z_permute(feed_z[1], 1), z_permute(feed_z[3], 3)
    feed_parts = dealt(partial_feed.reshape(4, 128, 2048), "y")

    grads = kernel_call(
        grad_attended_kernel,
        (*[quarter] * 4,),
        (grad_branch, w_out),
        scalars=(place,),
        scratch=(four,),
        flops=2 * 512 * 256 * 2048,
    )
    feed_1, feed_3, *grads = tied((feed_1, feed_3, *grads))
    *grads, feed_2 = tied((*across(grads), feed_z[2]))
    feed_2 = z_permute(feed_2, 2)
    scratch = (
        pltpu.VMEM((2, 4, 128, BLOCK), LOW),
        pltpu.VMEM((BLOCK, 128), LOW),
        pltpu.VMEM((BLOCK, 128), LOW),
        pltpu.VMEM((1, BLOCK), WIDE),
        pltpu.VMEM((2, 4, BLOCK, 128), WIDE),
        four,
        four,
    )
    blocks = shape_of(4, BLOCK, 128)
    acc, keep1, send1 = kernel_call(
        functools.partial(backward_kernel, (2, 3), True),
        (state[0], blocks, blocks),
        (kv_z, kv_zc, *queries, *grads, out_t, total, begin),
        scalars=(place,),
        scratch=scratch,
        flops=20 * 10 * BLOCK * BLOCK * 128,
        exps=20 * BLOCK * BLOCK,
        mib=28,
    )
    acc, send1, feed_parts = tied((acc, send1, feed_parts))
    (feed_half,) = kernel_call(
        feed_sum_kernel, (shape_of(128, 2048),), (feed_parts, middle), scalars=(place,)
    )
    far = (keep1.astype(WIDE) + swapped(send1, "core").astype(WIDE)).astype(LOW)
    acc, far, feed_half = tied((acc, far, feed_half))
    near = kernel_call(
        functools.partial(backward_kernel, (0, 1), False),
        (*[quarter] * 4, blocks, blocks),
        (kv, kv_c, *queries, *grads, out_t, total, begin, acc),
        scalars=(place,),
        scratch=(*scratch, pltpu.VMEM((4, 128, BLOCK), WIDE), four),
        flops=20 * 10 * BLOCK * BLOCK * 128,
        exps=20 * BLOCK * BLOCK,
        mib=28,
    )
    *near, far, feed_other, feed_2 = tied(
        (*near, swapped(far, "zl"), swapped(feed_half, "xl"), feed_2)
    )
    *grad_queries, keep0, send0 = near
    near = keep0.astype(WIDE) + swapped(send0, "core").astype(WIDE)
    grad_queries = across(grad_queries)
    grad_kv = across([(near[k] + far[k].astype(WIDE)).astype(LOW) for k in range(4)])
    (copies4,) = kernel_call(layer_out_kernel, (shape_of(4, 128, 2048),), (feed_half, feed_other))
    layer_out = dealt(copies4, "y").reshape(BLOCK, 2048)
    feed_keep, feed_send = xh_halves([feed_z[0], feed_1, feed_2, feed_3])
    feed_other = swapped(feed_send, "xh")
    grad_mixed, partial_normed, gain_sum, shift_sum, bias_sum = kernel_call(
        grad_project_kernel,
        (shape_of(BLOCK, 768), shape_of(BLOCK, 2048)),
        (*grad_kv, *grad_queries, cosine, sine, tokens, stats1, w3),
        small_outs=(
            shape_of(1, 2048, kind=WIDE),
            shape_of(1, 2048, kind=WIDE),
            shape_of(3, 256, kind=WIDE),
        ),
        scalars=(place,),
        scratch=(pltpu.VMEM((4, BLOCK, 128), LOW), four),
        late=3,
        flops=2 * 512 * 2048 * 768,
    )
    partial_normed, layer_out, feed_other = tied((partial_normed, layer_out, feed_other))
    normed_parts = tp_parts(partial_normed)

    rest_mine, rest_theirs = weight_grads(
        ((grad_mixed, normed_low), (attended_low, grad_branch)), place
    )
    vectors = jnp.concatenate([gain_sum, shift_sum, second_sums], axis=0).reshape(32, 256)
    vectors = jnp.concatenate([vectors, bias_sum], axis=0)
    normed_parts, rest_mine, vectors = tied((normed_parts, rest_mine, vectors))
    rest_received = swapped(rest_theirs, "core")
    (copies5,) = kernel_call(
        first_gradient_kernel,
        (copies,),
        (normed_parts, grad_middle, tok_share, my_share(stats1)),
        small=(first_gain[None],),
    )
    grad_tokens = tp_rows(copies5)

    rest_z = z_parts(rest_mine, rest_received)
    vectors, *rest_z = tied((vectors, *rest_z))
    vectors = summed_by_pairs(vectors, (("core", 2, 1), ("zl", 2, 1), ("zh", 2, 1)))
    vectors, *rest_z = tied(
        (vectors, rest_z[0], *[z_permute(rest_z[k], k) for k in range(1, 4)])
    )
    rest_keep, rest_send = xh_halves(rest_z)
    vectors, rest_send = tied((vectors, rest_send))
    rest_w = rest_keep + swapped(rest_send, "xh").astype(WIDE)
    feed_w = feed_keep + feed_other.astype(WIDE)
    vectors = summed_by_pairs(vectors, (("xh", 2, 1),))
    bias_grad = vectors[32:]
    vectors = vectors[:32].reshape(4, 2048)
    vectors = summed_by_pairs(vectors, (("y", 4, 1), ("y", 4, 2), ("xl", 2, 1)))
    return (
        layer_out,
        grad_tokens,
        vectors[0],
        vectors[1],
        vectors[2],
        vectors[3],
        jnp.transpose(rest_w[:768].reshape(3, 256, 128), (2, 0, 1)),
        bias_grad,
        rest_w[768:],
        jnp.transpose(feed_w[:1408].reshape(2, 704, 128), (2, 0, 1)),
        feed_w[1408:],
    )


def solution(mesh):
    fine = Mesh(
        mesh.devices.reshape(2, 2, 2, 2, 4, 2), ("xh", "zh", "zl", "core", "y", "xl")
    )
    rows = P(CTX, None)
    return jax.shard_map(
        body,
        mesh=fine,
        in_specs=(
            rows, rows, P(), P(), P(), P(), P(),
            P(None, None, TP), P(None, TP), P(TP, None), P(None, None, TP), P(TP, None),
        ),
        out_specs=(
            rows, rows, P(), P(), P(), P(),
            P(CTX, None, TP), P(None, TP), P(TP, CTX), P(CTX, None, TP), P(TP, CTX),
        ),
        check_vma=False,
    )
```

time: 642 us -> 482 us (0.75)
  the two profiles are of different devices: /device:TPU:0 before, /device:TPU:6 now
where the time goes in v3:
time: 482 us; the launch traced here: 473 us
  waiting for transfers between devices  168 us (35%)
  Pallas kernels  120 us (25%)
  starting transfers between devices  100 us (21%)
  local copies, waits for them, and re-layouts  58 us (12%)
  other arithmetic  21.8 us (5%)
    pallas_call x17, Pallas kernels, kernel_call(): pl.pallas_call(run, out_shape=(*outs, *small_outs), in_specs=[pl.BlockSpe...  120 us
    all_to_all x8, waiting for transfers between devices, dealt(): return lax.all_to_all(x, axis, split_axis=0, concat_axis=0, tiled=True)  84.9 us
    unnamed x171, local copies, waits for them, and re-layouts  46.3 us
    all_to_all x8, starting transfers between devices, dealt(): return lax.all_to_all(x, axis, split_axis=0, concat_axis=0, tiled=True)  41.9 us
    ppermute x18, starting transfers between devices, across(): lax.ppermute(pieces[k], SPREAD, [(i, i ^ k) for i in range(4)])  39.6 us
    ppermute x7, waiting for transfers between devices, summed_by_pairs(): x = x + lax.ppermute(x, axis, [(i, i ^ distance) for i in range(size)])  33.4 us
    ppermute x18, waiting for transfers between devices, across(): lax.ppermute(pieces[k], SPREAD, [(i, i ^ k) for i in range(4)])  32.6 us
    ppermute x11, waiting for transfers between devices, swapped(): return lax.ppermute(x, axis, [(0, 1), (1, 0)])  17.2 us
  transfers between devices with their start and end apart: 50, of which 22 were waited for; matrix products, arithmetic and copies ran while one was open for 6% of the time, Pallas kernels for 18%

profile of v3, /device:TPU:6, one launch (start us, length us, event | category | flops | bytes accessed | tf_op | source)
XLA Modules:
  0.0 472.8 jit_solution(5666959105717066536)
XLA Ops:
  8.4 7.2 %shard_map.203 = (bf16[512,2048]{1,0:T(8,128)(2,1)S(1)}, f32[512,128]{1,0:T(8,128)S(1)}, bf16[512,128]{1,0:T(8,128)(2,1)S(1)}, bf16[512,128]{1,0:T(8,128)(2,1)S(...) custom-call(s32[4]{0:T(128)S(1)} %pad_add_fusion.refs_0_, ...), custom_call_target="tpu_custom_call" | custom-call | flops 1610612736 | bytes 8945664 | tf_op jit(solution)/shard_map/pallas_call | solution.py:67
  16.9 4.8 %collective-permute-start.2 = (bf16[512,128]{1,0:T(8,128)(2,1)S(1)}, bf16[512,128]{1,0:T(8,128)(2,1)S(1)}, u32[]{:S(2)}, u32[]{:S(2)}) collective-permute-start(bf16[512,128]{1,0:T(8,128)(2,1)S(1)} %get-tuple-element.127), channel_id=1, source_target_pairs={{0,96},{32,64},{64,32},{96,0},{1,97},{33,65},{65,33},{97,1},{2,98}... | collective-permute-start | bytes 393224 | tf_op jit(solution)/shard_map/ppermute | solution.py:531
  23.8 3.5 collective-permute-done.2
  27.3 2.6 collective-permute-done.1
  31.8 2.9 collective-permute-start.4
  38.3 11.4 %collective-permute-done.4.refs_4_ = bf16[256,128]{1,0:T(8,128)(2,1)S(1)} collective-permute-done((bf16[256,128]{1,0:T(8,128)(2,1)S(1)}, bf16[256,128]{1,0:T(8,128)(2,1)S(1)}, u32[]{:S(2)}, u32[]{:S(2)}) %collective-permute-start.4) | collective-permute-done | bytes 65568 | tf_op jit(solution)/shard_map/ppermute | solution.py:531
  49.8 12.4 %shard_map.204 = (f32[4,128,512]{2,1,0:T(8,128)S(1)}, f32[4,8,512]{2,1,0:T(8,128)S(1)}) custom-call(s32[4]{0:T(128)S(1)} %pad_add_fusion.refs_0_, bf16[4,512,128]{2,1,0:T(8,128)(2,1)S(1)} %pad_maximum_fusion.refs_1_, bf16[4,512,128]{2,1,0:T(8,128)(2,1)S(1)} %collective-permute-done.3.refs_2_, bf16[256,128]{1,0:T(8,128)(2,1)S(1)} %get-tuple-element.128.refs_3_, ...), custom_call_target="tpu_custom_call" | custom-call | flops 2684354560 | bytes 2490368 | tf_op jit(solution)/shard_map/pallas_call | solution.py:67
  64.3 13.7 %shard_map.205 = (bf16[256,128]{1,0:T(8,128)(2,1)S(1)}, bf16[256,128]{1,0:T(8,128)(2,1)S(1)}, bf16[256,128]{1,0:T(8,128)(2,1)S(1)}, bf16[256,128]{1,0:T(8,128)(2...) custom-call(s32[4]{0:T(128)S(1)} %pad_add_fusion.refs_0_, ...), custom_call_target="tpu_custom_call" | custom-call | flops 2684354560 | bytes 3866624 | tf_op jit(solution)/shard_map/pallas_call | solution.py:67
  80.6 4.6 collective-permute-start.11
  85.2 3.6 collective-permute-done.11.refs_4_
  92.9 6.1 %all-to-all-start = ((bf16[8,64,2048]{2,1,0:T(8,128)(2,1)}), bf16[8,64,2048]{2,1,0:T(8,128)(2,1)S(1)}, u32[]{:S(2)}, u32[]{:S(2)}) async-start(bf16[8,64,2048]{2,1,0:T(8,128)(2,1)} %bitcast.101), calls=%async_computation | async-start | bytes 4194304 | tf_op jit(solution)/shard_map/all_to_all | solution.py:562
  100.9 23.1 %all-to-all-done.refs_0_ = bf16[8,64,2048]{2,1,0:T(8,128)(2,1)S(1)} async-done(((bf16[8,64,2048]{2,1,0:T(8,128)(2,1)}), bf16[8,64,2048]{2,1,0:T(8,128)(2,1)S(1)}, u32[]{:S(2)}, u32[]{:S(2)}) %all-to-all-start) | async-done | bytes 2097184 | tf_op jit(solution)/shard_map/all_to_all | solution.py:562
  128.5 5.7 %all-to-all-start.1 = ((bf16[8,64,2048]{2,1,0:T(8,128)(2,1)}), bf16[8,64,2048]{2,1,0:T(8,128)(2,1)}, u32[]{:S(2)}, u32[]{:S(2)}) async-start(bf16[8,64,2048]{2,1,0:T(8,128)(2,1)} %copy-done.16), calls=%async_computation.1 | async-start | bytes 4194304 | tf_op jit(solution)/shard_map/all_to_all | solution.py:562
  134.2 5.2 %fusion.24 = (bf16[1,704,2048]{2,1,0:T(8,128)(2,1)S(1)}, bf16[1,704,2048]{2,1,0:T(8,128)(2,1)}) fusion(bf16[2,704,2048]{2,1,0:T(8,128)(2,1)} %bitcast.111), kind=kLoop, calls=%fused_computation.61 | loop fusion | bytes 11534336 | tf_op jit(solution)/shard_map/slice | solution.py:684
  142.9 15.8 %all-to-all-done.1 = bf16[8,64,2048]{2,1,0:T(8,128)(2,1)} async-done(((bf16[8,64,2048]{2,1,0:T(8,128)(2,1)}), bf16[8,64,2048]{2,1,0:T(8,128)(2,1)}, u32[]{:S(2)}, u32[]{:S(2)}) %all-to-all-start.1) | async-done | bytes 2097184 | tf_op jit(solution)/shard_map/all_to_all | solution.py:562
  161.9 10.2 %shard_map.209 = (bf16[512,704]{1,0:T(8,128)(2,1)S(1)}, bf16[512,704]{1,0:T(8,128)(2,1)S(1)}, bf16[512,704]{1,0:T(8,128)(2,1)S(1)}, bf16[512,2048]{1,0:T(8,128)(2,1)S(1)}) custom-call(bf16[512,2048]{1,0:T(8,128)(2,1)} %bitcast.14.refs_0_.refs_4_.refs_5_, bf16[1,704,2048]{2,1,0:T(8,128)(2,1)S(1)} %copy-done.6, ...), custom_call_target="tpu_custom_call" | custom-call | flops 5905580032 | bytes 13565952 | tf_op jit(solution)/shard_map/pallas_call | solution.py:67
  176.1 4.6 all-to-all-start.2
  185.8 10.3 %shard_map.210 = (bf16[8,2112,128]{2,1,0:T(8,128)(2,1)S(1)}, bf16[8,2112,128]{2,1,0:T(8,128)(2,1)S(1)}) custom-call(s32[4]{0:T(128)S(1)} %pad_add_fusion.refs_0_, bf16[512,704]{1,0:T(8,128)(2,1)S(1)} %copy-done.72, bf16[512,704]{1,0:T(8,128)(2,1)S(1)} %copy-done.74, bf16[512,704]{1,0:T(8,128)(2,1)S(1)} %copy-done.66, ...), custom_call_target="tpu_custom_call" | custom-call | flops 4429185024 | bytes 17104896 | tf_op jit(solution)/shard_map/pallas_call | solution.py:67
  200.2 5.7 %all-to-all-done.2.refs_0_ = bf16[8,64,2048]{2,1,0:T(8,128)(2,1)S(1)} async-done(((bf16[8,64,2048]{2,1,0:T(8,128)(2,1)}), bf16[8,64,2048]{2,1,0:T(8,128)(2,1)S(1)}, u32[]{:S(2)}, u32[]{:S(2)}) %all-to-all-start.2) | async-done | bytes 2097184 | tf_op jit(solution)/shard_map/all_to_all | solution.py:562
  209.5 5.1 %all-to-all-start.3 = ((bf16[8,64,2048]{2,1,0:T(8,128)(2,1)}), bf16[8,64,2048]{2,1,0:T(8,128)(2,1)S(1)}, u32[]{:S(2)}, u32[]{:S(2)}) async-start(bf16[8,64,2048]{2,1,0:T(8,128)(2,1)} %copy-done.11), calls=%async_computation.3 | async-start | bytes 4194304 | tf_op jit(solution)/shard_map/all_to_all | solution.py:562
  214.6 6.5 %add_convert_fusion = (bf16[2,1,2112,128]{3,2,1,0:T(8,128)(2,1)}, bf16[2,2112,128]{2,1,0:T(8,128)(2,1)}, bf16[2,2112,128]{2,1,0:T(8,128)(2,1)}, bf16[2,2112,128]{2,1,0:T(8,128)(2,1)}) fusion(bf16[2,4,2112,128]{3,2,1,0:T(8,128)(2,1)} %bitcast.18, s32[]{:T(128)S(6)} %select_n.71, bf16[2,4,2112,128]{3,2,1,0:T(8,128)(2,1)} %bitcast.96, s32[]{:T(128)S(6)} %select_n.70, ...), kind=kLoop, calls=%fused_computation.1 | loop fusion | flops 8650752 | bytes 12976144 | tf_op jit(solution)/shard_map/convert_element_type | solution.py:544
  221.3 3.0 collective-permute-start.14
  224.3 3.1 convolution_convert_fusion
  227.5 13.9 %all-to-all-done.3 = bf16[8,64,2048]{2,1,0:T(8,128)(2,1)S(1)} async-done(((bf16[8,64,2048]{2,1,0:T(8,128)(2,1)}), bf16[8,64,2048]{2,1,0:T(8,128)(2,1)S(1)}, u32[]{:S(2)}, u32[]{:S(2)}) %all-to-all-start.3) | async-done | bytes 2097184 | tf_op jit(solution)/shard_map/all_to_all | solution.py:562
  241.3 4.5 all-to-all-start.4
  257.7 4.1 collective-permute-done.17.refs_10_
  261.8 19.5 %shard_map.213 = (f32[4,128,512]{2,1,0:T(8,128)S(1)}, bf16[4,512,128]{2,1,0:T(8,128)(2,1)S(1)}, bf16[4,512,128]{2,1,0:T(8,128)(2,1)}) custom-call(s32[4]{0:T(128)S(1)} %pad_add_fusion.refs_0_, bf16[4,512,128]{2,1,0:T(8,128)(2,1)S(1)} %copy-done.47, bf16[4,512,128]{2,1,0:T(8,128)(2,1)S(1)} %copy-done.49, bf16[256,128]{1,0:T(8,128)(2,1)S(1)} %copy-done.63, ...), custom_call_target="tpu_custom_call" | custom-call | flops 6710886400 | bytes 4849664 | tf_op jit(solution)/shard_map/pallas_call | solution.py:67
  284.9 2.8 shard_map.214.refs_0_
  289.5 20.5 %shard_map.215 = (bf16[256,128]{1,0:T(8,128)(2,1)S(1)}, bf16[256,128]{1,0:T(8,128)(2,1)}, bf16[256,128]{1,0:T(8,128)(2,1)}, bf16[256,128]{1,0:T(8,128)(2,1)}, bf...) custom-call(s32[4]{0:T(128)S(1)} %pad_add_fusion.refs_0_, bf16[4,512,128]{2,1,0:T(8,128)(2,1)S(1)} %copy-done.26, ...), custom_call_target="tpu_custom_call" | custom-call | flops 6710886400 | bytes 5111808 | tf_op jit(solution)/shard_map/pallas_call | solution.py:67
  310.7 9.6 %collective-permute-done.19 = bf16[4,512,128]{2,1,0:T(8,128)(2,1)S(1)} collective-permute-done((bf16[4,512,128]{2,1,0:T(8,128)(2,1)S(1)}, bf16[4,512,128]{2,1,0:T(8,128)(2,1)S(1)}, u32[]{:S(2)}, u32[]{:S(2)}) %collective-permute-start.19) | collective-permute-done | bytes 524320 | tf_op jit(solution)/shard_map/ppermute | solution.py:526
  323.2 4.9 %all-to-all-start.5 = ((bf16[4,128,2048]{2,1,0:T(8,128)(2,1)}), bf16[4,128,2048]{2,1,0:T(8,128)(2,1)}, u32[]{:S(2)}, u32[]{:S(2)}) async-start(bf16[4,128,2048]{2,1,0:T(8,128)(2,1)} %copy-done), calls=%async_computation.5 | async-start | bytes 4194304 | tf_op jit(solution)/shard_map/all_to_all | solution.py:562
  328.1 2.8 collective-permute-start.26
  337.3 2.9 collective-permute-start.23
  347.2 4.9 %collective-permute-done.25.refs_4_ = bf16[512,128]{1,0:T(8,128)(2,1)S(1)} collective-permute-done((bf16[512,128]{1,0:T(8,128)(2,1)S(1)}, bf16[512,128]{1,0:T(8,128)(2,1)S(1)}, u32[]{:S(2)}, u32[]{:S(2)}) %collective-permute-start.25) | collective-permute-done | bytes 131104 | tf_op jit(solution)/shard_map/ppermute | solution.py:531
  352.2 5.2 %shard_map.216 = (bf16[512,768]{1,0:T(8,128)(2,1)S(1)}, bf16[512,2048]{1,0:T(8,128)(2,1)S(1)}, f32[1,2048]{1,0:T(1,128)S(1)}, f32[1,2048]{1,0:T(1,128)S(1)}, f32[3,256]{1,0:T(4,128)S(1)}) custom-call(s32[4]{0:T(128)S(1)} %pad_add_fusion.refs_0_, bf16[512,128]{1,0:T(8,128)(2,1)S(1)} %get-tuple-element.250.refs_1_, ...), custom_call_target="tpu_custom_call" | custom-call | flops 1610612736 | bytes 9699328 | tf_op jit(solution)/shard_map/pallas_call | solution.py:67
  358.7 5.8 %shard_map.218 = (bf16[8,1024,128]{2,1,0:T(8,128)(2,1)S(1)}, bf16[8,1024,128]{2,1,0:T(8,128)(2,1)}) custom-call(s32[4]{0:T(128)S(1)} %pad_add_fusion.refs_0_, bf16[512,768]{1,0:T(8,128)(2,1)S(1)} %get-tuple-element.211.refs_1_, bf16[512,256]{1,0:T(8,128)(2,1)S(1)} %copy-done.61, bf16[512,2048]{1,0:T(8,128)(2,1)S(1)} %copy-done.59, bf16[512,2048]{1,0:T(8,128)(2,1)S(1)} %bitcast.95), custom_call_target="tpu_custom_call" | custom-call | flops 2147483648 | bytes 9437184 | tf_op jit(solution)/shard_map/pallas_call | solution.py:67
  366.0 6.3 %all-to-all-start.6 = ((bf16[8,64,2048]{2,1,0:T(8,128)(2,1)}), bf16[8,64,2048]{2,1,0:T(8,128)(2,1)S(1)}, u32[]{:S(2)}, u32[]{:S(2)}) async-start(bf16[8,64,2048]{2,1,0:T(8,128)(2,1)} %bitcast.100), calls=%async_computation.6 | async-start | bytes 4194304 | tf_op jit(solution)/shard_map/all_to_all | solution.py:562
  372.4 26.4 %all-to-all-done.6.refs_0_ = bf16[8,64,2048]{2,1,0:T(8,128)(2,1)S(1)} async-done(((bf16[8,64,2048]{2,1,0:T(8,128)(2,1)}), bf16[8,64,2048]{2,1,0:T(8,128)(2,1)S(1)}, u32[]{:S(2)}, u32[]{:S(2)}) %all-to-all-start.6) | async-done | bytes 2097184 | tf_op jit(solution)/shard_map/all_to_all | solution.py:562
  398.7 3.9 fusion.14
  402.7 2.6 collective-permute-start.35
  408.4 4.7 %all-to-all-start.7 = ((bf16[8,64,2048]{2,1,0:T(8,128)(2,1)}), bf16[8,64,2048]{2,1,0:T(8,128)(2,1)S(1)}, u32[]{:S(2)}, u32[]{:S(2)}) async-start(bf16[8,64,2048]{2,1,0:T(8,128)(2,1)} %shard_map.219), calls=%async_computation.7 | async-start | bytes 4194304 | tf_op jit(solution)/shard_map/all_to_all | solution.py:562
  415.8 14.7 %collective-permute-done.32 = f32[35,256]{1,0:T(8,128)S(1)} collective-permute-done((f32[35,256]{1,0:T(8,128)S(1)}, f32[35,256]{1,0:T(8,128)S(1)}, u32[]{:S(2)}, u32[]{:S(2)}) %collective-permute-start.32) | collective-permute-done | bytes 35872 | tf_op jit(solution)/shard_map/ppermute | solution.py:575
  430.9 5.1 %collective-permute-done.33 = f32[35,256]{1,0:T(8,128)S(1)} collective-permute-done((f32[35,256]{1,0:T(8,128)S(1)}, f32[35,256]{1,0:T(8,128)S(1)}, u32[]{:S(2)}, u32[]{:S(2)}) %collective-permute-start.33) | collective-permute-done | bytes 35872 | tf_op jit(solution)/shard_map/ppermute | solution.py:575
  438.3 4.6 collective-permute-done.37
  443.8 3.1 collective-permute-done.38
  447.9 4.6 collective-permute-done.39
  459.4 5.8 %collective-permute-done.41 = bf16[1024,128]{1,0:T(8,128)(2,1)S(1)} collective-permute-done((bf16[1024,128]{1,0:T(8,128)(2,1)S(1)}, bf16[1024,128]{1,0:T(8,128)(2,1)S(1)}, u32[]{:S(2)}, u32[]{:S(2)}) %collective-permute-start.41) | collective-permute-done | bytes 262176 | tf_op jit(solution)/shard_map/ppermute | solution.py:526
  468.1 3.2 copy.63
  (284 shorter events, 113.5 us)
Async XLA Ops:
  16.9 10.4 %collective-permute-start.2 = (bf16[512,128]{1,0:T(8,128)(2,1)S(1)}, bf16[512,128]{1,0:T(8,128)(2,1)S(1)}, u32[]{:S(2)}, u32[]{:S(2)}) collective-permute-start(bf16[512,128]{1,0:T(8,128)(2,1)S(1)} %get-tuple-element.127), channel_id=1, source_target_pairs={{0,96},{32,64},{64,32},{96,0},{1,97},{33,65},{65,33},{97,1},{2,98}... | collective-permute-start | bytes 393224 | tf_op jit(solution)/shard_map/ppermute | solution.py:531
  21.7 8.1 %collective-permute-start.1 = (bf16[512,128]{1,0:T(8,128)(2,1)S(1)}, bf16[512,128]{1,0:T(8,128)(2,1)S(1)}, u32[]{:S(2)}, u32[]{:S(2)}) collective-permute-start(bf16[512,128]{1,0:T(8,128)(2,1)S(1)} %get-tuple-element.126), channel_id=1, source_target_pairs={{0,64},{32,96},{64,0},{96,32},{1,65},{33,97},{65,1},{97,33},{2,66}... | collective-permute-start | bytes 393224 | tf_op jit(solution)/shard_map/ppermute | solution.py:531
  23.8 6.5 %collective-permute-start = (bf16[512,128]{1,0:T(8,128)(2,1)S(1)}, bf16[512,128]{1,0:T(8,128)(2,1)S(1)}, u32[]{:S(2)}, u32[]{:S(2)}) collective-permute-start(bf16[512,128]{1,0:T(8,128)(2,1)S(1)} %get-tuple-element.125), channel_id=1, source_target_pairs={{0,32},{32,0},{64,96},{96,64},{1,33},{33,1},{65,97},{97,65},{2,34}... | collective-permute-start | bytes 393224 | tf_op jit(solution)/shard_map/ppermute | solution.py:531
  30.4 19.4 %collective-permute-start.3 = (bf16[4,512,128]{2,1,0:T(8,128)(2,1)S(1)}, bf16[4,512,128]{2,1,0:T(8,128)(2,1)S(1)}, u32[]{:S(2)}, u32[]{:S(2)}) collective-permute-start(bf16[4,512,128]{2,1,0:T(8,128)(2,1)S(1)} %pad_maximum_fusion.refs_1_), channel_id=1, source_target_pairs={{0,8},{8,0},{1,9},{9,1},{2,10},{10,2},{3,11},{11,3},{4,12},{12,4},... | collective-permute-start | bytes 1572872 | tf_op jit(solution)/shard_map/ppermute | solution.py:526
  30.5 31.7 %collective-permute-start.7 = (bf16[4,512,128]{2,1,0:T(8,128)(2,1)S(1)}, bf16[4,512,128]{2,1,0:T(8,128)(2,1)S(1)}, u32[]{:S(2)}, u32[]{:S(2)}) collective-permute-start(bf16[4,512,128]{2,1,0:T(8,128)(2,1)S(1)} %pad_maximum_fusion.refs_1_), channel_id=1, source_target_pairs={{0,16},{16,0},{1,17},{17,1},{2,18},{18,2},{3,19},{19,3},{4,20},{20... | collective-permute-start | bytes 1572872 | tf_op jit(solution)/shard_map/ppermute | solution.py:526
  31.8 18.0 %collective-permute-start.4 = (bf16[256,128]{1,0:T(8,128)(2,1)S(1)}, bf16[256,128]{1,0:T(8,128)(2,1)S(1)}, u32[]{:S(2)}, u32[]{:S(2)}) collective-permute-start(bf16[256,128]{1,0:T(8,128)(2,1)S(1)} %get-tuple-element.129), channel_id=1, source_target_pairs={{0,32},{32,0},{64,96},{96,64},{1,33},{33,1},{65,97},{97,65},{2,34}... | collective-permute-start | bytes 196616 | tf_op jit(solution)/shard_map/ppermute | solution.py:531
  34.7 15.0 %collective-permute-start.5 = (bf16[256,128]{1,0:T(8,128)(2,1)S(1)}, bf16[256,128]{1,0:T(8,128)(2,1)S(1)}, u32[]{:S(2)}, u32[]{:S(2)}) collective-permute-start(bf16[256,128]{1,0:T(8,128)(2,1)S(1)} %get-tuple-element.130), channel_id=1, source_target_pairs={{0,64},{32,96},{64,0},{96,32},{1,65},{33,97},{65,1},{97,33},{2,66}... | collective-permute-start | bytes 196616 | tf_op jit(solution)/shard_map/ppermute | solution.py:531
  36.1 13.6 %collective-permute-start.6 = (bf16[256,128]{1,0:T(8,128)(2,1)S(1)}, bf16[256,128]{1,0:T(8,128)(2,1)S(1)}, u32[]{:S(2)}, u32[]{:S(2)}) collective-permute-start(bf16[256,128]{1,0:T(8,128)(2,1)S(1)} %get-tuple-element.131), channel_id=1, source_target_pairs={{0,96},{32,64},{64,32},{96,0},{1,97},{33,65},{65,33},{97,1},{2,98}... | collective-permute-start | bytes 196616 | tf_op jit(solution)/shard_map/ppermute | solution.py:531
  78.7 6.5 %collective-permute-start.9 = (bf16[256,128]{1,0:T(8,128)(2,1)S(1)}, bf16[256,128]{1,0:T(8,128)(2,1)S(1)}, u32[]{:S(2)}, u32[]{:S(2)}) collective-permute-start(bf16[256,128]{1,0:T(8,128)(2,1)S(1)} %get-tuple-element.138), channel_id=1, source_target_pairs={{0,32},{32,0},{64,96},{96,64},{1,33},{33,1},{65,97},{97,65},{2,34}... | collective-permute-start | bytes 196616 | tf_op jit(solution)/shard_map/ppermute | solution.py:531
  79.3 5.9 %collective-permute-start.10 = (bf16[256,128]{1,0:T(8,128)(2,1)S(1)}, bf16[256,128]{1,0:T(8,128)(2,1)S(1)}, u32[]{:S(2)}, u32[]{:S(2)}) collective-permute-start(bf16[256,128]{1,0:T(8,128)(2,1)S(1)} %get-tuple-element.139), channel_id=1, source_target_pairs={{0,64},{32,96},{64,0},{96,32},{1,65},{33,97},{65,1},{97,33},{2,66}... | collective-permute-start | bytes 196616 | tf_op jit(solution)/shard_map/ppermute | solution.py:531
  80.6 8.2 %collective-permute-start.11 = (bf16[256,128]{1,0:T(8,128)(2,1)S(1)}, bf16[256,128]{1,0:T(8,128)(2,1)S(1)}, u32[]{:S(2)}, u32[]{:S(2)}) collective-permute-start(bf16[256,128]{1,0:T(8,128)(2,1)S(1)} %get-tuple-element.140), channel_id=1, source_target_pairs={{0,96},{32,64},{64,32},{96,0},{1,97},{33,65},{65,33},{97,1},{2,98}... | collective-permute-start | bytes 196616 | tf_op jit(solution)/shard_map/ppermute | solution.py:531
  92.9 31.1 %all-to-all-start = ((bf16[8,64,2048]{2,1,0:T(8,128)(2,1)}), bf16[8,64,2048]{2,1,0:T(8,128)(2,1)S(1)}, u32[]{:S(2)}, u32[]{:S(2)}) async-start(bf16[8,64,2048]{2,1,0:T(8,128)(2,1)} %bitcast.101), calls=%async_computation | async-start | bytes 4194304 | tf_op jit(solution)/shard_map/all_to_all | solution.py:562
  128.5 30.2 %all-to-all-start.1 = ((bf16[8,64,2048]{2,1,0:T(8,128)(2,1)}), bf16[8,64,2048]{2,1,0:T(8,128)(2,1)}, u32[]{:S(2)}, u32[]{:S(2)}) async-start(bf16[8,64,2048]{2,1,0:T(8,128)(2,1)} %copy-done.16), calls=%async_computation.1 | async-start | bytes 4194304 | tf_op jit(solution)/shard_map/all_to_all | solution.py:562
  176.1 29.8 %all-to-all-start.2 = ((bf16[8,64,2048]{2,1,0:T(8,128)(2,1)}), bf16[8,64,2048]{2,1,0:T(8,128)(2,1)S(1)}, u32[]{:S(2)}, u32[]{:S(2)}) async-start(bf16[8,64,2048]{2,1,0:T(8,128)(2,1)} %bitcast.102), calls=%async_computation.2 | async-start | bytes 4194304 | tf_op jit(solution)/shard_map/all_to_all | solution.py:562
  206.0 8.6 %collective-permute-start.12 = (bf16[8,2112,128]{2,1,0:T(8,128)(2,1)}, bf16[8,2112,128]{2,1,0:T(8,128)(2,1)}, u32[]{:S(2)}, u32[]{:S(2)}) collective-permute-start(bf16[8,2112,128]{2,1,0:T(8,128)(2,1)} %copy-done.43), channel_id=1, source_target_pairs={{0,8},{8,0},{1,9},{9,1},{2,10},{10,2},{3,11},{11,3},{4,12},{12,4},... | collective-permute-start | bytes 12976136 | tf_op jit(solution)/shard_map/ppermute | solution.py:526
  209.5 31.9 %all-to-all-start.3 = ((bf16[8,64,2048]{2,1,0:T(8,128)(2,1)}), bf16[8,64,2048]{2,1,0:T(8,128)(2,1)S(1)}, u32[]{:S(2)}, u32[]{:S(2)}) async-start(bf16[8,64,2048]{2,1,0:T(8,128)(2,1)} %copy-done.11), calls=%async_computation.3 | async-start | bytes 4194304 | tf_op jit(solution)/shard_map/all_to_all | solution.py:562
  221.1 28.0 %collective-permute-start.13 = (bf16[2,2112,128]{2,1,0:T(8,128)(2,1)}, bf16[2,2112,128]{2,1,0:T(8,128)(2,1)}, u32[]{:S(2)}, u32[]{:S(2)}) collective-permute-start(bf16[2,2112,128]{2,1,0:T(8,128)(2,1)} %get-tuple-element.240), channel_id=1, source_target_pairs={{0,16},{16,32},{32,48},{48,0},{1,17},{17,33},{33,49},{49,1},{2,18}... | collective-permute-start | bytes 3244040 | tf_op jit(solution)/shard_map/ppermute | solution.py:549
  221.3 27.8 %collective-permute-start.14 = (bf16[2,2112,128]{2,1,0:T(8,128)(2,1)}, bf16[2,2112,128]{2,1,0:T(8,128)(2,1)}, u32[]{:S(2)}, u32[]{:S(2)}) collective-permute-start(bf16[2,2112,128]{2,1,0:T(8,128)(2,1)} %get-tuple-element.239), channel_id=1, source_target_pairs={{0,48},{16,0},{32,16},{48,32},{1,49},{17,1},{33,17},{49,33},{2,50}... | collective-permute-start | bytes 3244040 | tf_op jit(solution)/shard_map/ppermute | solution.py:549
  241.3 41.8 %all-to-all-start.4 = ((bf16[4,128,2048]{2,1,0:T(8,128)(2,1)}), bf16[4,128,2048]{2,1,0:T(8,128)(2,1)}, u32[]{:S(2)}, u32[]{:S(2)}) async-start(bf16[4,128,2048]{2,1,0:T(8,128)(2,1)} %bitcast.112), calls=%async_computation.4 | async-start | bytes 4194304 | tf_op jit(solution)/shard_map/all_to_all | solution.py:562
  249.1 6.6 %collective-permute-start.15 = (bf16[256,128]{1,0:T(8,128)(2,1)S(1)}, bf16[256,128]{1,0:T(8,128)(2,1)S(1)}, u32[]{:S(2)}, u32[]{:S(2)}) collective-permute-start(bf16[256,128]{1,0:T(8,128)(2,1)S(1)} %get-tuple-element.167), channel_id=1, source_target_pairs={{0,32},{32,0},{64,96},{96,64},{1,33},{33,1},{65,97},{97,65},{2,34}... | collective-permute-start | bytes 196616 | tf_op jit(solution)/shard_map/ppermute | solution.py:531
  251.5 6.2 %collective-permute-start.16 = (bf16[256,128]{1,0:T(8,128)(2,1)S(1)}, bf16[256,128]{1,0:T(8,128)(2,1)S(1)}, u32[]{:S(2)}, u32[]{:S(2)}) collective-permute-start(bf16[256,128]{1,0:T(8,128)(2,1)S(1)} %get-tuple-element.168), channel_id=1, source_target_pairs={{0,64},{32,96},{64,0},{96,32},{1,65},{33,97},{65,1},{97,33},{2,66}... | collective-permute-start | bytes 196616 | tf_op jit(solution)/shard_map/ppermute | solution.py:531
  253.6 8.2 %collective-permute-start.17 = (bf16[256,128]{1,0:T(8,128)(2,1)S(1)}, bf16[256,128]{1,0:T(8,128)(2,1)S(1)}, u32[]{:S(2)}, u32[]{:S(2)}) collective-permute-start(bf16[256,128]{1,0:T(8,128)(2,1)S(1)} %get-tuple-element.169), channel_id=1, source_target_pairs={{0,96},{32,64},{64,32},{96,0},{1,97},{33,65},{65,33},{97,1},{2,98}... | collective-permute-start | bytes 196616 | tf_op jit(solution)/shard_map/ppermute | solution.py:531
  283.2 4.6 collective-permute-start.18
  283.2 37.1 %collective-permute-start.21 = (bf16[2,2112,128]{2,1,0:T(8,128)(2,1)}, bf16[2,2112,128]{2,1,0:T(8,128)(2,1)S(1)}, u32[]{:S(2)}, u32[]{:S(2)}) collective-permute-start(bf16[2,2112,128]{2,1,0:T(8,128)(2,1)} %get-tuple-element.193), channel_id=1, source_target_pairs={{0,32},{16,48},{32,0},{48,16},{1,33},{17,49},{33,1},{49,17},{2,34}... | collective-permute-start | bytes 3244040 | tf_op jit(solution)/shard_map/ppermute | solution.py:549
  287.9 32.4 %collective-permute-start.19 = (bf16[4,512,128]{2,1,0:T(8,128)(2,1)S(1)}, bf16[4,512,128]{2,1,0:T(8,128)(2,1)S(1)}, u32[]{:S(2)}, u32[]{:S(2)}) collective-permute-start(bf16[4,512,128]{2,1,0:T(8,128)(2,1)S(1)} %add_convert_fusion.8), channel_id=1, source_target_pairs={{0,16},{16,0},{1,17},{17,1},{2,18},{18,2},{3,19},{19,3},{4,20},{20... | collective-permute-start | bytes 1572872 | tf_op jit(solution)/shard_map/ppermute | solution.py:526
  288.8 31.5 %collective-permute-start.20 = (bf16[128,2048]{1,0:T(8,128)(2,1)S(1)}, bf16[128,2048]{1,0:T(8,128)(2,1)S(1)}, u32[]{:S(2)}, u32[]{:S(2)}) collective-permute-start(bf16[128,2048]{1,0:T(8,128)(2,1)S(1)} %shard_map.214.refs_0_), channel_id=1, source_target_pairs={{0,1},{1,0},{2,3},{3,2},{4,5},{5,4},{6,7},{7,6},{8,9},{9,8},{10,11... | collective-permute-start | bytes 1572872 | tf_op jit(solution)/shard_map/ppermute | solution.py:526
  320.3 14.3 %collective-permute-start.22 = (bf16[4,512,128]{2,1,0:T(8,128)(2,1)}, bf16[4,512,128]{2,1,0:T(8,128)(2,1)}, u32[]{:S(2)}, u32[]{:S(2)}) collective-permute-start(bf16[4,512,128]{2,1,0:T(8,128)(2,1)} %get-tuple-element.195), channel_id=1, source_target_pairs={{0,8},{8,0},{1,9},{9,1},{2,10},{10,2},{3,11},{11,3},{4,12},{12,4},... | collective-permute-start | bytes 1572872 | tf_op jit(solution)/shard_map/ppermute | solution.py:526
  323.2 42.7 %all-to-all-start.5 = ((bf16[4,128,2048]{2,1,0:T(8,128)(2,1)}), bf16[4,128,2048]{2,1,0:T(8,128)(2,1)}, u32[]{:S(2)}, u32[]{:S(2)}) async-start(bf16[4,128,2048]{2,1,0:T(8,128)(2,1)} %copy-done), calls=%async_computation.5 | async-start | bytes 4194304 | tf_op jit(solution)/shard_map/all_to_all | solution.py:562
  328.1 14.2 %collective-permute-start.26 = (bf16[256,128]{1,0:T(8,128)(2,1)}, bf16[256,128]{1,0:T(8,128)(2,1)S(1)}, u32[]{:S(2)}, u32[]{:S(2)}) collective-permute-start(bf16[256,128]{1,0:T(8,128)(2,1)} %get-tuple-element.198), channel_id=1, source_target_pairs={{0,32},{32,0},{64,96},{96,64},{1,33},{33,1},{65,97},{97,65},{2,34}... | collective-permute-start | bytes 196616 | tf_op jit(solution)/shard_map/ppermute | solution.py:531
  330.9 14.8 %collective-permute-start.27 = (bf16[256,128]{1,0:T(8,128)(2,1)}, bf16[256,128]{1,0:T(8,128)(2,1)S(1)}, u32[]{:S(2)}, u32[]{:S(2)}) collective-permute-start(bf16[256,128]{1,0:T(8,128)(2,1)} %get-tuple-element.199), channel_id=1, source_target_pairs={{0,64},{32,96},{64,0},{96,32},{1,65},{33,97},{65,1},{97,33},{2,66}... | collective-permute-start | bytes 196616 | tf_op jit(solution)/shard_map/ppermute | solution.py:531
  332.9 14.3 %collective-permute-start.28 = (bf16[256,128]{1,0:T(8,128)(2,1)}, bf16[256,128]{1,0:T(8,128)(2,1)S(1)}, u32[]{:S(2)}, u32[]{:S(2)}) collective-permute-start(bf16[256,128]{1,0:T(8,128)(2,1)} %get-tuple-element.200), channel_id=1, source_target_pairs={{0,96},{32,64},{64,32},{96,0},{1,97},{33,65},{65,33},{97,1},{2,98}... | collective-permute-start | bytes 196616 | tf_op jit(solution)/shard_map/ppermute | solution.py:531
  337.3 9.9 %collective-permute-start.23 = (bf16[512,128]{1,0:T(8,128)(2,1)S(1)}, bf16[512,128]{1,0:T(8,128)(2,1)S(1)}, u32[]{:S(2)}, u32[]{:S(2)}) collective-permute-start(bf16[512,128]{1,0:T(8,128)(2,1)S(1)} %get-tuple-element.249), channel_id=1, source_target_pairs={{0,32},{32,0},{64,96},{96,64},{1,33},{33,1},{65,97},{97,65},{2,34}... | collective-permute-start | bytes 393224 | tf_op jit(solution)/shard_map/ppermute | solution.py:531
  340.2 7.0 %collective-permute-start.24 = (bf16[512,128]{1,0:T(8,128)(2,1)S(1)}, bf16[512,128]{1,0:T(8,128)(2,1)S(1)}, u32[]{:S(2)}, u32[]{:S(2)}) collective-permute-start(bf16[512,128]{1,0:T(8,128)(2,1)S(1)} %get-tuple-element.248), channel_id=1, source_target_pairs={{0,64},{32,96},{64,0},{96,32},{1,65},{33,97},{65,1},{97,33},{2,66}... | collective-permute-start | bytes 393224 | tf_op jit(solution)/shard_map/ppermute | solution.py:531
  342.3 9.9 %collective-permute-start.25 = (bf16[512,128]{1,0:T(8,128)(2,1)S(1)}, bf16[512,128]{1,0:T(8,128)(2,1)S(1)}, u32[]{:S(2)}, u32[]{:S(2)}) collective-permute-start(bf16[512,128]{1,0:T(8,128)(2,1)S(1)} %get-tuple-element.247), channel_id=1, source_target_pairs={{0,96},{32,64},{64,32},{96,0},{1,97},{33,65},{65,33},{97,1},{2,98}... | collective-permute-start | bytes 393224 | tf_op jit(solution)/shard_map/ppermute | solution.py:531
  345.7 20.2 %collective-permute-start.29 = (bf16[2112,128]{1,0:T(8,128)(2,1)S(1)}, bf16[2112,128]{1,0:T(8,128)(2,1)}, u32[]{:S(2)}, u32[]{:S(2)}) collective-permute-start(bf16[2112,128]{1,0:T(8,128)(2,1)S(1)} %fusion.10), channel_id=1, source_target_pairs={{0,64},{64,0},{1,65},{65,1},{2,66},{66,2},{3,67},{67,3},{4,68},{68... | collective-permute-start | bytes 1622024 | tf_op jit(solution)/shard_map/ppermute | solution.py:526
  366.0 32.8 %collective-permute-start.30 = (bf16[8,1024,128]{2,1,0:T(8,128)(2,1)}, bf16[8,1024,128]{2,1,0:T(8,128)(2,1)}, u32[]{:S(2)}, u32[]{:S(2)}) collective-permute-start(bf16[8,1024,128]{2,1,0:T(8,128)(2,1)} %get-tuple-element.223), channel_id=1, source_target_pairs={{0,8},{8,0},{1,9},{9,1},{2,10},{10,2},{3,11},{11,3},{4,12},{12,4},... | collective-permute-start | bytes 6291464 | tf_op jit(solution)/shard_map/ppermute | solution.py:526
  366.0 32.8 %all-to-all-start.6 = ((bf16[8,64,2048]{2,1,0:T(8,128)(2,1)}), bf16[8,64,2048]{2,1,0:T(8,128)(2,1)S(1)}, u32[]{:S(2)}, u32[]{:S(2)}) async-start(bf16[8,64,2048]{2,1,0:T(8,128)(2,1)} %bitcast.100), calls=%async_computation.6 | async-start | bytes 4194304 | tf_op jit(solution)/shard_map/all_to_all | solution.py:562
  402.7 33.3 %collective-permute-start.34 = (bf16[2,1024,128]{2,1,0:T(8,128)(2,1)}, bf16[2,1024,128]{2,1,0:T(8,128)(2,1)}, u32[]{:S(2)}, u32[]{:S(2)}) collective-permute-start(bf16[2,1024,128]{2,1,0:T(8,128)(2,1)} %get-tuple-element.226), channel_id=1, source_target_pairs={{0,16},{16,32},{32,48},{48,0},{1,17},{17,33},{33,49},{49,1},{2,18}... | collective-permute-start | bytes 1572872 | tf_op jit(solution)/shard_map/ppermute | solution.py:549
  402.7 33.3 %collective-permute-start.35 = (bf16[2,1024,128]{2,1,0:T(8,128)(2,1)}, bf16[2,1024,128]{2,1,0:T(8,128)(2,1)}, u32[]{:S(2)}, u32[]{:S(2)}) collective-permute-start(bf16[2,1024,128]{2,1,0:T(8,128)(2,1)} %get-tuple-element.227), channel_id=1, source_target_pairs={{0,32},{16,48},{32,0},{48,16},{1,33},{17,49},{33,1},{49,17},{2,34}... | collective-permute-start | bytes 1572872 | tf_op jit(solution)/shard_map/ppermute | solution.py:549
  405.3 30.7 %collective-permute-start.36 = (bf16[2,1024,128]{2,1,0:T(8,128)(2,1)}, bf16[2,1024,128]{2,1,0:T(8,128)(2,1)}, u32[]{:S(2)}, u32[]{:S(2)}) collective-permute-start(bf16[2,1024,128]{2,1,0:T(8,128)(2,1)} %get-tuple-element.228), channel_id=1, source_target_pairs={{0,48},{16,0},{32,16},{48,32},{1,49},{17,1},{33,17},{49,33},{2,50}... | collective-permute-start | bytes 1572872 | tf_op jit(solution)/shard_map/ppermute | solution.py:549
  408.4 59.7 %all-to-all-start.7 = ((bf16[8,64,2048]{2,1,0:T(8,128)(2,1)}), bf16[8,64,2048]{2,1,0:T(8,128)(2,1)S(1)}, u32[]{:S(2)}, u32[]{:S(2)}) async-start(bf16[8,64,2048]{2,1,0:T(8,128)(2,1)} %shard_map.219), calls=%async_computation.7 | async-start | bytes 4194304 | tf_op jit(solution)/shard_map/all_to_all | solution.py:562
  414.3 16.2 %collective-permute-start.32 = (f32[35,256]{1,0:T(8,128)S(1)}, f32[35,256]{1,0:T(8,128)S(1)}, u32[]{:S(2)}, u32[]{:S(2)}) collective-permute-start(f32[35,256]{1,0:T(8,128)S(1)} %add.273), channel_id=1, source_target_pairs={{0,16},{16,0},{1,17},{17,1},{2,18},{18,2},{3,19},{19,3},{4,20},{20... | collective-permute-start | bytes 107528 | tf_op jit(solution)/shard_map/ppermute | solution.py:575
  430.5 5.5 %collective-permute-start.33 = (f32[35,256]{1,0:T(8,128)S(1)}, f32[35,256]{1,0:T(8,128)S(1)}, u32[]{:S(2)}, u32[]{:S(2)}) collective-permute-start(f32[35,256]{1,0:T(8,128)S(1)} %add.274), channel_id=1, source_target_pairs={{0,32},{32,0},{1,33},{33,1},{2,34},{34,2},{3,35},{35,3},{4,36},{36... | collective-permute-start | bytes 107528 | tf_op jit(solution)/shard_map/ppermute | solution.py:575
  437.4 5.6 %collective-permute-start.37 = (f32[35,256]{1,0:T(8,128)S(1)}, f32[35,256]{1,0:T(8,128)S(1)}, u32[]{:S(2)}, u32[]{:S(2)}) collective-permute-start(f32[35,256]{1,0:T(8,128)S(1)} %add.275), channel_id=1, source_target_pairs={{0,64},{64,0},{1,65},{65,1},{2,66},{66,2},{3,67},{67,3},{4,68},{68... | collective-permute-start | bytes 107528 | tf_op jit(solution)/shard_map/ppermute | solution.py:575
  443.0 4.0 collective-permute-start.38
  447.0 5.5 %collective-permute-start.39 = (f32[4,2048]{1,0:T(4,128)S(1)}, f32[4,2048]{1,0:T(4,128)S(1)}, u32[]{:S(2)}, u32[]{:S(2)}) collective-permute-start(f32[4,2048]{1,0:T(4,128)S(1)} %add.281), channel_id=1, source_target_pairs={{0,4},{2,6},{4,0},{6,2},{1,5},{3,7},{5,1},{7,3},{8,12},{10,14},{12... | collective-permute-start | bytes 98312 | tf_op jit(solution)/shard_map/ppermute | solution.py:575
  452.5 6.3 %collective-permute-start.40 = (f32[4,2048]{1,0:T(4,128)S(1)}, f32[4,2048]{1,0:T(4,128)S(1)}, u32[]{:S(2)}, u32[]{:S(2)}) collective-permute-start(f32[4,2048]{1,0:T(4,128)S(1)} %add.282), channel_id=1, source_target_pairs={{0,1},{1,0},{2,3},{3,2},{4,5},{5,4},{6,7},{7,6},{8,9},{9,8},{10,11... | collective-permute-start | bytes 98312 | tf_op jit(solution)/shard_map/ppermute | solution.py:575
  457.3 7.9 %collective-permute-start.41 = (bf16[1024,128]{1,0:T(8,128)(2,1)S(1)}, bf16[1024,128]{1,0:T(8,128)(2,1)S(1)}, u32[]{:S(2)}, u32[]{:S(2)}) collective-permute-start(bf16[1024,128]{1,0:T(8,128)(2,1)S(1)} %fusion.15), channel_id=1, source_target_pairs={{0,64},{64,0},{1,65},{65,1},{2,66},{66,2},{3,67},{67,3},{4,68},{68... | collective-permute-start | bytes 786440 | tf_op jit(solution)/shard_map/ppermute | solution.py:526
  (86 other events, 727.2 us)
